TPU v7x, 32 devices: a whole 2x2x4 slice. The times are simulated.
32 devices in a mesh: seq: 4 (over y, x), mp: 8 (over z, core).
Axes of the slice: x: 2, y: 2, z: 4, core: 2. Of those that a mesh axis runs over, the one named last changes fastest.
Arguments:
- layer_in: bfloat16 [8, 1536, 1024], P('mp', 'seq'), may hold values from -6 to 6
- out_grad: bfloat16 [8, 1536, 1024], P('mp', 'seq'), may hold values from -6 to 6
- seq_lengths: int32 [8, 3], P('mp'), may hold values from 1 to 1248, 1536 in all within a row
- dealing: int32 [8, 1536], P('mp'), may hold values from 0 to 1535, each once within a row
- log_decay: float32 [8, 1536, 8], P('mp', 'seq'), may hold values from -0.75 to 0
- w_qkv: bfloat16 [1024, 4096], P(('seq', 'mp')), may hold values from -0.1875 to 0.1875
- w_out_gate: bfloat16 [1024, 2048], P(('seq', 'mp')), may hold values from -0.1875 to 0.1875
- w_beta: bfloat16 [1024, 8], P(('seq', 'mp')), may hold values from -0.1875 to 0.1875
- conv_w: bfloat16 [4096, 4], P(('seq', 'mp')), may hold values from -3 to 3
- gain_in: bfloat16 [1024], P(('seq', 'mp')), may hold values from 0.099609375 to 1.8984375
- gain_o: bfloat16 [256], P(('seq', 'mp')), may hold values from 0.099609375 to 1.8984375
- w_out: bfloat16 [2048, 1024], P(None, ('seq', 'mp')), may hold values from -0.125 to 0.125
- gain_mid: bfloat16 [1024], P(('seq', 'mp')), may hold values from 0.099609375 to 1.8984375
- w_gate_up: bfloat16 [1024, 5632], P(('seq', 'mp')), may hold values from -0.1875 to 0.1875
- w_down: bfloat16 [2816, 1024], P(None, ('seq', 'mp')), may hold values from -0.109375 to 0.109375
Outputs:
- mixed_out: bfloat16 [8, 1536, 1024], P('mp', 'seq')
- input_grad: bfloat16 [8, 1536, 1024], P('mp', 'seq')
- grad_w_qkv: float32 [1024, 4096], P(('seq', 'mp'))
- grad_w_out_gate: float32 [1024, 2048], P(('seq', 'mp'))
- grad_w_beta: float32 [1024, 8], P(('seq', 'mp'))
- grad_conv_w: float32 [4096, 4], P(('seq', 'mp'))
- grad_gain_in: float32 [1024], P(('seq', 'mp'))
- grad_gain_o: float32 [256], P(('seq', 'mp'))
- grad_w_out: float32 [2048, 1024], P(None, ('seq', 'mp'))
- grad_gain_mid: float32 [1024], P(('seq', 'mp'))
- grad_w_gate_up: float32 [1024, 5632], P(('seq', 'mp'))
- grad_w_down: float32 [2816, 1024], P(None, ('seq', 'mp'))
Inputs may be any that keep to these rules, and one draw needn't show every extreme that they name: `seq_lengths`: each row holds the lengths of 3 sequences packed in this order, summing to 1536; the largest is exactly 1248. `dealing`: each row is a permutation of the group's rows.
All inputs are finite; a program needn't handle non-finite values.
Results may differ from a plain program's by a relative error of at most 0.012.
The roundings to bfloat16 on the way count: a program that leaves them out, or rounds other values in their place, can miss the bound.
Values may be sent and summed in bfloat16 or wider, within the bound.
No kernel may reach another device: no remote copies, remote signals or barrier semaphores. Data moves between devices by JAX's collectives and lax.ppermute only.
A program may use at most 320 MiB of HBM per device.

v0:
```python
import jax
import jax.numpy as jnp
from jax import lax
from jax.sharding import PartitionSpec as P

HEAD_COUNT = 8
DK = 128
DV = 256
STRETCH = 64


EXACT_PRECISION = lax.Precision.HIGHEST


def shifted(value, axis, by):
    devices = lax.axis_size(axis)
    pairs = [(i, i + by) for i in range(devices) if 0 <= i + by < devices]
    return lax.ppermute(value, axis, pairs)


def batch_mm(left, right):
    return jnp.einsum("hij,hjk->hik", left, right, precision=EXACT_PRECISION)


def rms_scale(values, gain):
    return values * lax.rsqrt(jnp.mean(values * values, axis=-1, keepdims=True) + 1e-05) * gain


def segments(positions, lengths):
    ends = jnp.cumsum(lengths)
    counted = jnp.sum((positions[:, None] >= ends[None, :]).astype(jnp.int32), axis=1)
    return jnp.where(positions < 0, -1, counted)


def conv_mix(extended, seg_ext, conv_f):
    taps = conv_f.shape[1]
    count = extended.shape[0] - taps + 1
    seg_now = seg_ext[taps - 1 :]
    total = jnp.zeros((count, extended.shape[1]), jnp.float32)
    for offset in range(taps):
        keeper = (seg_ext[offset : offset + count] == seg_now).astype(jnp.float32)
        total = (
            total + extended[offset : offset + count] * keeper[:, None] * conv_f[:, offset][None, :]
        )
    return jax.nn.silu(total)


def split_feats(feats, heads, key_dim, val_dim):
    count = feats.shape[0]
    queries = feats[:, : heads * key_dim].reshape(count, heads, key_dim)
    raw_keys = feats[:, heads * key_dim : 2 * heads * key_dim].reshape(count, heads, key_dim)
    values = feats[:, 2 * heads * key_dim :].reshape(count, heads, val_dim)
    keys_n = raw_keys * lax.rsqrt(jnp.sum(raw_keys * raw_keys, axis=-1, keepdims=True) + 1e-06)
    return (queries, keys_n, values)


def unit_inverse(lower_mat):
    size = lower_mat.shape[-1]
    ident = jnp.eye(size, dtype=jnp.float32)
    result = ident - lower_mat
    power = lower_mat
    span = 2
    while span < size:
        power = batch_mm(power, power)
        result = batch_mm(result, ident + power)
        span = span * 2
    return result


def stretch_terms(queries, keys_n, values, beta, decay, seg, seg_prev):
    size = queries.shape[1]
    cum = jnp.cumsum(decay, axis=1)
    index = jnp.arange(size)
    strict = index[:, None] > index[None, :]
    within = (index[:, None] >= index[None, :]) & (seg[:, None] == seg[None, :])
    keep_in = (seg == seg_prev).astype(jnp.float32)
    keep_out = (seg == seg[size - 1]).astype(jnp.float32)
    diff = cum[:, :, None] - cum[:, None, :]
    dmat = jnp.where(within[None], jnp.exp(jnp.where(within[None], diff, 0.0)), 0.0)
    inner = jnp.einsum("hik,hjk->hij", keys_n, keys_n, precision=EXACT_PRECISION)
    lower_mat = jnp.where(strict[None], beta[:, :, None] * inner * dmat, 0.0)
    inverse = unit_inverse(lower_mat)
    elog = jnp.exp(cum) * keep_in[None, :]
    umat = batch_mm(inverse, beta[:, :, None] * values)
    wmat = batch_mm(inverse, (beta * elog)[:, :, None] * keys_n)
    qkd = jnp.einsum("hik,hjk->hij", queries, keys_n, precision=EXACT_PRECISION) * dmat
    gmat = queries * elog[:, :, None] - batch_mm(qkd, wmat)
    o_local = batch_mm(qkd, umat)
    last = cum[:, size - 1]
    key_boundary = keys_n * (jnp.exp(last[:, None] - cum) * keep_out[None, :])[:, :, None]
    carried_factor = jnp.exp(last) * keep_in[size - 1]
    return (o_local, gmat, wmat, umat, key_boundary, carried_factor)


def to_blocks(array, stretches):
    return array.reshape((stretches, STRETCH) + array.shape[1:]).swapaxes(1, 2)


def prepare(queries, keys_n, values, beta, decay, seg, seg_prev):
    count, heads, key_dim = queries.shape
    val_dim = values.shape[2]
    stretches = count // STRETCH
    items = (
        to_blocks(queries, stretches),
        to_blocks(keys_n, stretches),
        to_blocks(values, stretches),
        to_blocks(beta, stretches),
        to_blocks(decay, stretches),
        seg.reshape(stretches, STRETCH),
        seg_prev,
    )
    ident = jnp.broadcast_to(jnp.eye(key_dim, dtype=jnp.float32), (heads, key_dim, key_dim))

    def advance(carry, item):
        memory_state, transform = carry
        o_local, gmat, wmat, umat, key_boundary, carried_factor = stretch_terms(*item)
        output = o_local + batch_mm(gmat, memory_state)
        reach = batch_mm(gmat, transform)
        shifted_state = umat - batch_mm(wmat, memory_state)
        newest_state = carried_factor[:, None, None] * memory_state + jnp.einsum(
            "izg,izu->igu", key_boundary, shifted_state, precision=EXACT_PRECISION
        )
        step_map = carried_factor[:, None, None] * ident - jnp.einsum(
            "hck,hcj->hkj", key_boundary, wmat, precision=EXACT_PRECISION
        )
        return ((newest_state, batch_mm(step_map, transform)), (output, reach))

    start = (jnp.zeros((heads, key_dim, val_dim), jnp.float32), ident)
    (b_state, a_mat), (output_rows, reaches) = lax.scan(advance, start, items)
    output_empty = output_rows.transpose(1, 0, 2, 3).reshape(heads, count, val_dim)
    rotation_matrix = reaches.transpose(1, 0, 2, 3).reshape(heads, count, key_dim)
    return (output_empty, b_state, a_mat, rotation_matrix)


def gated_norm(output_rows, gate_logit, gain):
    scaled = (
        output_rows
        * lax.rsqrt(jnp.mean(output_rows * output_rows, axis=-1, keepdims=True) + 1e-05)
        * gain
    )
    return scaled * jax.nn.silu(gate_logit)


def swiglu(gate_up):
    half = gate_up.shape[1] // 2
    return jax.nn.silu(gate_up[:, :half]) * gate_up[:, half:]


def left_product(left, right):
    return lax.dot_general(
        left, right, (((0,), (0,)), ((), ())), preferred_element_type=jnp.float32
    )


def right_product(left, right):
    return lax.dot_general(
        left, right, (((1,), (1,)), ((), ())), preferred_element_type=jnp.float32
    )


def body(
    layer_in,
    out_grad,
    seq_lengths,
    dealing,
    log_decay,
    w_qkv,
    w_out_gate,
    w_beta,
    conv_w,
    gain_in,
    gain_o,
    w_out,
    gain_mid,
    w_gate_up,
    w_down,
):
    count = layer_in.shape[1]
    taps = conv_w.shape[1]
    seq_count = lax.axis_size("seq")
    seq_rank = lax.axis_index("seq")
    first_row = seq_rank * count
    lengths = seq_lengths[0]
    order = dealing[0]
    group_tok = order.shape[0]
    decay = log_decay[0]
    dealt_pair = (
        lax.all_gather(layer_in[0], "seq", axis=0, tiled=True),
        lax.all_gather(out_grad[0], "seq", axis=0, tiled=True),
    )
    own_rows = lax.dynamic_slice_in_dim(order, first_row, count)
    packed = dealt_pair[0][own_rows].astype(jnp.float32)
    packed_grad = dealt_pair[1][own_rows].astype(jnp.float32)
    positions = first_row + jnp.arange(count, dtype=jnp.int32)
    seg_now = segments(positions, lengths)
    seg_ext = segments(
        first_row - (taps - 1) + jnp.arange(count + taps - 1, dtype=jnp.int32), lengths
    )
    seg_prev = segments(
        first_row + jnp.arange(count // STRETCH, dtype=jnp.int32) * STRETCH - 1, lengths
    )
    mixer = (
        lax.all_gather(w_qkv, ("seq", "mp"), axis=0, tiled=True),
        lax.all_gather(w_out_gate, ("seq", "mp"), axis=0, tiled=True),
        lax.all_gather(w_beta, ("seq", "mp"), axis=0, tiled=True),
        lax.all_gather(conv_w, ("seq", "mp"), axis=0, tiled=True),
        lax.all_gather(gain_in, ("seq", "mp"), axis=0, tiled=True),
        lax.all_gather(gain_o, ("seq", "mp"), axis=0, tiled=True),
        lax.all_gather(w_out, ("seq", "mp"), axis=1, tiled=True),
    )
    full_qkv, full_gate, full_beta, full_conv, full_gin, full_go, full_out = mixer
    normed_f, pull_in = jax.vjp(rms_scale, packed, full_gin.astype(jnp.float32))
    normed = normed_f.astype(jnp.bfloat16)
    proj = jnp.dot(normed, full_qkv, preferred_element_type=jnp.float32).astype(jnp.bfloat16)
    edge_rows = shifted(proj[count - (taps - 1) :], "seq", 1)
    extended = jnp.concatenate([edge_rows, proj], 0).astype(jnp.float32)
    beta_logit = jnp.dot(normed, full_beta, preferred_element_type=jnp.float32)
    gate_logit = jnp.dot(normed, full_gate, preferred_element_type=jnp.float32).reshape(
        count, HEAD_COUNT, DV
    )

    def local_mix(ext_values, conv_values, logits):
        feats = conv_mix(ext_values, seg_ext, conv_values)
        queries, keys_n, values = split_feats(feats, HEAD_COUNT, DK, DV)
        return prepare(queries, keys_n, values, jax.nn.sigmoid(logits), decay, seg_now, seg_prev)

    (output_empty, b_state, a_mat, rotation_matrix), pull_mix = jax.vjp(
        local_mix, extended, full_conv.astype(jnp.float32), beta_logit
    )
    arriving_state = jnp.zeros_like(b_state)
    for hop_index in range(seq_count - 1):
        leaving = batch_mm(a_mat, arriving_state) + b_state
        arriving_state = shifted(leaving, "seq", 1)
    output_rows = (
        output_empty
        + jnp.einsum("obi,oin->obn", rotation_matrix, arriving_state, precision=EXACT_PRECISION)
    ).transpose(1, 0, 2)
    gated, pull_gate = jax.vjp(gated_norm, output_rows, gate_logit, full_go.astype(jnp.float32))
    attn_out = gated.reshape(count, HEAD_COUNT * DV).astype(jnp.bfloat16)
    residual = packed + jnp.dot(attn_out, full_out, preferred_element_type=jnp.float32)
    mlp = (
        lax.all_gather(w_gate_up, ("seq", "mp"), axis=0, tiled=True),
        lax.all_gather(w_down, ("seq", "mp"), axis=1, tiled=True),
        lax.all_gather(gain_mid, ("seq", "mp"), axis=0, tiled=True),
    )
    full_gu, full_down, full_gmid = mlp
    mid_f, pull_mid = jax.vjp(rms_scale, residual, full_gmid.astype(jnp.float32))
    mid_normed = mid_f.astype(jnp.bfloat16)
    gate_up = jnp.dot(mid_normed, full_gu, preferred_element_type=jnp.float32)
    hidden_f, pull_act = jax.vjp(swiglu, gate_up)
    hidden = hidden_f.astype(jnp.bfloat16)
    layer_out = residual + jnp.dot(hidden, full_down, preferred_element_type=jnp.float32)
    out_rows = layer_out.astype(jnp.bfloat16)
    back_gu, back_down = (
        lax.all_gather(w_gate_up, ("seq", "mp"), axis=0, tiled=True),
        lax.all_gather(w_down, ("seq", "mp"), axis=1, tiled=True),
    )
    down_grad = packed_grad.astype(jnp.bfloat16)
    g_down = left_product(hidden, down_grad)
    hidden_grad = right_product(down_grad, back_down)
    (gu_grad,) = pull_act(hidden_grad)
    gu_grad_b = gu_grad.astype(jnp.bfloat16)
    g_gu = left_product(mid_normed, gu_grad_b)
    mid_grad = right_product(gu_grad_b, back_gu)
    res_part, g_mid = pull_mid(mid_grad)
    res_grad = packed_grad + res_part
    mlp_sums = (
        lax.psum_scatter(g_gu, ("seq", "mp"), scatter_dimension=0, tiled=True),
        lax.psum_scatter(g_down, ("seq", "mp"), scatter_dimension=1, tiled=True),
        lax.psum_scatter(g_mid, ("seq", "mp"), scatter_dimension=0, tiled=True),
    )
    back_qkv, back_gate, back_beta, back_out = (
        lax.all_gather(w_qkv, ("seq", "mp"), axis=0, tiled=True),
        lax.all_gather(w_out_gate, ("seq", "mp"), axis=0, tiled=True),
        lax.all_gather(w_beta, ("seq", "mp"), axis=0, tiled=True),
        lax.all_gather(w_out, ("seq", "mp"), axis=1, tiled=True),
    )
    out_proj_grad = res_grad.astype(jnp.bfloat16)
    g_out = left_product(attn_out, out_proj_grad)
    attn_grad = right_product(out_proj_grad, back_out).reshape(count, HEAD_COUNT, DV)
    o_grad, gate_grad, g_go = pull_gate(attn_grad)
    gate_grad_b = gate_grad.reshape(count, HEAD_COUNT * DV).astype(jnp.bfloat16)
    g_gate = left_product(normed, gate_grad_b)
    normed_grad = right_product(gate_grad_b, back_gate)
    output_gradient_head = o_grad.transpose(1, 0, 2)
    local_reverse = jnp.einsum(
        "bui,bum->bim", rotation_matrix, output_gradient_head, precision=EXACT_PRECISION
    )
    a_turned = a_mat.transpose(0, 2, 1)
    trailing_state = jnp.zeros_like(local_reverse)
    for hop_index in range(seq_count - 1):
        leaving_grad = batch_mm(a_turned, trailing_state) + local_reverse
        trailing_state = shifted(leaving_grad.astype(jnp.bfloat16), "seq", -1).astype(
            leaving_grad.dtype
        )
    transition_gradient = jnp.einsum(
        "rwb,rab->rwa", trailing_state, arriving_state, precision=EXACT_PRECISION
    )
    r_grad = jnp.einsum(
        "htv,hjv->htj", output_gradient_head, arriving_state, precision=EXACT_PRECISION
    )
    ext_grad, g_conv, logit_grad = pull_mix(
        (output_gradient_head, trailing_state, transition_gradient, r_grad)
    )
    returned = shifted(ext_grad[: taps - 1].astype(jnp.bfloat16), "seq", -1).astype(jnp.float32)
    proj_grad = ext_grad[taps - 1 :].at[count - (taps - 1) :].add(returned)
    proj_grad_b = proj_grad.astype(jnp.bfloat16)
    logit_grad_b = logit_grad.astype(jnp.bfloat16)
    g_qkv = left_product(normed, proj_grad_b)
    g_beta = left_product(normed, logit_grad_b)
    normed_grad = (
        normed_grad + right_product(proj_grad_b, back_qkv) + right_product(logit_grad_b, back_beta)
    )
    in_part, g_gin = pull_in(normed_grad)
    in_grad = res_grad + in_part
    mixer_sums = (
        lax.psum_scatter(g_qkv, ("seq", "mp"), scatter_dimension=0, tiled=True),
        lax.psum_scatter(g_gate, ("seq", "mp"), scatter_dimension=0, tiled=True),
        lax.psum_scatter(g_beta, ("seq", "mp"), scatter_dimension=0, tiled=True),
        lax.psum_scatter(g_conv, ("seq", "mp"), scatter_dimension=0, tiled=True),
        lax.psum_scatter(g_gin, ("seq", "mp"), scatter_dimension=0, tiled=True),
        lax.psum_scatter(g_go, ("seq", "mp"), scatter_dimension=0, tiled=True),
        lax.psum_scatter(g_out, ("seq", "mp"), scatter_dimension=1, tiled=True),
    )
    back_pair = (
        lax.all_gather(out_rows, "seq", axis=0, tiled=True),
        lax.all_gather(in_grad.astype(jnp.bfloat16), "seq", axis=0, tiled=True),
    )
    inverse = (
        jnp.zeros((group_tok,), jnp.int32).at[order].set(jnp.arange(group_tok, dtype=jnp.int32))
    )
    picked = lax.dynamic_slice_in_dim(inverse, first_row, count)
    mixed_rows = back_pair[0][picked][None]
    grad_rows = back_pair[1][picked][None]
    return (
        mixed_rows,
        grad_rows,
        mixer_sums[0],
        mixer_sums[1],
        mixer_sums[2],
        mixer_sums[3],
        mixer_sums[4],
        mixer_sums[5],
        mixer_sums[6],
        mlp_sums[2],
        mlp_sums[0],
        mlp_sums[1],
    )


def solution(mesh):
    in_specs = (
        P("mp", "seq", None),
        P("mp", "seq", None),
        P("mp", None),
        P("mp", None),
        P("mp", "seq", None),
        P(("seq", "mp"), None),
        P(("seq", "mp"), None),
        P(("seq", "mp"), None),
        P(("seq", "mp"), None),
        P(("seq", "mp")),
        P(("seq", "mp")),
        P(None, ("seq", "mp")),
        P(("seq", "mp")),
        P(("seq", "mp"), None),
        P(None, ("seq", "mp")),
    )
    out_specs = (
        P("mp", "seq", None),
        P("mp", "seq", None),
        P(("seq", "mp"), None),
        P(("seq", "mp"), None),
        P(("seq", "mp"), None),
        P(("seq", "mp"), None),
        P(("seq", "mp")),
        P(("seq", "mp")),
        P(None, ("seq", "mp")),
        P(("seq", "mp")),
        P(("seq", "mp"), None),
        P(None, ("seq", "mp")),
    )
    return jax.shard_map(body, mesh=mesh, in_specs=in_specs, out_specs=out_specs, check_vma=False)
```

profile of v0, /device:TPU:0, one launch (start us, length us, event | category | flops | bytes accessed | tf_op | source)
XLA Modules:
  0.0 2411.1 jit_solution(1812203057428292193)
XLA Ops:
  13.4 43.3 %all_gather.51 = bf16[4096,4]{0,1:T(4,128)(2,1)S(1)} all-gather(bf16[128,4]{0,1:T(4,128)(2,1)S(1)} %copy-done.63), channel_id=1, replica_groups=mesh['seq'=4,'mp'=8] {'seq','mp'}, dimensions={0}, use_global_device_ids=true | all-gather | bytes 33792 | tf_op jit(solution)/shard_map/all_gather | solution.py:206
  58.3 37.5 %all-reduce.20 = (bf16[1024]{0:T(1024)(128)(2,1)S(1)}, bf16[256]{0:T(256)(128)(2,1)S(1)}, bf16[1024]{0:T(1024)(128)(2,1)S(1)}) all-reduce(bf16[1024]{0:T(1024)(128)(2,1)S(1)} %dynamic-update-slice.3, bf16[256]{0:T(256)(128)(2,1)S(1)} %dynamic-update-slice.4, ...), channel_id=1, replica_groups=mesh['seq'=4,'mp'=8] {'seq','mp'}, use_global_device_ids=true, to_apply=%add.13 | all-reduce | flops 2304 | bytes 9216
  96.0 41.2 %all-gather.2 = bf16[32,32,8]{1,2,0:T(8,128)(2,1)S(1)} all-gather(bf16[1,32,8]{1,2,0:T(8,128)(2,1)S(1)} %bitcast.936), channel_id=1, replica_groups=mesh['seq'=4,'mp'=8] {'seq','mp'}, dimensions={0}, use_global_device_ids=true | all-gather | bytes 16896 | tf_op jit(solution)/shard_map/all_gather | solution.py:205
  137.3 5.1 gather_fusion
  142.7 7.6 convolution_convert_fusion
  158.5 6.2 fusion.257
  192.2 242.9 %while.120 = (s32[]{:T(128)}, f32[8,128,256]{2,1,0:T(8,128)S(1)}, f32[8,128,128]{2,1,0:T(8,128)S(1)}, f32[6,8,64,256]{3,2,0,1:T(8,128)}, f32[6,8,64,128]{3,2,0,1...) while((s32[]{:T(128)}, f32[8,128,256]{2,1,0:T(8,128)S(1)}, ...), condition=%wide.region_8.9_spmd.clone.clone, body=%wide.region_6.8_spmd.clone.clone.sunk | while | flops 1664999680 | bytes 35568512 | solution.py:129
  435.7 4.7 collective-permute-start.1
  440.5 32.3 %collective-permute-done.1 = f32[8,128,256]{2,1,0:T(8,128)S(1)} collective-permute-done((f32[8,128,256]{2,1,0:T(8,128)S(1)}, f32[8,128,256]{2,1,0:T(8,128)S(1)}, u32[]{:S(2)}, u32[]{:S(2)}) %collective-permute-start.1) | collective-permute-done | bytes 1048608 | tf_op jit(solution)/shard_map/ppermute | solution.py:18
  473.8 4.8 collective-permute-start.2
  478.7 20.8 collective-permute-done.2
  501.5 5.3 collective-permute-start.3
  506.8 5.7 gather_fusion.2
  516.0 10.9 collective-permute-done.3
  527.9 7.3 fusion.265
  535.2 8.3 multiply_convert_fusion.1
  543.5 5.7 multiply_reduce_fusion.9
  549.3 12.8 fusion.319
  562.1 10.0 fusion.296
  572.1 13.7 multiply_reduce_fusion.6
  592.4 5.1 multiply_reduce_fusion.5
  604.7 12.5 collective-permute-done.4
  619.1 11.7 collective-permute-done.5
  637.5 7.0 fusion.337
  652.4 471.4 %while.119 = (s32[]{:T(128)}, f32[8,128,256]{2,1,0:T(8,128)S(1)}, f32[8,128,128]{2,1,0:T(8,128)}, f32[6,8,64,128]{3,2,1,0:T(8,128)}, f32[6,8,64,128]{3,1,2,0:T(8...) while((s32[]{:T(128)}, f32[8,128,256]{2,1,0:T(8,128)S(1)}, ...), condition=%wide.region_18.19_spmd.clone, body=%wide.region_14.18_spmd.clone.sunk | while | flops 3325427712 | bytes 69937352 | solution.py:129
  1143.1 9.0 multiply_reduce_fusion.4
  1155.6 6.6 add_convert_fusion.1
  1162.6 5.8 fusion.334
  1168.4 5.7 broadcast_multiply_fusion
  1174.1 6.2 pad_add_fusion
  1189.1 9.1 fusion.272
  1199.7 7.3 fusion.322
  1207.5 7.0 fusion.297
  1215.7 7.6 fusion.339
  1223.3 10.2 fusion.279
  1234.9 14.5 fusion.291
  1250.1 6.2 scatter_custom_fusion
  1256.4 41.6 %all-reduce.19 = (f32[1024]{0:T(1024)S(1)}, f32[256]{0:T(256)S(1)}, f32[1024]{0:T(1024)S(1)}) all-reduce(f32[1024]{0:T(1024)S(1)} %get-tuple-element.2717, f32[256]{0:T(256)S(1)} %copy-done.60, f32[1024]{0:T(1024)S(1)} %copy-done.61), channel_id=8, replica_groups=mesh['seq'=4,'mp'=8] {'seq','mp'}, use_global_device_ids=true, to_apply=%region_30.31.clone | all-reduce | flops 2304 | bytes 18432
  1301.2 106.8 %reduce-scatter.24.cloned.1.call-done = f32[128,4]{1,0:T(8,128)} async-done(((f32[4096,4]{1,0:T(8,128)}), f32[128,4]{1,0:T(8,128)}) %reduce-scatter.24.cloned.1.call-update) | async-done | bytes 2064
  1409.4 41.3 %all-gather.23.cloned.1.call-done = bf16[1536,1024]{1,0:T(8,128)(2,1)} async-done(((bf16[384,1024]{1,0:T(8,128)(2,1)}), bf16[1536,1024]{1,0:T(8,128)(2,1)}) %all-gather.23.cloned.1.call-update) | async-done | bytes 3145744 | tf_op jit(solution)/shard_map/all_gather | solution.py:326
  1450.7 5.7 gather_fusion.1
  1456.4 40.2 %all-gather.25.cloned.1.call-done = bf16[1536,1024]{1,0:T(8,128)(2,1)} async-done(((bf16[384,1024]{1,0:T(8,128)(2,1)}), bf16[1536,1024]{1,0:T(8,128)(2,1)}) %all-gather.25.cloned.1.call-update) | async-done | bytes 3145744 | tf_op jit(solution)/shard_map/all_gather | solution.py:327
  1496.6 5.7 gather_fusion.3
  1502.3 149.2 %reduce-scatter.14.cloned.1.call-done = f32[32,2048]{1,0:T(8,128)} async-done(((f32[1024,2048]{1,0:T(8,128)}), f32[32,2048]{1,0:T(8,128)}) %reduce-scatter.14.cloned.1.call-update) | async-done | bytes 262160 | tf_op jit(solution)/shard_map/reduce_scatter | solution.py:318
  1651.5 152.3 %reduce-scatter.16.cloned.1.call-done = f32[2048,32]{0,1:T(8,128)} async-done(((f32[2048,1024]{0,1:T(8,128)}), f32[2048,32]{0,1:T(8,128)}) %reduce-scatter.16.cloned.1.call-update) | async-done | bytes 262160 | tf_op jit(solution)/shard_map/reduce_scatter | solution.py:323
  1803.8 161.0 %reduce-scatter.20.cloned.1.call-done = f32[2816,32]{0,1:T(8,128)} async-done(((f32[2816,1024]{0,1:T(8,128)}), f32[2816,32]{0,1:T(8,128)}) %reduce-scatter.20.cloned.1.call-update) | async-done | bytes 360464 | tf_op jit(solution)/shard_map/reduce_scatter | solution.py:269
  1964.8 187.0 %reduce-scatter.12.cloned.1.call-done = f32[32,4096]{1,0:T(8,128)} async-done(((f32[1024,4096]{1,0:T(8,128)}), f32[32,4096]{1,0:T(8,128)}) %reduce-scatter.12.cloned.1.call-update) | async-done | bytes 524304 | tf_op jit(solution)/shard_map/reduce_scatter | solution.py:317
  2151.8 252.6 %reduce-scatter.18.cloned.1.call-done = f32[32,5632]{1,0:T(8,128)} async-done(((f32[1024,5632]{1,0:T(8,128)}), f32[32,5632]{1,0:T(8,128)}) %reduce-scatter.18.cloned.1.call-update) | async-done | bytes 720912 | tf_op jit(solution)/shard_map/reduce_scatter | solution.py:268
  (919 shorter events, 821.8 us)
Async XLA Ops:
  7.2 50.3 %copy-start.66 = (bf16[32]{0:T(256)(128)(2,1)S(1)}, bf16[32]{0:T(256)(128)(2,1)}, u32[]{:S(2)}) copy-start(bf16[32]{0:T(256)(128)(2,1)} %param.30) | copy-start | bytes 196
  7.2 50.6 %copy-start.67 = (bf16[32]{0:T(256)(128)(2,1)S(1)}, bf16[32]{0:T(256)(128)(2,1)}, u32[]{:S(2)}) copy-start(bf16[32]{0:T(256)(128)(2,1)} %param.33) | copy-start | bytes 196
  7.2 50.8 %copy-start.68 = (bf16[8]{0:T(256)(128)(2,1)S(1)}, bf16[8]{0:T(256)(128)(2,1)}, u32[]{:S(2)}) copy-start(bf16[8]{0:T(256)(128)(2,1)} %param.31) | copy-start | bytes 52
  7.2 88.7 %copy-start.62 = (bf16[32,8]{0,1:T(8,128)(2,1)S(1)}, bf16[32,8]{0,1:T(8,128)(2,1)}, u32[]{:S(2)}) copy-start(bf16[32,8]{0,1:T(8,128)(2,1)} %param.28) | copy-start | bytes 1540
  7.2 130.1 %all-gather.27.cloned.1.call-start = ((), (), s32[]{:S(2)}) async-start(), calls=%async_computation.19 | async-start | bytes 3932160 | tf_op jit(solution)/shard_map/all_gather | solution.py:188
  8.0 134.7 %all-gather.13.cloned.1.call-start = ((), (), s32[]{:S(2)}) async-start(), calls=%async_computation.7 | async-start | bytes 8650752 | tf_op jit(solution)/shard_map/all_gather | solution.py:203
  8.7 498.1 %all-gather.29.cloned.1.call-start = ((), (), s32[]{:S(2)}) async-start(), calls=%async_computation.20 | async-start | bytes 3932160 | tf_op jit(solution)/shard_map/all_gather | solution.py:189
  9.5 525.7 %all-gather.15.cloned.1.call-start = ((), (), s32[]{:S(2)}) async-start(), calls=%async_computation.8 | async-start | bytes 4325376 | tf_op jit(solution)/shard_map/all_gather | solution.py:204
  10.0 533.5 %all-gather.17.cloned.1.call-start = ((), (), s32[]{:S(2)}) async-start(), calls=%async_computation.9 | async-start | bytes 4325376 | tf_op jit(solution)/shard_map/all_gather | solution.py:209
  10.6 538.6 %all-gather.19.cloned.1.call-start = ((), (), s32[]{:S(2)}) async-start(), calls=%async_computation.10 | async-start | bytes 11894784 | tf_op jit(solution)/shard_map/all_gather | solution.py:242
  11.2 550.9 %all-gather.21.cloned.1.call-start = ((), (), s32[]{:S(2)}) async-start(), calls=%async_computation.11 | async-start | bytes 5947392 | tf_op jit(solution)/shard_map/all_gather | solution.py:243
  12.0 1287.8 %reduce-scatter.22.cloned.1.call-start = ((), (), s32[]{:S(2)}) async-start(), calls=%async_computation.21 | async-start | bytes 540672
  56.8 101.7 %copy-start.33 = (f32[4096,1]{0,1:T(1,128)}, f32[4096,1]{0,1:T(1,128)S(1)}, u32[]{:S(2)}) copy-start(f32[4096,1]{0,1:T(1,128)S(1)} %get-tuple-element.3000) | copy-start | bytes 49156
  56.8 101.7 %copy-start.35 = (f32[4096,1]{0,1:T(1,128)}, f32[4096,1]{0,1:T(1,128)S(1)}, u32[]{:S(2)}) copy-start(f32[4096,1]{0,1:T(1,128)S(1)} %get-tuple-element.3001) | copy-start | bytes 49156
  56.8 101.7 %copy-start.37 = (f32[4096,1]{0,1:T(1,128)}, f32[4096,1]{0,1:T(1,128)S(1)}, u32[]{:S(2)}) copy-start(f32[4096,1]{0,1:T(1,128)S(1)} %get-tuple-element.3002) | copy-start | bytes 49156
  56.8 101.7 %copy-start.39 = (f32[4096,1]{0,1:T(1,128)}, f32[4096,1]{0,1:T(1,128)S(1)}, u32[]{:S(2)}) copy-start(f32[4096,1]{0,1:T(1,128)S(1)} %get-tuple-element.3003) | copy-start | bytes 49156
  96.0 62.6 %copy-start.50 = (f32[384]{0:T(512)}, f32[384]{0:T(512)S(1)}, u32[]{:S(2)}) copy-start(f32[384]{0:T(512)S(1)} %get-tuple-element.3004) | copy-start | bytes 4612
  96.0 62.6 %copy-start.52 = (f32[384]{0:T(512)}, f32[384]{0:T(512)S(1)}, u32[]{:S(2)}) copy-start(f32[384]{0:T(512)S(1)} %get-tuple-element.3005) | copy-start | bytes 4612
  96.0 62.6 %copy-start.54 = (f32[384]{0:T(512)}, f32[384]{0:T(512)S(1)}, u32[]{:S(2)}) copy-start(f32[384]{0:T(512)S(1)} %get-tuple-element.3006) | copy-start | bytes 4612
  137.3 16.3 copy-start.46
  142.4 11.2 copy-start.6
  142.6 7.6 copy-start.56
  152.0 3.6 collective-permute-start
  435.2 38.7 %copy-start.43 = (f32[6,8,64]{2,1,0:T(8,128)}, f32[6,8,64]{2,1,0:T(8,128)S(1)}, u32[]{:S(2)}) copy-start(f32[6,8,64]{2,1,0:T(8,128)S(1)} %get-tuple-element.3935) | copy-start | bytes 36868
  435.7 37.1 %collective-permute-start.1 = (f32[8,128,256]{2,1,0:T(8,128)S(1)}, f32[8,128,256]{2,1,0:T(8,128)S(1)}, u32[]{:S(2)}, u32[]{:S(2)}) collective-permute-start(f32[8,128,256]{2,1,0:T(8,128)S(1)} %convolution_add_fusion.32), channel_id=1, source_target_pairs={{0,8},{8,16},{16,24},{1,9},{9,17},{17,25},{2,10},{10,18},{18,26},{... | collective-permute-start | bytes 3145736 | tf_op jit(solution)/shard_map/ppermute | solution.py:18
  473.8 25.6 %collective-permute-start.2 = (f32[8,128,256]{2,1,0:T(8,128)S(1)}, f32[8,128,256]{2,1,0:T(8,128)S(1)}, u32[]{:S(2)}, u32[]{:S(2)}) collective-permute-start(f32[8,128,256]{2,1,0:T(8,128)S(1)} %convolution_add_fusion.31), channel_id=1, source_target_pairs={{0,8},{8,16},{16,24},{1,9},{9,17},{17,25},{2,10},{10,18},{18,26},{... | collective-permute-start | bytes 3145736 | tf_op jit(solution)/shard_map/ppermute | solution.py:18
  501.5 25.4 %collective-permute-start.3 = (f32[8,128,256]{2,1,0:T(8,128)}, f32[8,128,256]{2,1,0:T(8,128)S(1)}, u32[]{:S(2)}, u32[]{:S(2)}) collective-permute-start(f32[8,128,256]{2,1,0:T(8,128)} %convolution_add_fusion.30), channel_id=1, source_target_pairs={{0,8},{8,16},{16,24},{1,9},{9,17},{17,25},{2,10},{10,18},{18,26},{... | collective-permute-start | bytes 3145736 | tf_op jit(solution)/shard_map/ppermute | solution.py:18
  506.8 79.0 %copy-start.31 = (f32[1024]{0:T(1024)}, f32[1024]{0:T(1024)S(1)}, u32[]{:S(2)}) copy-start(f32[1024]{0:T(1024)S(1)} %convert_element_type.159) | copy-start | bytes 12292
  527.9 7.3 copy-start.7
  549.2 36.6 %copy-start.44 = (f32[384]{0:T(512)}, f32[384]{0:T(512)S(1)}, u32[]{:S(2)}) copy-start(f32[384]{0:T(512)S(1)} %fusion.313) | copy-start | bytes 4612
  549.3 12.8 copy-start.22
  598.9 18.9 copy-start.4
  603.4 13.8 collective-permute-start.4
  617.8 13.0 collective-permute-start.5
  632.3 13.6 collective-permute-start.6
  652.4 471.5 %copy-start.49 = (f32[384,8]{0,1:T(8,128)S(1)}, f32[384,8]{0,1:T(8,128)}, u32[]{:S(2)}) copy-start(f32[384,8]{0,1:T(8,128)} %copy-done.48) | copy-start | bytes 36868
  1137.9 270.0 %reduce-scatter.24.cloned.1.call-start = ((), (), s32[]{:S(2)}) async-start(), calls=%async_computation.22 | async-start | bytes 2162688
  1154.2 296.5 %all-gather.23.cloned.1.call-start = ((), (), s32[]{:S(2)}) async-start(), calls=%async_computation.12 | async-start | bytes 3932160 | tf_op jit(solution)/shard_map/all_gather | solution.py:326
  1162.2 334.4 %all-gather.25.cloned.1.call-start = ((), (), s32[]{:S(2)}) async-start(), calls=%async_computation.13 | async-start | bytes 3932160 | tf_op jit(solution)/shard_map/all_gather | solution.py:327
  1174.1 7.6 copy-start.47
  1180.4 7.1 collective-permute-start.7
  1189.1 9.1 copy-start.57
  1189.1 9.2 copy-start.14
  1199.6 451.8 %reduce-scatter.14.cloned.1.call-start = ((), (), s32[]{:S(2)}) async-start(), calls=%async_computation.15 | async-start | bytes 8650752 | tf_op jit(solution)/shard_map/reduce_scatter | solution.py:318
  1207.0 596.7 %reduce-scatter.16.cloned.1.call-start = ((), (), s32[]{:S(2)}) async-start(), calls=%async_computation.16 | async-start | bytes 8650752 | tf_op jit(solution)/shard_map/reduce_scatter | solution.py:323
  1214.6 750.2 %reduce-scatter.20.cloned.1.call-start = ((), (), s32[]{:S(2)}) async-start(), calls=%async_computation.18 | async-start | bytes 11894784 | tf_op jit(solution)/shard_map/reduce_scatter | solution.py:269
  1223.2 928.5 %reduce-scatter.12.cloned.1.call-start = ((), (), s32[]{:S(2)}) async-start(), calls=%async_computation.14 | async-start | bytes 17301504 | tf_op jit(solution)/shard_map/reduce_scatter | solution.py:317
  1233.5 1170.9 %reduce-scatter.18.cloned.1.call-start = ((), (), s32[]{:S(2)}) async-start(), calls=%async_computation.17 | async-start | bytes 23789568 | tf_op jit(solution)/shard_map/reduce_scatter | solution.py:268
  (60 other events, 197.9 us)
Sparse Core Ops, SparseCore 0:
  9.9 46.7 all-gather.26
  59.7 78.0 all-gather.12
  139.7 43.0 all-gather.28
  185.7 62.1 all-gather.14
  250.7 60.7 all-gather.16
  314.2 90.0 all-gather.18
  407.1 76.0 all-gather.20
  1138.1 134.5 reduce-scatter.21
  1275.0 132.9 reduce-scatter.23
  1410.2 40.4 all-gather.22
  1452.6 43.9 all-gather.24
  1499.3 152.0 reduce-scatter.13
  1654.3 149.3 reduce-scatter.15
  1806.5 158.2 reduce-scatter.19
  1967.5 184.2 reduce-scatter.11
  2154.5 249.7 reduce-scatter.17
where the time goes:
time: 2430 us; the launch traced here: 2410 us
  waiting for transfers between devices  1190 us (49%)
  matrix products  770 us (32%)
  blocking collectives  164 us (7%)
  local copies, waits for them, and re-layouts  136 us (6%)
  other arithmetic  101 us (4%)
    dot_general x330, matrix products, batch_mm(): return jnp.einsum('hij,hjk->hik', left, right, precision=EXACT_PRECISION)  519 us
    reduce_scatter x1, waiting for transfers between devices, body(): lax.psum_scatter(g_gu, ('seq', 'mp'), scatter_dimension=0, tiled=True)  253 us
    reduce_scatter x1, waiting for transfers between devices, body(): lax.psum_scatter(g_qkv, ('seq', 'mp'), scatter_dimension=0, tiled=True)  187 us
    reduce_scatter x1, waiting for transfers between devices, body(): lax.psum_scatter(g_down, ('seq', 'mp'), scatter_dimension=1, tiled=True)  161 us
    reduce_scatter x1, waiting for transfers between devices, body(): lax.psum_scatter(g_out, ('seq', 'mp'), scatter_dimension=1, tiled=True)  152 us
    reduce_scatter x1, waiting for transfers between devices, body(): lax.psum_scatter(g_gate, ('seq', 'mp'), scatter_dimension=0, tiled=True)  149 us
    unnamed x18, waiting for transfers between devices  111 us
    ppermute x8, waiting for transfers between devices, shifted(): return lax.ppermute(value, axis, pairs)  91.5 us
  transfers between devices with their start and end apart: 24, of which 15 were waited for; matrix products, arithmetic and copies ran while one was open for 20% of the time, Pallas kernels for 0%

commit v1 on v0

v1 whole, which is shorter than its diff:
```python
import functools

import jax
import jax.numpy as jnp
from jax import lax
from jax.experimental import pallas as pl
from jax.experimental.pallas import tpu as pltpu
from jax.sharding import PartitionSpec as P

HEAD_COUNT = 8
DK = 128
DV = 256
BLOCK = 128
PER_STEP = 2
F32 = jnp.float32
BF16 = jnp.bfloat16


def mm(left, right):
    return jnp.dot(left.astype(BF16), right.astype(BF16), preferred_element_type=F32)


def mm_nt(left, right):
    return lax.dot_general(
        left.astype(BF16),
        right.astype(BF16),
        (((1,), (1,)), ((), ())),
        preferred_element_type=F32,
    )


def mm_tn(left, right):
    return lax.dot_general(
        left.astype(BF16),
        right.astype(BF16),
        (((0,), (0,)), ((), ())),
        preferred_element_type=F32,
    )


def masks():
    rows = lax.broadcasted_iota(jnp.int32, (BLOCK, BLOCK), 0)
    cols = lax.broadcasted_iota(jnp.int32, (BLOCK, BLOCK), 1)
    return rows, cols


def unit_inverses(mats, rows, cols):
    ident = (rows == cols).astype(F32)
    near = (rows // 16) == (cols // 16)
    power = [jnp.where(near, a, 0.0) for a in mats]
    result = [ident - p for p in power]
    span = 2
    while span < 16:
        power = [mm(p, p) for p in power]
        result = [t + mm(t, p) for t, p in zip(result, power)]
        span *= 2
    size = 16
    while size < BLOCK:
        off = ((rows // (2 * size)) == (cols // (2 * size))) & ((rows // size) != (cols // size))
        reach = [mm(jnp.where(off, a, 0.0), t) for a, t in zip(mats, result)]
        result = [t - mm(t, x) for t, x in zip(result, reach)]
        size *= 2
    return result


def convolve(ext_ref, conv_ref, col_ref, start, first, width):
    cols = pl.ds(first, width)
    total = ext_ref[pl.ds(16 + start, BLOCK), cols] * conv_ref[3:4, cols]
    for tap in range(3):
        keep = col_ref[pl.ds(start, BLOCK), tap : tap + 1]
        total += ext_ref[pl.ds(13 + tap + start, BLOCK), cols] * keep * conv_ref[tap : tap + 1, cols]
    return total


def column(col_ref, start, index):
    return col_ref[pl.ds(start, BLOCK), index : index + 1]


def strength(logit_ref, start, head, heads):
    return jax.nn.sigmoid(column(logit_ref, start, head))


def exact_nt(left, right):
    left_high, right_high = left.astype(BF16), right.astype(BF16)
    left_low = left - left_high.astype(F32)
    right_low = right - right_high.astype(F32)
    return mm_nt(left_high, right_high) + (mm_nt(left_high, right_low) + mm_nt(left_low, right_high))


def decay_matrix(col_ref, row_ref, start, head, heads, rows, cols):
    cum_i = column(col_ref, start, 5 + head)
    cum_j = row_ref[head : head + 1, pl.ds(start, BLOCK)]
    seg_i = column(col_ref, start, 3)
    seg_j = row_ref[heads : heads + 1, pl.ds(start, BLOCK)]
    within = (rows >= cols) & (seg_i == seg_j)
    return jnp.where(within, jnp.exp(jnp.where(within, cum_i - cum_j, 0.0)), 0.0)


def silu(values):
    return values * jax.nn.sigmoid(values)


def forward_kernel(
    heads, edge_ref, proj_ref, conv_ref, col_ref, row_ref, logit_ref,
    o_ref, s_ref, n_ref, t_ref, w_ref, p_ref, ext_ref, state_ref,
):
    steps = proj_ref.shape[0] // BLOCK

    @pl.when(pl.program_id(0) == 0)
    def _():
        state_ref[...] = jnp.zeros_like(state_ref)

    ext_ref[:16, :] = edge_ref[...].astype(F32)
    ext_ref[16:, :] = proj_ref[...].astype(F32)
    rows, cols = masks()
    strict = rows > cols
    units = [(g, h) for g in range(steps) for h in range(heads)]
    queries, keys, values, mats, decays, betas = {}, {}, {}, [], {}, {}
    for g, h in units:
        start = g * BLOCK
        taken = functools.partial(convolve, ext_ref, conv_ref, col_ref, start)
        queries[g, h] = silu(taken(h * DK, DK))
        raw = silu(taken((heads + h) * DK, DK))
        keys[g, h] = raw * lax.rsqrt(jnp.sum(raw * raw, axis=1, keepdims=True) + 1e-06)
        values[g, h] = silu(taken(2 * heads * DK + h * DV, DV))
        decays[g, h] = decay_matrix(col_ref, row_ref, start, h, heads, rows, cols)
        betas[g, h] = strength(logit_ref, start, h, heads)
        beta = betas[g, h]
        inner = mm_nt(keys[g, h], keys[g, h])
        mats.append(jnp.where(strict, beta * inner * decays[g, h], 0.0))
    inverses = unit_inverses(mats, rows, cols)
    umats, wmats, pmats, boundary, reads = {}, {}, {}, {}, {}
    for (g, h), inverse in zip(units, inverses):
        start = g * BLOCK
        beta = betas[g, h]
        elog = column(col_ref, start, 5 + heads + h)
        flog = column(col_ref, start, 5 + 2 * heads + h)
        inverse = inverse.astype(BF16)
        t_ref[g, h] = inverse
        umats[g, h] = mm(inverse, beta * values[g, h])
        wmats[g, h] = mm(inverse, (beta * elog) * keys[g, h]).astype(BF16)
        w_ref[g, h] = wmats[g, h]
        pmats[g, h] = (exact_nt(queries[g, h], keys[g, h]) * decays[g, h]).astype(BF16)
        p_ref[g, h] = pmats[g, h]
        boundary[g, h] = (keys[g, h] * flog).T.astype(BF16)
        reads[g, h] = (queries[g, h] * elog).astype(BF16)
    for g in range(steps):
        start = g * BLOCK
        for h in range(heads):
            state = state_ref[h]
            low = state.astype(BF16)
            s_ref[g, h] = low
            news = (umats[g, h] - mm(wmats[g, h], low)).astype(BF16)
            n_ref[g, h] = news
            carried = col_ref[pl.ds(start + BLOCK - 1, 1), 5 + heads + h : 6 + heads + h]
            state_ref[h] = carried * state + mm(boundary[g, h], news)
            output = mm(reads[g, h], low) + mm(pmats[g, h], news)
            o_ref[pl.ds(start, BLOCK), h * DV : (h + 1) * DV] = output.astype(BF16)


def backward_kernel(
    heads, edge_ref, proj_ref, conv_ref, col_ref, row_ref, logit_ref,
    s_ref, n_ref, t_ref, w_ref, p_ref, do_ref, *refs,
):
    grad_ref, gconv_ref, ext_ref, shift_ref, dstate_ref, head_ref = refs[-6:]
    count = proj_ref.shape[0]
    steps = count // BLOCK
    channels = proj_ref.shape[1]

    @pl.when(pl.program_id(0) == 0)
    def _():
        dstate_ref[...] = jnp.zeros_like(dstate_ref)
        head_ref[...] = jnp.zeros_like(head_ref)
        gconv_ref[...] = jnp.zeros_like(gconv_ref)

    ext_ref[:16, :] = edge_ref[...].astype(F32)
    ext_ref[16:, :] = proj_ref[...].astype(F32)
    for tap in range(3):
        shift_ref[tap, count : count + 8, :] = head_ref[tap]
    rows, cols = masks()
    strict = rows > cols
    units = [(g, h) for g in reversed(range(steps)) for h in range(heads)]
    queries, keys, pre, reads, first, gains = {}, {}, {}, {}, {}, {}
    for g, h in units:
        start = g * BLOCK
        taken = functools.partial(convolve, ext_ref, conv_ref, col_ref, start)
        elog = column(col_ref, start, 5 + heads + h)
        out_grad = do_ref[pl.ds(start, BLOCK), h * DV : (h + 1) * DV]
        queries[g, h] = silu(taken(h * DK, DK))
        raw = silu(taken((heads + h) * DK, DK))
        scale = lax.rsqrt(jnp.sum(raw * raw, axis=1, keepdims=True) + 1e-06)
        keys[g, h] = (raw * scale, scale)
        first[g, h] = mm_tn(p_ref[g, h], out_grad)
        gains[g, h] = mm_tn(queries[g, h] * elog, out_grad)
    news_grads, state_grads = {}, {}
    for g in reversed(range(steps)):
        start = g * BLOCK
        for h in range(heads):
            flog = column(col_ref, start, 5 + 2 * heads + h)
            dstate = dstate_ref[h]
            low = dstate.astype(BF16)
            state_grads[g, h] = low
            news_grad = (first[g, h] + mm(keys[g, h][0] * flog, low)).astype(BF16)
            news_grads[g, h] = news_grad
            carried = col_ref[pl.ds(start + BLOCK - 1, 1), 5 + heads + h : 6 + heads + h]
            dstate_ref[h] = gains[g, h] + carried * dstate - mm_tn(w_ref[g, h], news_grad)
    lane = lax.broadcasted_iota(jnp.int32, (BLOCK, 128), 1)

    def through_conv(g, first_col, width, grad):
        start = g * BLOCK
        cols_ = pl.ds(first_col, width)
        value = convolve(ext_ref, conv_ref, col_ref, start, first_col, width)
        gate = jax.nn.sigmoid(value)
        grad = grad * (gate * (1.0 + value * (1.0 - gate)))
        shift_ref[3, pl.ds(start, BLOCK), cols_] = grad * conv_ref[3:4, cols_]
        sums = []
        for tap in range(3):
            kept = grad * col_ref[pl.ds(start, BLOCK), tap : tap + 1]
            shift_ref[tap, pl.ds(start, BLOCK), cols_] = kept * conv_ref[tap : tap + 1, cols_]
            sums.append(
                jnp.sum(kept * ext_ref[pl.ds(13 + tap + start, BLOCK), cols_], axis=0, keepdims=True)
            )
        sums.append(
            jnp.sum(grad * ext_ref[pl.ds(16 + start, BLOCK), cols_], axis=0, keepdims=True)
        )
        for tap in range(4):
            gconv_ref[tap : tap + 1, cols_] += sums[tap]

    logit_grads = {}
    for g, h in units:
        start = g * BLOCK
        beta = strength(logit_ref, start, h, heads)
        elog = column(col_ref, start, 5 + heads + h)
        flog = column(col_ref, start, 5 + 2 * heads + h)
        key, scale = keys[g, h]
        query = queries[g, h]
        out_grad = do_ref[pl.ds(start, BLOCK), h * DV : (h + 1) * DV]
        decay = decay_matrix(col_ref, row_ref, start, h, heads, rows, cols)
        key_low = key.astype(BF16)
        inner = mm_nt(key_low, key_low) * decay
        news, state, dstate = n_ref[g, h], s_ref[g, h], state_grads[g, h]
        rhs_grad = mm_tn(t_ref[g, h], news_grads[g, h])
        rhs_low = rhs_grad.astype(BF16)
        within = (mm_nt(out_grad, news) * decay).astype(BF16)
        mat_grad = jnp.where(strict, -mm_nt(rhs_low, news), 0.0)
        pair = (mat_grad * beta * decay).astype(BF16)
        back = mm_nt(rhs_low, state)
        q_grad = mm(within, key_low) + elog * mm_nt(out_grad, state)
        k_grad = (
            mm_tn(within, query)
            + mm(pair, key_low)
            + mm_tn(pair, key_low)
            + flog * mm_nt(news, dstate)
            - (beta * elog) * back
        )
        value = silu(convolve(ext_ref, conv_ref, col_ref, start, 2 * heads * DK + h * DV, DV))
        beta_grad = (
            jnp.sum(mat_grad * inner - elog * (key * back), axis=1, keepdims=True)
            + jnp.sum(rhs_grad * value, axis=1, keepdims=True)
        )
        logit_grads[g, h] = beta_grad * beta * (1.0 - beta)
        raw_grad = scale * (k_grad - key * jnp.sum(k_grad * key, axis=1, keepdims=True))
        through_conv(g, h * DK, DK, q_grad)
        through_conv(g, (heads + h) * DK, DK, raw_grad)
        through_conv(g, 2 * heads * DK + h * DV, DV, beta * rhs_grad)
    for g in range(steps):
        total = jnp.zeros((BLOCK, 128), F32)
        for h in range(heads):
            total = jnp.where(lane == h, logit_grads[g, h], total)
        grad_ref[pl.ds(g * BLOCK, BLOCK), channels:] = total.astype(BF16)
    total = shift_ref[3, :count, :]
    for tap in range(3):
        total += shift_ref[tap, pl.ds(3 - tap, count), :]
    grad_ref[:, :channels] = total.astype(BF16)
    for tap in range(3):
        head_ref[tap] = shift_ref[tap, :8, :]


def saved_shapes(blocks, heads):
    return (
        jax.ShapeDtypeStruct((blocks, heads, DK, DV), BF16),
        jax.ShapeDtypeStruct((blocks, heads, BLOCK, DV), BF16),
        jax.ShapeDtypeStruct((blocks, heads, BLOCK, BLOCK), BF16),
        jax.ShapeDtypeStruct((blocks, heads, BLOCK, DK), BF16),
        jax.ShapeDtypeStruct((blocks, heads, BLOCK, BLOCK), BF16),
    )


def saved_specs(shapes, index):
    return [
        pl.BlockSpec((PER_STEP,) + shape.shape[1:], lambda i: (index(i), 0, 0, 0))
        for shape in shapes
    ]


def common_specs(step, channels, logits, index):
    return [
        pl.BlockSpec((16, channels), lambda i: (jnp.maximum(index(i) * (step // 16) - 1, 0), 0)),
        pl.BlockSpec((step, channels), lambda i: (index(i), 0)),
        pl.BlockSpec((8, channels), lambda i: (0, 0)),
        pl.BlockSpec((step, 128), lambda i: (index(i), 0)),
        pl.BlockSpec((8, step), lambda i: (0, index(i))),
        pl.BlockSpec((step, logits), lambda i: (index(i), 0)),
    ]


VMEM_BYTES = 56 * 1024 * 1024
SMALL_COST = pl.CostEstimate(flops=10**6, bytes_accessed=10**6, transcendentals=0)
ANYWHERE = pl.BlockSpec(memory_space=pl.ANY)
WHOLE = pl.BlockSpec(memory_space=pltpu.VMEM)
SCALAR = pl.BlockSpec(memory_space=pltpu.SMEM)


def params():
    return pltpu.CompilerParams(dimension_semantics=("arbitrary",), vmem_limit_bytes=VMEM_BYTES)


def forward_recurrence(proj, conv, cols, rows, logits, heads):
    count, channels = proj.shape
    step = BLOCK * PER_STEP
    shapes = saved_shapes(count // BLOCK, heads)
    index = lambda i: i
    return pl.pallas_call(
        functools.partial(forward_kernel, heads),
        grid=(count // step,),
        in_specs=common_specs(step, channels, 128, index),
        out_specs=[pl.BlockSpec((step, heads * DV), lambda i: (i, 0))] + saved_specs(shapes, index),
        out_shape=(jax.ShapeDtypeStruct((count, heads * DV), BF16),) + shapes,
        scratch_shapes=[
            pltpu.VMEM((step + 16, channels), F32),
            pltpu.VMEM((heads, DK, DV), F32),
        ],
        compiler_params=params(),
        cost_estimate=SMALL_COST,
        name="recurrence_forward",
    )(proj, proj, conv, cols, rows, logits)


def backward_recurrence(proj, conv, cols, rows, logits, saved, out_grad, heads, tokens):
    count, channels = proj.shape
    step = BLOCK * PER_STEP
    last = count // step - 1
    index = lambda i: last - i
    return pl.pallas_call(
        functools.partial(backward_kernel, heads),
        grid=(count // step,),
        in_specs=common_specs(step, channels, 128, index)
        + saved_specs(saved, index)
        + [pl.BlockSpec((step, heads * DV), lambda i: (index(i), 0))]
        + [ANYWHERE] * len(tokens),
        out_specs=[
            pl.BlockSpec((step, channels + 128), lambda i: (index(i), 0)),
            pl.BlockSpec((8, channels), lambda i: (0, 0)),
        ],
        out_shape=(
            jax.ShapeDtypeStruct((count, channels + 128), BF16),
            jax.ShapeDtypeStruct((8, channels), F32),
        ),
        scratch_shapes=[
            pltpu.VMEM((step + 16, channels), F32),
            pltpu.VMEM((4, step + 8, channels), F32),
            pltpu.VMEM((heads, DK, DV), F32),
            pltpu.VMEM((3, 8, channels), F32),
        ],
        compiler_params=params(),
        cost_estimate=SMALL_COST,
        name="recurrence_backward",
    )(proj, proj, conv, cols, rows, logits, *saved, out_grad, *tokens)


def project_kernel(
    channels, rank_ref, x_ref, gain_ref, w_ref, col_ref, normed_ref, gate_ref, proj_ref, logit_ref, all_ref, rows_ref
):
    step = pl.program_id(0)
    count = x_ref.shape[0]
    chunks = rows_ref.shape[0] // count

    @pl.when(step == 0)
    def _():
        width = w_ref.shape[0] * w_ref.shape[2]
        for k in range(w_ref.shape[1]):
            place = pl.ds(pl.multiple_of((rank_ref[0] ^ k) * width, width), width)
            all_ref[place, :] = w_ref[:, k].reshape(width, w_ref.shape[3])

    @pl.when(step < chunks)
    def _():
        x = x_ref[...].astype(F32)
        scale = lax.rsqrt(jnp.mean(x * x, axis=1, keepdims=True) + 1e-05)
        normed = (x * scale * gain_ref[...]).astype(BF16)
        normed_ref[...] = normed
        total = mm(normed, all_ref[...])
        gate_ref[...] = total[:, channels + 128 :]
        logit = total[:, channels : channels + 128]
        high = logit.astype(BF16)
        place = pl.ds(pl.multiple_of(step * count, count), count)
        rows_ref[place, : channels + 128] = total[:, : channels + 128].astype(BF16)
        rows_ref[place, channels + 128 :] = (logit - high.astype(F32)).astype(BF16)

    @pl.when(step >= chunks)
    def _():
        order = lax.broadcasted_iota(jnp.int32, (proj_ref.shape[0], rows_ref.shape[0]), 1)
        picked = (col_ref[:, 4:5].astype(jnp.int32) == order).astype(F32)
        packed = mm(picked, rows_ref[...])
        proj_ref[...] = packed[:, :channels].astype(BF16)
        logit_ref[...] = packed[:, channels : channels + 128] + packed[:, channels + 128 :]


def project(rank, x_all, gain, weights, cols, count, channels):
    total, width = x_all.shape
    gates = weights.shape[3] - channels - 128
    chunks = total // count
    block = 256
    first = lambda i: jnp.minimum(i, chunks - 1)
    later = lambda i: jnp.maximum(i - chunks, 0)
    return pl.pallas_call(
        functools.partial(project_kernel, channels),
        grid=(chunks + total // block,),
        in_specs=[
            SCALAR,
            pl.BlockSpec((count, width), lambda i: (first(i), 0)),
            pl.BlockSpec((1, width), lambda i: (0, 0)),
            pl.BlockSpec(weights.shape, lambda i: (0, 0, 0, 0)),
            pl.BlockSpec((block, 128), lambda i: (later(i), 0)),
        ],
        out_specs=[
            pl.BlockSpec((count, width), lambda i: (first(i), 0)),
            pl.BlockSpec((count, gates), lambda i: (first(i), 0)),
            pl.BlockSpec((block, channels), lambda i: (later(i), 0)),
            pl.BlockSpec((block, 128), lambda i: (later(i), 0)),
            pl.BlockSpec((width, weights.shape[3]), lambda i: (0, 0)),
        ],
        out_shape=(
            jax.ShapeDtypeStruct((total, width), BF16),
            jax.ShapeDtypeStruct((total, gates), F32),
            jax.ShapeDtypeStruct((total, channels), BF16),
            jax.ShapeDtypeStruct((total, 128), F32),
            jax.ShapeDtypeStruct((width, weights.shape[3]), BF16),
        ),
        scratch_shapes=[pltpu.VMEM((total, channels + 256), BF16)],
        compiler_params=params(),
        cost_estimate=SMALL_COST,
        name="project",
    )(rank, x_all, gain, weights, cols)


def gate_kernel(heads, count, o_ref, place_ref, gate_ref, gain_ref, *refs):
    dealt_ref, chunk_refs = refs[-1 - place_ref.shape[1] // count], refs[-(place_ref.shape[1] // count) :]
    for k, chunk_ref in enumerate(chunk_refs):
        order = lax.broadcasted_iota(jnp.int32, (count, o_ref.shape[0]), 0) + k * count
        picked = (place_ref[...].astype(jnp.int32) == order).astype(F32)
        rows = mm(picked, o_ref[...])
        place = pl.ds(k * count, count)
        dealt_ref[place, :] = rows.astype(BF16)
        for h in range(heads):
            lanes = slice(h * DV, (h + 1) * DV)
            value = rows[:, lanes]
            scale = lax.rsqrt(jnp.mean(value * value, axis=1, keepdims=True) + 1e-05)
            gated = value * scale * gain_ref[...] * silu(gate_ref[place, lanes])
            chunk_ref[:, lanes] = gated.astype(BF16)


def gate_rows(output, place, gate_logit, gain, count, heads, tokens):
    total, cols = output.shape
    chunks = total // count
    whole = pl.BlockSpec(memory_space=pltpu.VMEM)
    outs = pl.pallas_call(
        functools.partial(gate_kernel, heads, count),
        in_specs=[whole] * 4 + [ANYWHERE] * len(tokens),
        out_specs=[whole] * (chunks + 1),
        out_shape=[jax.ShapeDtypeStruct((total, cols), BF16)]
        + [jax.ShapeDtypeStruct((count, cols), BF16)] * chunks,
        compiler_params=pltpu.CompilerParams(vmem_limit_bytes=VMEM_BYTES),
        cost_estimate=SMALL_COST,
        name="gate_rows",
    )(output, place, gate_logit, gain, *tokens)
    return outs[0], outs[1:]


def ungate_kernel(heads, chunks, dealt_ref, col_ref, gate_ref, gain_ref, *refs):
    grad_refs = refs[:chunks]
    gate_grad_ref, o_grad_ref, gain_grad_ref, rows_ref = refs[-4:]
    count = grad_refs[0].shape[0]
    total = dealt_ref.shape[0]
    sums = jnp.zeros((1, DV), F32)
    for k in range(chunks):
        place = pl.ds(k * count, count)
        for h in range(heads):
            lanes = slice(h * DV, (h + 1) * DV)
            value = dealt_ref[place, lanes].astype(F32)
            grad = grad_refs[k][:, lanes].astype(F32)
            logit = gate_ref[place, lanes]
            scale = lax.rsqrt(jnp.mean(value * value, axis=1, keepdims=True) + 1e-05)
            unit = value * scale
            gate = jax.nn.sigmoid(logit)
            slid = logit * gate
            sums += jnp.sum(grad * unit * slid, axis=0, keepdims=True)
            grad = grad * gain_ref[...]
            slope = gate * (1.0 + logit * (1.0 - gate))
            gate_grad_ref[place, lanes] = (grad * unit * slope).astype(BF16)
            grad = grad * slid
            inner = jnp.mean(grad * unit, axis=1, keepdims=True)
            rows_ref[place, lanes] = (scale * (grad - unit * inner)).astype(BF16)
    gain_grad_ref[...] = sums
    for k in range(chunks):
        place = pl.ds(k * count, count)
        order = lax.broadcasted_iota(jnp.int32, (count, total), 1)
        picked = (col_ref[place, 4:5].astype(jnp.int32) == order).astype(F32)
        o_grad_ref[place, :] = mm(picked, rows_ref[...]).astype(BF16)


def ungate_rows(dealt_rows, cols, gate_logit, gain, grads, heads, tokens):
    total, width = dealt_rows.shape
    whole = pl.BlockSpec(memory_space=pltpu.VMEM)
    return pl.pallas_call(
        functools.partial(ungate_kernel, heads, len(grads)),
        in_specs=[whole] * (4 + len(grads)) + [ANYWHERE] * len(tokens),
        out_specs=[whole] * 3,
        out_shape=(
            jax.ShapeDtypeStruct((total, width), BF16),
            jax.ShapeDtypeStruct((total, width), BF16),
            jax.ShapeDtypeStruct((1, DV), F32),
        ),
        scratch_shapes=[pltpu.VMEM((total, width), BF16)],
        compiler_params=pltpu.CompilerParams(vmem_limit_bytes=VMEM_BYTES),
        cost_estimate=SMALL_COST,
        name="ungate_rows",
    )(dealt_rows, cols, gate_logit, gain, *grads, *tokens)


def unpack_kernel(grad_ref, place_ref, normed_ref, w_ref, *refs):
    dealt_ref, g_ref, sums_ref, picked_ref = refs[-4:]
    step = pl.program_id(0)
    total = grad_ref.shape[0]

    @pl.when(step == 0)
    def _():
        part = 256
        for k in range(total // part):
            order = lax.broadcasted_iota(jnp.int32, (part, total), 0) + k * part
            picked = (place_ref[...].astype(jnp.int32) == order).astype(F32)
            picked_ref[k * part : (k + 1) * part, :] = picked.astype(BF16)
        sums_ref[...] = jnp.zeros_like(sums_ref)

    grad = mm(picked_ref[...], grad_ref[...]).astype(BF16)
    dealt_ref[...] = grad
    share = mm_tn(normed_ref[...], grad)
    g_ref[...] = share.astype(BF16)
    sums_ref[...] += jnp.sum(share * w_ref[...].astype(F32), axis=1, keepdims=True)


def unpack(grad, place, normed, weights, tokens):
    total, cols = grad.shape
    width = normed.shape[1]
    tile = 384
    return pl.pallas_call(
        unpack_kernel,
        grid=(cols // tile,),
        in_specs=[
            pl.BlockSpec((total, tile), lambda i: (0, i)),
            pl.BlockSpec(place.shape, lambda i: (0, 0)),
            pl.BlockSpec(normed.shape, lambda i: (0, 0)),
            pl.BlockSpec((width, tile), lambda i: (0, i)),
        ]
        + [ANYWHERE] * len(tokens),
        out_specs=[
            pl.BlockSpec((total, tile), lambda i: (0, i)),
            pl.BlockSpec((width, tile), lambda i: (0, i)),
            pl.BlockSpec((width, 1), lambda i: (0, 0)),
        ],
        out_shape=(
            jax.ShapeDtypeStruct((total, cols), BF16),
            jax.ShapeDtypeStruct((width, cols), BF16),
            jax.ShapeDtypeStruct((width, 1), F32),
        ),
        scratch_shapes=[pltpu.VMEM((total, total), BF16)],
        compiler_params=params(),
        cost_estimate=SMALL_COST,
        name="unpack",
    )(grad, place, normed, weights, *tokens)


def unproject_kernel(wide, grad_ref, gate_ref, w_ref, *refs):
    part_ref, turned_ref = refs[-2:]

    @pl.when(pl.program_id(0) == 0)
    def _():
        turned_ref[...] = w_ref[...].T

    part = mm(grad_ref[...], turned_ref[:wide, :]) + mm(gate_ref[...], turned_ref[wide:, :])
    part_ref[...] = part.astype(BF16)


def unproject(grad, gate_grad, weights, count, tokens):
    total, cols = grad.shape
    width = weights.shape[0]
    return pl.pallas_call(
        functools.partial(unproject_kernel, cols),
        grid=(total // count,),
        in_specs=[
            pl.BlockSpec((count, cols), lambda i: (i, 0)),
            pl.BlockSpec((count, gate_grad.shape[1]), lambda i: (i, 0)),
            pl.BlockSpec(weights.shape, lambda i: (0, 0)),
        ]
        + [ANYWHERE] * len(tokens),
        out_specs=pl.BlockSpec((count, width), lambda i: (i, 0)),
        out_shape=jax.ShapeDtypeStruct((total, width), BF16),
        scratch_shapes=[pltpu.VMEM(weights.shape[::-1], BF16)],
        compiler_params=params(),
        cost_estimate=SMALL_COST,
        name="unproject",
    )(grad, gate_grad, weights, *tokens)


def copy_kernel(value_ref, *refs):
    refs[-1][...] = value_ref[...]


def copied(value, *tokens):
    whole = pl.BlockSpec(memory_space=pltpu.VMEM)
    return pl.pallas_call(
        copy_kernel,
        in_specs=[whole] + [ANYWHERE] * len(tokens),
        out_specs=whole,
        out_shape=jax.ShapeDtypeStruct(value.shape, value.dtype),
        cost_estimate=SMALL_COST,
        name="copied",
    )(value, *tokens)


def weight_grad_kernel(parts, sums, *refs):
    total = mm_tn(refs[0][...], refs[parts][...])
    for k in range(1, parts):
        total += mm_tn(refs[k][...], refs[parts + k][...])
    if sums:
        refs[-2][...] = total.astype(BF16)
        refs[-1][...] = jnp.sum(total * refs[2 * parts][...].astype(F32), axis=1, keepdims=True)
    else:
        refs[-1][...] = total.astype(BF16)


def weight_grad(lefts, rights, tile, *tokens, weights=None):
    parts = len(lefts)
    count, width = lefts[0].shape
    cols = rights[0].shape[1]
    sums = weights is not None
    outs = pl.pallas_call(
        functools.partial(weight_grad_kernel, parts, sums),
        grid=(cols // tile,),
        in_specs=[pl.BlockSpec((count, width), lambda i: (0, 0))] * parts
        + [pl.BlockSpec((count, tile), lambda i: (0, i))] * parts
        + [pl.BlockSpec((width, tile), lambda i: (0, i))] * sums
        + [ANYWHERE] * len(tokens),
        out_specs=[pl.BlockSpec((width, tile), lambda i: (0, i))]
        + [pl.BlockSpec((width, 1), lambda i: (0, 0))] * sums,
        out_shape=[jax.ShapeDtypeStruct((width, cols), BF16)]
        + [jax.ShapeDtypeStruct((width, 1), F32)] * sums,
        compiler_params=params(),
        cost_estimate=pl.CostEstimate(
            flops=4 * parts * count * width * cols, bytes_accessed=10**7, transcendentals=0
        ),
        name="weight_grad",
    )(*lefts, *rights, *([weights] if sums else []), *tokens)
    return outs if sums else outs[0]


def out_project_kernel(rank_ref, x_ref, gain_ref, *refs):
    residual_ref, mid_ref, all_ref = refs[-3:]
    chunks = (len(refs) - 3) // 2
    rank = rank_ref[0]
    for k in range(chunks):
        width = refs[k].shape[1]
        all_ref[:, pl.ds(pl.multiple_of((rank ^ k) * width, width), width)] = refs[k][...]
    for k in range(chunks):
        width = refs[chunks + k].shape[0]
        cols = pl.ds(pl.multiple_of((rank ^ k) * width, width), width)
        residual_ref[:, cols] = x_ref[:, cols].astype(F32) + mm_nt(all_ref[...], refs[chunks + k][...])
    residual = residual_ref[...]
    scale = lax.rsqrt(jnp.mean(residual * residual, axis=1, keepdims=True) + 1e-05)
    mid_ref[...] = (residual * scale * gain_ref[...]).astype(BF16)


def out_project(rank, x, gain, attn, blocks):
    count, width = x.shape
    return pl.pallas_call(
        out_project_kernel,
        in_specs=[SCALAR] + [WHOLE] * (2 + len(attn) + len(blocks)),
        out_specs=[WHOLE] * 2,
        out_shape=(
            jax.ShapeDtypeStruct((count, width), F32),
            jax.ShapeDtypeStruct((count, width), BF16),
        ),
        scratch_shapes=[pltpu.VMEM((count, blocks[0].shape[1]), BF16)],
        compiler_params=pltpu.CompilerParams(vmem_limit_bytes=VMEM_BYTES),
        cost_estimate=SMALL_COST,
        name="out_project",
    )(rank, x, gain, *attn, *blocks)


def mid_back_kernel(chunks, rank_ref, grad_ref, residual_ref, gain_ref, *refs):
    parts, blocks, outs = refs[:chunks], refs[chunks : 2 * chunks], refs[-chunks - 4 :]
    res_grad_ref, low_ref, gain_grad_ref, chunk_refs, all_ref = outs[0], outs[1], outs[2], outs[3:-1], outs[-1]
    rank = rank_ref[0]
    mid_grad = parts[0][...].astype(F32)
    for k in range(1, chunks):
        mid_grad += parts[k][...].astype(F32)
    residual = residual_ref[...]
    scale = lax.rsqrt(jnp.mean(residual * residual, axis=1, keepdims=True) + 1e-05)
    unit = residual * scale
    gain_grad_ref[...] = jnp.sum(mid_grad * unit, axis=0, keepdims=True)
    scaled = mid_grad * gain_ref[...]
    inner = jnp.mean(scaled * unit, axis=1, keepdims=True)
    res_grad = grad_ref[...].astype(F32) + scale * (scaled - unit * inner)
    res_grad_ref[...] = res_grad
    low_ref[...] = res_grad.astype(BF16)
    for k in range(chunks):
        width = blocks[k].shape[0]
        cols = pl.ds(pl.multiple_of((rank ^ k) * width, width), width)
        share = mm(low_ref[:, cols], blocks[k][...])
        if k == 0:
            all_ref[...] = share
        else:
            all_ref[...] += share
    for k in range(chunks):
        width = chunk_refs[k].shape[1]
        cols = pl.ds(pl.multiple_of((rank ^ k) * width, width), width)
        chunk_refs[k][...] = all_ref[:, cols].astype(BF16)


def mid_back(rank, grad, residual, gain, parts, blocks, tokens):
    count, width = residual.shape
    chunks = len(parts)
    wide = blocks[0].shape[1]
    outs = pl.pallas_call(
        functools.partial(mid_back_kernel, chunks),
        in_specs=[SCALAR] + [WHOLE] * (3 + 2 * chunks) + [ANYWHERE] * len(tokens),
        out_specs=[WHOLE] * (3 + chunks),
        out_shape=[
            jax.ShapeDtypeStruct((count, width), F32),
            jax.ShapeDtypeStruct((count, width), BF16),
            jax.ShapeDtypeStruct((1, width), F32),
        ]
        + [jax.ShapeDtypeStruct((count, wide // chunks), BF16)] * chunks,
        scratch_shapes=[pltpu.VMEM((count, wide), F32)],
        compiler_params=pltpu.CompilerParams(vmem_limit_bytes=VMEM_BYTES),
        cost_estimate=SMALL_COST,
        name="mid_back",
    )(rank, grad, residual, gain, *parts, *blocks, *tokens)
    return outs[0], outs[1], outs[2], outs[3:]


def in_back_kernel(chunks, x_ref, res_grad_ref, gain_ref, *refs):
    x = x_ref[...].astype(F32)
    grad = refs[0][...].astype(F32)
    for k in range(1, chunks):
        grad += refs[k][...].astype(F32)
    scale = lax.rsqrt(jnp.mean(x * x, axis=1, keepdims=True) + 1e-05)
    unit = x * scale
    scaled = grad * gain_ref[...]
    inner = jnp.mean(scaled * unit, axis=1, keepdims=True)
    refs[-1][...] = (res_grad_ref[...] + scale * (scaled - unit * inner)).astype(BF16)


def in_back(x, res_grad, gain, parts, tokens):
    return pl.pallas_call(
        functools.partial(in_back_kernel, len(parts)),
        in_specs=[WHOLE] * (3 + len(parts)) + [ANYWHERE] * len(tokens),
        out_specs=WHOLE,
        out_shape=jax.ShapeDtypeStruct(x.shape, BF16),
        compiler_params=pltpu.CompilerParams(vmem_limit_bytes=VMEM_BYTES),
        cost_estimate=SMALL_COST,
        name="in_back",
    )(x, res_grad, gain, *parts, *tokens)


def swapped(value, axis, mask):
    devices = lax.axis_size(axis)
    return lax.ppermute(value, axis, [(i, i ^ mask) for i in range(devices)])


def spread(value):
    return [value] + [swapped(value, "seq", k) for k in range(1, lax.axis_size("seq"))]


def returned(chunks):
    return [chunks[0]] + [swapped(chunks[k], "seq", k) for k in range(1, len(chunks))]


def gathered_rows(pieces):
    own = lax.all_to_all(pieces, "seq", 0, 0, tiled=True)
    return lax.all_gather(own, "mp", axis=0, tiled=False)


def gathered_near(pieces):
    rank = lax.axis_index("seq")
    chunks = [lax.dynamic_index_in_dim(pieces, rank ^ k, 0, keepdims=False) for k in range(pieces.shape[0])]
    return lax.all_gather(jnp.stack(returned(chunks)), "mp", axis=0, tiled=False)


class RowSum:
    def __init__(self, grad):
        self.seq_count, self.mp_count = lax.axis_size("seq"), lax.axis_size("mp")
        self.rank = lax.axis_index("mp")
        self.cols = grad.shape[1]
        self.short = self.mp_count <= 8
        if not self.short:
            parts = grad.astype(F32).reshape(self.seq_count, self.mp_count, -1, self.cols)
            self.grad = parts.transpose(1, 0, 2, 3).reshape(-1, self.cols)
            return
        self.grad = grad.reshape(self.seq_count, self.mp_count // 2, 2, -1, self.cols)
        self.core = self.rank % 2
        sent = lax.dynamic_index_in_dim(self.grad, 1 - self.core, 2, keepdims=False)
        self.got = swapped(sent, "mp", 1)

    def join(self):
        if self.short:
            kept = lax.dynamic_index_in_dim(self.grad, self.core, 2, keepdims=False)
            self.half = (kept.astype(F32) + self.got.astype(F32)).astype(BF16)
            return self.half
        return self.grad

    def send(self, half):
        if not self.short:
            own = lax.psum_scatter(half, "mp", scatter_dimension=0, tiled=True)
            self.own = own.reshape(self.seq_count, -1, self.cols)
            self.parts = [self.own]
            return
        chip = self.rank // 2
        self.parts = [lax.dynamic_index_in_dim(half, chip, 1, keepdims=False)]
        for j in range(1, self.mp_count // 2):
            piece = lax.dynamic_index_in_dim(half, chip ^ j, 1, keepdims=False)
            self.parts.append(swapped(piece, "mp", 2 * j))

    def total(self):
        if self.short:
            self.own = sum(p.astype(F32) for p in self.parts)
        return self.own.astype(BF16)


def dealt(own):
    return lax.all_to_all(own, "seq", 0, 0, tiled=True).astype(F32)


def left_product(left, right):
    return lax.dot_general(
        left, right, (((0,), (0,)), ((), ())), preferred_element_type=jnp.float32
    )


def right_product(left, right):
    return lax.dot_general(
        left, right, (((1,), (1,)), ((), ())), preferred_element_type=jnp.float32
    )


def dot(left, right):
    return jnp.dot(left, right, preferred_element_type=jnp.float32)


def silu_slope(values):
    gate = jax.nn.sigmoid(values)
    return gate * (1.0 + values * (1.0 - gate))


def body(
    layer_in,
    out_grad,
    seq_lengths,
    dealing,
    log_decay,
    w_qkv,
    w_out_gate,
    w_beta,
    conv_w,
    gain_in,
    gain_o,
    w_out,
    gain_mid,
    w_gate_up,
    w_down,
):
    seq_count, mp_count = lax.axis_size("seq"), lax.axis_size("mp")
    rank = lax.axis_index("seq")
    count = layer_in.shape[1]
    rows = w_qkv.shape[0]
    heads = HEAD_COUNT // seq_count
    key_cols, val_cols = heads * DK, heads * DV
    half = w_down.shape[0] // seq_count
    wide = -(-half // 128) * 128
    taps = conv_w.shape[1]
    total = dealing.shape[1]
    devices = seq_count * mp_count

    mix_pieces, ffn_pieces = [], []
    turned_down = w_down.T
    small = jnp.concatenate([conv_w.T.reshape(-1), gain_in, gain_mid, gain_o])
    small_count = small.shape[0]
    spare = 128 - heads
    filler = jnp.concatenate([small, jnp.zeros((rows * spare - small_count,), BF16)])
    filler = filler.reshape(rows, spare)
    wide_filler = jnp.zeros((rows, wide - half), BF16)
    all_keys, ffn = HEAD_COUNT * DK, w_down.shape[0]
    for j in range(seq_count):
        mix_pieces.append(
            jnp.concatenate(
                [
                    w_qkv[:, j * key_cols : (j + 1) * key_cols],
                    w_qkv[:, all_keys + j * key_cols : all_keys + (j + 1) * key_cols],
                    w_qkv[:, 2 * all_keys + j * val_cols : 2 * all_keys + (j + 1) * val_cols],
                    w_beta[:, j * heads : (j + 1) * heads],
                    filler,
                    w_out_gate[:, j * val_cols : (j + 1) * val_cols],
                ],
                1,
            )
        )
        ffn_pieces.append(
            jnp.concatenate(
                [
                    w_gate_up[:, j * half : (j + 1) * half],
                    wide_filler,
                    w_gate_up[:, ffn + j * half : ffn + (j + 1) * half],
                    wide_filler,
                    turned_down[:, j * half : (j + 1) * half],
                    wide_filler,
                ],
                1,
            )
        )
    channels = 2 * key_cols + val_cols
    gathered = gathered_near(jnp.stack(mix_pieces))
    smalls = gathered[:, :, :, channels + heads : channels + 128].transpose(1, 0, 2, 3)
    smalls = jnp.take(smalls, rank ^ jnp.arange(seq_count), axis=0)
    smalls = smalls.reshape(devices, -1)[:, :small_count]
    out_block = lax.all_gather(w_out.T, "mp", axis=0, tiled=True)
    ffn_w = gathered_rows(jnp.stack(ffn_pieces)).transpose(1, 0, 2, 3).reshape(devices * rows, -1)
    w_gu, down_turned = ffn_w[:, : 2 * wide], ffn_w[:, 2 * wide :]

    own_taps = conv_w.shape[0] * taps
    full_conv = smalls[:, :own_taps].reshape(-1, taps, conv_w.shape[0]).transpose(1, 0, 2)
    full_conv = full_conv.reshape(taps, -1).astype(F32)
    conv = jnp.concatenate(
        [
            lax.dynamic_slice_in_dim(full_conv, rank * key_cols, key_cols, 1),
            lax.dynamic_slice_in_dim(full_conv, all_keys + rank * key_cols, key_cols, 1),
            lax.dynamic_slice_in_dim(full_conv, 2 * all_keys + rank * val_cols, val_cols, 1),
        ],
        1,
    )
    conv = jnp.concatenate([conv, jnp.zeros((8 - taps, channels), F32)], 0)
    gains = smalls[:, own_taps:].astype(F32)
    full_gin = gains[:, :rows].reshape(-1)
    full_gmid = gains[:, rows : 2 * rows].reshape(-1)
    full_go = gains[:, 2 * rows :].reshape(-1)

    chunks_in = spread(layer_in[0])
    decay_chunks = spread(log_decay[0].T)
    out_blocks = spread(copied(out_block, chunks_in[1], chunks_in[2]))
    order = dealing[0]
    place = ((order // count) ^ rank) * count + order % count
    index = jnp.arange(total, dtype=jnp.int32)

    decay = jnp.zeros((heads, total), F32)
    for k in range(seq_count):
        own = lax.dynamic_slice_in_dim(decay_chunks[k], rank * heads, heads, 0)
        decay = lax.dynamic_update_slice_in_dim(decay, own, (rank ^ k) * count, 1)
    decay = decay.reshape(heads, -1, BLOCK)
    cum = jnp.cumsum(decay, axis=2)
    ends = jnp.cumsum(seq_lengths[0])
    seg = jnp.sum((index[None, :] >= ends[:, None]).astype(jnp.int32), axis=0)
    seg_blocks = seg.reshape(-1, BLOCK)
    seg_before = jnp.concatenate([jnp.full((1,), -1, jnp.int32), seg_blocks[:-1, -1]])
    keep_in = (seg_blocks == seg_before[:, None]).astype(F32)
    keep_out = (seg_blocks == seg_blocks[:, -1:]).astype(F32)
    elog = (jnp.exp(cum) * keep_in[None]).reshape(heads, total)
    flog = (jnp.exp(cum[:, :, -1:] - cum) * keep_out[None]).reshape(heads, total)
    cum = cum.reshape(heads, total)
    keeps = []
    for tap in range(taps - 1):
        by = taps - 1 - tap
        before = jnp.concatenate([jnp.full((by,), -1, jnp.int32), seg[:-by]])
        keeps.append((before == seg).astype(F32)[None])
    seg_row = seg.astype(F32)[None]
    place_row = place.astype(F32)[None]
    row_info = jnp.concatenate([cum, seg_row, jnp.zeros((8 - heads - 1, total), F32)], 0)
    col_info = jnp.concatenate(
        keeps
        + [seg_row, place_row, cum, elog, flog, jnp.zeros((128 - 5 - 3 * heads, total), F32)],
        0,
    ).T

    rank_word = rank.astype(jnp.int32).reshape(1)
    normed, gate_logit, proj, logit_parts, mix = project(
        rank_word, jnp.concatenate(chunks_in, 0), full_gin[None], gathered, col_info, count, channels
    )
    chunks_grad = spread(copied(out_grad[0], proj))
    outs = forward_recurrence(proj, conv, col_info, row_info, logit_parts, heads)
    dealt_rows, attn = gate_rows(
        outs[0], place_row, gate_logit, full_go[None], count, heads, chunks_grad[1:] + out_blocks[1:]
    )
    attn_parts = returned(attn)
    residual, mid_own = out_project(rank_word, layer_in[0], full_gmid[None], attn_parts, out_blocks)

    mids = [mid_own, swapped(mid_own, "seq", 1), swapped(mid_own, "seq", 2)]
    hiddens, gu_grads, layer_parts, mid_parts = [], [], [], []
    for k in range(seq_count):
        if k == 1:
            mids.append(swapped(copied(mid_own, mids[1], mid_parts[0]), "seq", 3))
        gate_up = dot(mids[k], w_gu)
        gate, up = gate_up[:, :wide], gate_up[:, wide:]
        hiddens.append((silu(gate) * up).astype(BF16))
        hidden_grad = dot(chunks_grad[k], down_turned)
        gu_grads.append(
            jnp.concatenate(
                [hidden_grad * up * silu_slope(gate), hidden_grad * silu(gate)], 1
            ).astype(BF16)
        )
        mid_parts.append(right_product(gu_grads[k], w_gu).astype(BF16))
    for k in range(seq_count):
        layer_parts.append(
            right_product(hiddens[k], down_turned).astype(BF16)
        )
    mid_parts = returned(mid_parts)
    g_down = weight_grad(chunks_grad, hiddens, wide, mid_parts[1])
    down_sum = RowSum(g_down)
    res_grad, out_proj_grad, g_mid, attn_grads = mid_back(
        rank_word, out_grad[0], residual, full_gmid[None], mid_parts, out_blocks, [g_down]
    )
    g_gu = weight_grad(mids, gu_grads, wide, attn_grads[0])
    attn_grads = returned(attn_grads)
    down_half = down_sum.join()
    down_sum.send(down_half)
    ffn_sum = RowSum(g_gu)
    opg_chunks = spread(copied(out_proj_grad, *attn_grads[1:]))
    layer_parts = returned(layer_parts)

    gate_grad, o_grad, g_go = ungate_rows(
        dealt_rows, col_info, gate_logit, full_go[None], attn_grads, heads, [g_gu]
    )
    ffn_half = ffn_sum.join()
    ffn_sum.send(ffn_half)
    proj_grad, g_conv = backward_recurrence(
        proj, conv, col_info, row_info, logit_parts, outs[1:], o_grad, heads,
        down_sum.parts[1:] + [ffn_half],
    )
    g_gate, gate_sums = weight_grad(
        [normed], [gate_grad], val_cols, proj_grad, weights=mix[:, channels + 128 :]
    )
    g_out = weight_grad(opg_chunks, attn, val_cols, proj_grad, *ffn_sum.parts[1:])
    out_sum = RowSum(jnp.concatenate([g_gate, g_out], 1))
    out_half = out_sum.join()
    out_sum.send(out_half)
    proj_grad, g_proj, proj_sums = unpack(proj_grad, place_row, normed, mix, [out_half] + layer_parts[1:])
    normed_low = unproject(proj_grad, gate_grad, mix, count, [])
    g_gin = (proj_sums + gate_sums)[:, 0] / full_gin
    conv_full = jnp.zeros((taps, conv_w.shape[0] * devices), F32)
    conv_full = lax.dynamic_update_slice_in_dim(
        conv_full, g_conv[:taps, :key_cols], rank * key_cols, 1
    )
    conv_full = lax.dynamic_update_slice_in_dim(
        conv_full, g_conv[:taps, key_cols : 2 * key_cols], all_keys + rank * key_cols, 1
    )
    conv_full = lax.dynamic_update_slice_in_dim(
        conv_full, g_conv[:taps, 2 * key_cols :], 2 * all_keys + rank * val_cols, 1
    )
    conv_full = conv_full.reshape(taps, devices, -1).transpose(1, 0, 2).reshape(devices, -1)
    small_cols = -(-small_count // rows)
    small_grad = jnp.concatenate(
        [
            conv_full,
            g_gin.reshape(devices, -1),
            g_mid.reshape(devices, -1),
            g_go.reshape(devices, -1),
            jnp.zeros((devices, small_cols * rows - small_count), F32),
        ],
        1,
    )
    small_grad = small_grad.reshape(devices * rows, small_cols).astype(BF16)
    mix_sum = RowSum(
        jnp.concatenate([g_proj[:, : channels + heads], small_grad], 1)
    )
    mix_half = mix_sum.join()
    mix_sum.send(mix_half)
    normed_chunks = returned(
        [normed_low[k * count : (k + 1) * count] for k in range(seq_count)]
    )
    ffn_pieces = dealt(jnp.concatenate([down_sum.total(), ffn_sum.total(), out_sum.total()], 2))
    layer_out = residual + sum(c.astype(F32) for c in layer_parts)
    mix_pieces = dealt(mix_sum.total())
    in_grad = in_back(layer_in[0], res_grad, full_gin[None], normed_chunks, [mix_half])

    small_sum = jnp.sum(mix_pieces[:, :, channels + heads :], axis=0).reshape(-1)[:small_count]
    grad_conv = small_sum[:own_taps].reshape(taps, -1).T
    small_sum = small_sum[own_taps:]

    def columns(pieces, first, width):
        return jnp.concatenate([pieces[j, :, first : first + width] for j in range(seq_count)], 1)

    grad_qkv = jnp.concatenate(
        [
            columns(mix_pieces, 0, key_cols),
            columns(mix_pieces, key_cols, key_cols),
            columns(mix_pieces, 2 * key_cols, val_cols),
        ],
        1,
    )
    return (
        layer_out.astype(BF16)[None],
        in_grad.astype(BF16)[None],
        grad_qkv,
        columns(ffn_pieces, 3 * wide, val_cols),
        columns(mix_pieces, channels, heads),
        grad_conv,
        small_sum[:rows],
        small_sum[2 * rows :],
        columns(ffn_pieces, 3 * wide + val_cols, val_cols).T,
        small_sum[rows : 2 * rows],
        jnp.concatenate([columns(ffn_pieces, wide, half), columns(ffn_pieces, 2 * wide, half)], 1),
        columns(ffn_pieces, 0, half).T,
    )


def solution(mesh):
    in_specs = (
        P("mp", "seq", None),
        P("mp", "seq", None),
        P("mp", None),
        P("mp", None),
        P("mp", "seq", None),
        P(("seq", "mp"), None),
        P(("seq", "mp"), None),
        P(("seq", "mp"), None),
        P(("seq", "mp"), None),
        P(("seq", "mp")),
        P(("seq", "mp")),
        P(None, ("seq", "mp")),
        P(("seq", "mp")),
        P(("seq", "mp"), None),
        P(None, ("seq", "mp")),
    )
    out_specs = (
        P("mp", "seq", None),
        P("mp", "seq", None),
        P(("seq", "mp"), None),
        P(("seq", "mp"), None),
        P(("seq", "mp"), None),
        P(("seq", "mp"), None),
        P(("seq", "mp")),
        P(("seq", "mp")),
        P(None, ("seq", "mp")),
        P(("seq", "mp")),
        P(("seq", "mp"), None),
        P(None, ("seq", "mp")),
    )
    return jax.shard_map(body, mesh=mesh, in_specs=in_specs, out_specs=out_specs, check_vma=False)
```

time: 2430 us -> 568 us (0.23)
  waiting for transfers between devices: 1190 us -> 131 us
  matrix products: 770 us -> 38.2 us
  Pallas kernels: 0 us -> 187 us
  blocking collectives: 164 us -> 12.3 us
  other arithmetic: 101 us -> 32.9 us
  local copies, waits for them, and re-layouts: 136 us -> 72.2 us
  starting transfers between devices: 22.8 us -> 69.1 us
    reduce_scatter x5 -> x0, waiting for transfers between devices: 902 us -> none  [the longest x1 253 us: body(): lax.psum_scatter(g_gu, ('seq', 'mp'), scatter_dimension=0, tiled=True)]
    dot_general x417 -> x8, matrix products: 726 us -> 19.2 us  [dot(): return jnp.dot(left, right, preferred_element_type=jnp.float32)]
    pallas_call x0 -> x18, Pallas kernels: none -> 187 us  [the longest x1 42.1 us: backward_recurrence(): pl.pallas_call(functools.partial(backward_kernel, heads), grid=(count //...]
    unnamed x18 -> x3, waiting for transfers between devices: 111 us -> 0.71 us
    all_gather x2 -> x0, blocking collectives: 84.5 us -> none  [the longest x1 43.3 us: body(): lax.all_gather(conv_w, ('seq', 'mp'), axis=0, tiled=True)]
    all_gather x9 -> x3, waiting for transfers between devices: 81.6 us -> 0.02 us  [the longest x1 0.01 us: body(): out_block = lax.all_gather(w_out.T, 'mp', axis=0, tiled=True)]
    unnamed x2 -> x0, blocking collectives: 79.1 us -> none
    ppermute x8 -> x52, starting transfers between devices: 21.6 us -> 62 us  [swapped(): return lax.ppermute(value, axis, [(i, i ^ mask) for i in range(devices)])]
  transfers between devices with their start and end apart: 24 -> 57, of which waited for: 15 -> 19; matrix products, arithmetic and copies ran while one was open for 20% -> 23% of each run, Pallas kernels for 0% -> 34%
where the time goes in v1:
time: 568 us; the launch traced here: 558 us
  Pallas kernels  187 us (33%)
  waiting for transfers between devices  131 us (23%)
  local copies, waits for them, and re-layouts  72.2 us (13%)
  starting transfers between devices  69.1 us (12%)
  matrix products  38.2 us (7%)
  other arithmetic  32.9 us (6%)
  between operations  15.3 us (3%)
  blocking collectives  12.3 us (2%)
    ppermute x52, waiting for transfers between devices, swapped(): return lax.ppermute(value, axis, [(i, i ^ mask) for i in range(devices)])  130 us
    ppermute x52, starting transfers between devices, swapped(): return lax.ppermute(value, axis, [(i, i ^ mask) for i in range(devices)])  62 us
    pallas_call x1, Pallas kernels, backward_recurrence(): pl.pallas_call(functools.partial(backward_kernel, heads), grid=(count //...  42.1 us
    pallas_call x4, Pallas kernels, weight_grad(): pl.pallas_call(functools.partial(weight_grad_kernel, parts, sums), grid=(...  29.5 us
    pallas_call x1, Pallas kernels, forward_recurrence(): pl.pallas_call(functools.partial(forward_kernel, heads), grid=(count // s...  23.5 us
    pallas_call x1, Pallas kernels, project(): pl.pallas_call(functools.partial(project_kernel, channels), grid=(chunks...  20.4 us
    dot_general x8, matrix products, dot(): return jnp.dot(left, right, preferred_element_type=jnp.float32)  19.2 us
    dot_general x8, matrix products, right_product(): lax.dot_general(left, right, (((1,), (1,)), ((), ())), preferred_element_...  19 us
  transfers between devices with their start and end apart: 57, of which 19 were waited for; matrix products, arithmetic and copies ran while one was open for 23% of the time, Pallas kernels for 34%

profile of v1, /device:TPU:0, one launch (start us, length us, event | category | flops | bytes accessed | tf_op | source)
XLA Modules:
  0.0 557.8 jit_solution(583773333929376001)
XLA Ops:
  8.0 2.8 concatenate.110
  14.4 3.0 collective-permute-start.1
  19.0 3.0 collective-permute-done.1
  25.6 12.3 %all_to_all.15 = bf16[4,32,2304]{2,1,0:T(8,128)(2,1)} all-to-all(bf16[4,32,2304]{2,1,0:T(8,128)(2,1)S(1)} %pad_maximum_fusion.8), channel_id=1, replica_groups=mesh['seq'=4,'mp'=8] {'seq'}, dimensions={0} | all-to-all | bytes 1179648 | tf_op jit(solution)/shard_map/all_to_all | solution.py:789
  57.0 5.3 concatenate.121
  62.2 13.1 %collective-permute-done.4.refs_1_ = bf16[384,1024]{1,0:T(8,128)(2,1)S(1)} collective-permute-done((bf16[384,1024]{1,0:T(8,128)(2,1)S(1)}, bf16[384,1024]{1,0:T(8,128)(2,1)S(1)}, u32[]{:S(2)}, u32[]{:S(2)}) %collective-permute-start.4) | collective-permute-done | bytes 786464 | tf_op jit(solution)/shard_map/ppermute | solution.py:777
  75.4 3.2 pad_maximum_fusion.x_ref
  91.2 20.4 %project.1 = (bf16[1536,1024]{1,0:T(8,128)(2,1)}, f32[1536,512]{1,0:T(8,128)}, bf16[1536,1024]{1,0:T(8,128)(2,1)}, f32[1536,128]{1,0:T(8,128)}, bf16[1024,1664]{1,0:T(8,128)(2,1)}) custom-call(s32[1]{0:T(128)} %bitcast.rank_ref, bf16[1536,1024]{1,0:T(8,128)(2,1)} %pad_maximum_fusion.x_ref, f32[1,1024]{1,0:T(1,128)} %broadcast_in_dim_reshape.13.gain_ref, ...), custom_call_target="tpu_custom_call" | custom-call | flops 1000000 | bytes 1000000 | tf_op jit(solution)/shard_map/project/pallas_call | solution.py:415
  120.6 23.5 %recurrence_forward.1 = (bf16[1536,512]{1,0:T(8,128)(2,1)}, bf16[12,2,128,256]{3,2,1,0:T(8,128)(2,1)}, bf16[12,2,128,256]{3,2,1,0:T(8,128)(2,1)}, bf16[12,2,128,...) custom-call(bf16[1536,1024]{1,0:T(8,128)(2,1)} %get-tuple-element.47.edge_ref.proj_ref.refs, ...), custom_call_target="tpu_custom_call" | custom-call | flops 1000000 | bytes 1000000 | tf_op jit(solution)/shard_map/recurrence_forward/pallas_call | solution.py:323
  144.2 14.0 %collective-permute-done.10.refs_1_.refs_2_ = bf16[384,1024]{1,0:T(8,128)(2,1)} collective-permute-done((bf16[384,1024]{1,0:T(8,128)(2,1)}, bf16[384,1024]{1,0:T(8,128)(2,1)}, u32[]{:S(2)}, u32[]{:S(2)}) %collective-permute-start.10) | collective-permute-done | bytes 786464 | tf_op jit(solution)/shard_map/ppermute | solution.py:777
  158.2 6.7 %gate_rows.1 = (bf16[1536,512]{1,0:T(8,128)(2,1)}, bf16[384,512]{1,0:T(8,128)(2,1)}, bf16[384,512]{1,0:T(8,128)(2,1)}, bf16[384,512]{1,0:T(8,128)(2,1)}, bf16[384,512]{1,0:T(8,128)(2,1)}) custom-call(bf16[1536,512]{1,0:T(8,128)(2,1)} %get-tuple-element.49.o_ref, f32[1,1536]{1,0:T(1,128)} %copy-done.49, f32[1536,512]{1,0:T(8,128)} %get-tuple-element.50.gate_ref, ...), custom_call_target="tpu_custom_call" | custom-call | flops 1000000 | bytes 1000000 | tf_op jit(solution)/shard_map/gate_rows/pallas_call | solution.py:466
  169.1 8.0 %collective-permute-done.15.refs_1_ = bf16[384,512]{1,0:T(8,128)(2,1)S(1)} collective-permute-done((bf16[384,512]{1,0:T(8,128)(2,1)}, bf16[384,512]{1,0:T(8,128)(2,1)S(1)}, u32[]{:S(2)}, u32[]{:S(2)}) %collective-permute-start.15) | collective-permute-done | bytes 393248 | tf_op jit(solution)/shard_map/ppermute | solution.py:777
  177.1 8.8 %collective-permute-done.16.refs_2_ = bf16[384,512]{1,0:T(8,128)(2,1)S(1)} collective-permute-done((bf16[384,512]{1,0:T(8,128)(2,1)}, bf16[384,512]{1,0:T(8,128)(2,1)S(1)}, u32[]{:S(2)}, u32[]{:S(2)}) %collective-permute-start.16) | collective-permute-done | bytes 393248 | tf_op jit(solution)/shard_map/ppermute | solution.py:777
  186.8 6.4 %out_project.1 = (f32[384,1024]{1,0:T(8,128)}, bf16[384,1024]{1,0:T(8,128)(2,1)}) custom-call(s32[1]{0:T(128)} %bitcast.rank_ref, bf16[384,1024]{1,0:T(8,128)(2,1)} %bitcast.302, f32[1,1024]{1,0:T(1,128)} %broadcast_in_dim_reshape.12.gain_ref, bf16[384,512]{1,0:T(8,128)(2,1)} %get-tuple-element.51.refs_0_.refs_4_, bf16[384,512]{1,0:T(8,128)(2,1)} %copy-done.36, ...), custom_call_target="tpu_custom_call" | custom-call | flops 1000000 | bytes 1000000 | tf_op jit(solution)/shard_map/out_project/pallas_call | solution.py:684
  197.5 2.7 copy.161
  201.6 10.1 %collective-permute-done.18.refs_0_.refs_1_ = bf16[384,1024]{1,0:T(8,128)(2,1)S(1)} collective-permute-done((bf16[384,1024]{1,0:T(8,128)(2,1)}, bf16[384,1024]{1,0:T(8,128)(2,1)S(1)}, u32[]{:S(2)}, u32[]{:S(2)}) %collective-permute-start.18) | collective-permute-done | bytes 786464 | tf_op jit(solution)/shard_map/ppermute | solution.py:777
  213.1 3.1 multiply_convert_fusion.5
  227.7 3.5 fusion.21
  231.2 3.5 multiply_convert_fusion.3
  242.7 10.0 %collective-permute-done.22.refs_3_ = bf16[384,1024]{1,0:T(8,128)(2,1)S(1)} collective-permute-done((bf16[384,1024]{1,0:T(8,128)(2,1)}, bf16[384,1024]{1,0:T(8,128)(2,1)S(1)}, u32[]{:S(2)}, u32[]{:S(2)}) %collective-permute-start.22) | collective-permute-done | bytes 786464 | tf_op jit(solution)/shard_map/ppermute | solution.py:777
  254.2 3.1 multiply_convert_fusion.1
  262.2 7.2 %weight_grad.4.refs_8_ = bf16[1024,768]{1,0:T(8,128)(2,1)} custom-call(bf16[384,1024]{1,0:T(8,128)(2,1)} %copied.4.refs_0_, bf16[384,1024]{1,0:T(8,128)(2,1)} %collective-permute-done.9.refs_0_.refs_1_, bf16[384,1024]{1,0:T(8,128)(2,1)} %collective-permute-done.10.refs_1_.refs_2_, bf16[384,1024]{1,0:T(8,128)(2,1)} %collective-permute-done.11.refs_2_.refs_3_, ...), custom_call_target="tpu_custom_call" | custom-call | flops 4831838208 | bytes 10000000 | tf_op jit(solution)/shard_map/weight_grad/pallas_call | solution.py:646
  269.3 2.4 constant_dynamic-slice_fusion.3
  273.9 11.8 %collective-permute-done.25.refs_2_ = bf16[384,1024]{1,0:T(8,128)(2,1)S(1)} collective-permute-done((bf16[384,1024]{1,0:T(8,128)(2,1)}, bf16[384,1024]{1,0:T(8,128)(2,1)S(1)}, u32[]{:S(2)}, u32[]{:S(2)}) %collective-permute-start.25) | collective-permute-done | bytes 786464 | tf_op jit(solution)/shard_map/ppermute | solution.py:777
  286.6 7.9 %mid_back.1 = (f32[384,1024]{1,0:T(8,128)}, bf16[384,1024]{1,0:T(8,128)(2,1)}, f32[1,1024]{1,0:T(1,128)}, bf16[384,512]{1,0:T(8,128)(2,1)}, bf16[384,512]{1,0:T(...) custom-call(s32[1]{0:T(128)} %bitcast.rank_ref, bf16[384,1024]{1,0:T(8,128)(2,1)} %bitcast.313, ...), custom_call_target="tpu_custom_call" | custom-call | flops 1000000 | bytes 1000000 | tf_op jit(solution)/shard_map/mid_back/pallas_call | solution.py:733
  294.6 11.1 %weight_grad.5.refs_4_ = bf16[1024,1536]{1,0:T(8,128)(2,1)} custom-call(bf16[384,1024]{1,0:T(8,128)(2,1)} %get-tuple-element.56.value_ref.refs_0_, bf16[384,1024]{1,0:T(8,128)(2,1)} %copy-done.22, bf16[384,1024]{1,0:T(8,128)(2,1)} %collective-permute-done.20.refs_2_, bf16[384,1024]{1,0:T(8,128)(2,1)} %copy-done.58, ...), custom_call_target="tpu_custom_call" | custom-call | flops 9663676416 | bytes 10000000 | tf_op jit(solution)/shard_map/weight_grad/pallas_call | solution.py:646
  314.9 2.7 collective-permute-start.32
  320.6 3.6 collective-permute-done.31.refs_0_
  325.7 6.2 %collective-permute-done.32.refs_1_ = bf16[4,32,768]{2,1,0:T(8,128)(2,1)S(1)} collective-permute-done((bf16[4,32,768]{2,1,0:T(8,128)(2,1)S(1)}, bf16[4,32,768]{2,1,0:T(8,128)(2,1)S(1)}, u32[]{:S(2)}, u32[]{:S(2)}) %collective-permute-start.32) | collective-permute-done | bytes 196640 | tf_op jit(solution)/shard_map/ppermute | solution.py:777
  337.0 6.8 %collective-permute-done.28.refs_2_.refs_1_ = bf16[384,512]{1,0:T(8,128)(2,1)} collective-permute-done((bf16[384,512]{1,0:T(8,128)(2,1)}, bf16[384,512]{1,0:T(8,128)(2,1)}, u32[]{:S(2)}, u32[]{:S(2)}) %collective-permute-start.28) | collective-permute-done | bytes 393248 | tf_op jit(solution)/shard_map/ppermute | solution.py:777
  349.4 9.2 %ungate_rows.1 = (bf16[1536,512]{1,0:T(8,128)(2,1)}, bf16[1536,512]{1,0:T(8,128)(2,1)}, f32[1,256]{1,0:T(1,128)}) custom-call(bf16[1536,512]{1,0:T(8,128)(2,1)} %get-tuple-element.63.dealt_ref, f32[1536,128]{1,0:T(8,128)} %bitcast.277, f32[1536,512]{1,0:T(8,128)} %get-tuple-element.50.gate_ref, f32[1,256]{1,0:T(1,128)} %broadcast_in_dim_reshape.14.gain_ref, ...), custom_call_target="tpu_custom_call" | custom-call | flops 1000000 | bytes 1000000 | tf_op jit(solution)/shard_map/ungate_rows/pallas_call | solution.py:514
  360.6 3.6 collective-permute-start.39
  364.2 2.4 collective-permute-done.35.refs_1_
  366.6 3.0 collective-permute-start.40
  372.7 42.1 %recurrence_backward.1 = (bf16[1536,1152]{1,0:T(8,128)(2,1)}, f32[8,1024]{1,0:T(8,128)}) custom-call(bf16[1536,1024]{1,0:T(8,128)(2,1)} %get-tuple-element.47.edge_ref.proj_ref.refs_0_, bf16[1536,1024]{1,0:T(8,128)(2,1)} %get-tuple-element.47.edge_ref.proj_ref.refs_0_, f32[8,1024]{1,0:T(8,128)} %select_maximum_fusion.conv_ref, f32[1536,128]{1,0:T(8,128)} %bitcast.278, ...), custom_call_target="tpu_custom_call" | custom-call | flops 1000000 | bytes 1000000 | tf_op jit(solution)/shard_map/recurrence_backward/pallas_call | solution.py:344
  414.8 5.6 %weight_grad.6 = (bf16[1024,512]{1,0:T(8,128)(2,1)}, f32[1024,1]{1,0:T(8,128)}) custom-call(bf16[1536,1024]{1,0:T(8,128)(2,1)} %get-tuple-element.70.refs_0_.normed_ref, bf16[1536,512]{1,0:T(8,128)(2,1)} %get-tuple-element.72.refs_1_.gate_ref, bf16[1024,512]{1,0:T(8,128)(2,1)} %slice.379.refs_2_, bf16[1536,1152]{1,0:T(8,128)(2,1)} %get-tuple-element.69.refs_3_.refs_8_.grad_ref), custom_call_target="tpu_custom_call" | custom-call | flops 3221225472 | bytes 10000000 | tf_op jit(solution)/shard_map/weight_grad/pallas_call | solution.py:646
  424.7 5.7 %weight_grad.7 = bf16[1024,512]{1,0:T(8,128)(2,1)} custom-call(bf16[384,1024]{1,0:T(8,128)(2,1)} %copied.7.refs_0_, bf16[384,1024]{1,0:T(8,128)(2,1)} %copy-done.57, bf16[384,1024]{1,0:T(8,128)(2,1)} %collective-permute-done.36.refs_2_, bf16[384,1024]{1,0:T(8,128)(2,1)} %collective-permute-done.37.refs_3_, ...), custom_call_target="tpu_custom_call" | custom-call | flops 3221225472 | bytes 10000000 | tf_op jit(solution)/shard_map/weight_grad/pallas_call | solution.py:646
  442.1 11.3 %collective-permute-done.21.refs_2_ = bf16[384,1024]{1,0:T(8,128)(2,1)S(1)} collective-permute-done((bf16[384,1024]{1,0:T(8,128)(2,1)}, bf16[384,1024]{1,0:T(8,128)(2,1)S(1)}, u32[]{:S(2)}, u32[]{:S(2)}) %collective-permute-start.21) | collective-permute-done | bytes 786464 | tf_op jit(solution)/shard_map/ppermute | solution.py:777
  455.1 17.7 %unpack.1 = (bf16[1536,1152]{1,0:T(8,128)(2,1)}, bf16[1024,1152]{1,0:T(8,128)(2,1)}, f32[1024,1]{1,0:T(8,128)}) custom-call(bf16[1536,1152]{1,0:T(8,128)(2,1)} %get-tuple-element.69.refs_3_.refs_8_.grad_ref, f32[1,1536]{1,0:T(1,128)} %copy-done.49, bf16[1536,1024]{1,0:T(8,128)(2,1)} %get-tuple-element.70.refs_0_.normed_ref, ...), custom_call_target="tpu_custom_call" | custom-call | flops 1000000 | bytes 1000000 | tf_op jit(solution)/shard_map/unpack/pallas_call | solution.py:555
  480.2 3.5 all-to-all-start.2
  483.7 4.6 fusion.8
  488.3 10.7 %unproject.1 = bf16[1536,1024]{1,0:T(8,128)(2,1)} custom-call(bf16[1536,1152]{1,0:T(8,128)(2,1)} %get-tuple-element.75.grad_ref, bf16[1536,512]{1,0:T(8,128)(2,1)} %get-tuple-element.72.refs_1_.gate_ref, bf16[1024,1664]{1,0:T(8,128)(2,1)} %get-tuple-element.71.w_ref), custom_call_target="tpu_custom_call" | custom-call | flops 1000000 | bytes 1000000 | tf_op jit(solution)/shard_map/unproject/pallas_call | solution.py:596
  499.0 3.6 fusion.67
  511.3 2.6 collective-permute-start.48
  514.6 6.6 %collective-permute-done.46 = bf16[4,32,1045]{2,1,0:T(8,128)(2,1)S(1)} collective-permute-done((bf16[4,32,1045]{2,1,0:T(8,128)(2,1)S(1)}, bf16[4,32,1045]{2,1,0:T(8,128)(2,1)S(1)}, u32[]{:S(2)}, u32[]{:S(2)}) %collective-permute-start.46) | collective-permute-done | bytes 267552 | tf_op jit(solution)/shard_map/ppermute | solution.py:777
  525.9 7.4 %collective-permute-done.47 = bf16[4,32,1045]{2,1,0:T(8,128)(2,1)} collective-permute-done((bf16[4,32,1045]{2,1,0:T(8,128)(2,1)}, bf16[4,32,1045]{2,1,0:T(8,128)(2,1)}, u32[]{:S(2)}, u32[]{:S(2)}) %collective-permute-start.47) | collective-permute-done | bytes 267552 | tf_op jit(solution)/shard_map/ppermute | solution.py:777
  535.3 3.5 all-to-all-start.1
  543.2 4.4 in_back.1
  (392 shorter events, 169.2 us)
Async XLA Ops:
  7.2 71.4 %all-gather.6.cloned.1.call-start = ((), (), s32[]{:S(2)}) async-start(), calls=%async_computation.3 | async-start | bytes 1179648 | tf_op jit(solution)/shard_map/all_gather | solution.py:934
  7.9 76.4 %all-gather.8.cloned.1.call-start = ((), (), s32[]{:S(2)}) async-start(), calls=%async_computation.4 | async-start | bytes 3833856 | tf_op jit(solution)/shard_map/all_gather | solution.py:796
  24.8 172.7 %all-gather.10.cloned.1.call-start = ((), (), s32[]{:S(2)}) async-start(), calls=%async_computation.5 | async-start | bytes 5308416 | tf_op jit(solution)/shard_map/all_gather | solution.py:790
  38.8 12.8 %collective-permute-start.7 = (f32[8,384]{1,0:T(8,128)S(1)}, f32[8,384]{1,0:T(8,128)S(1)}, u32[]{:S(2)}, u32[]{:S(2)}) collective-permute-start(f32[8,384]{1,0:T(8,128)S(1)} %bitcast.347), channel_id=1, source_target_pairs={{0,16},{8,24},{16,0},{24,8},{1,17},{9,25},{17,1},{25,9},{2,18},{10... | collective-permute-start | bytes 36872 | tf_op jit(solution)/shard_map/ppermute | solution.py:777
  41.5 20.7 %collective-permute-start.3 = (bf16[384,1024]{1,0:T(8,128)(2,1)S(1)}, bf16[384,1024]{1,0:T(8,128)(2,1)S(1)}, u32[]{:S(2)}, u32[]{:S(2)}) collective-permute-start(bf16[384,1024]{1,0:T(8,128)(2,1)S(1)} %bitcast.304), channel_id=1, source_target_pairs={{0,8},{8,0},{16,24},{24,16},{1,9},{9,1},{17,25},{25,17},{2,10},{10... | collective-permute-start | bytes 2359304 | tf_op jit(solution)/shard_map/ppermute | solution.py:777
  42.3 33.1 %collective-permute-start.4 = (bf16[384,1024]{1,0:T(8,128)(2,1)S(1)}, bf16[384,1024]{1,0:T(8,128)(2,1)S(1)}, u32[]{:S(2)}, u32[]{:S(2)}) collective-permute-start(bf16[384,1024]{1,0:T(8,128)(2,1)S(1)} %bitcast.305), channel_id=1, source_target_pairs={{0,16},{8,24},{16,0},{24,8},{1,17},{9,25},{17,1},{25,9},{2,18},{10... | collective-permute-start | bytes 2359304 | tf_op jit(solution)/shard_map/ppermute | solution.py:777
  49.3 26.1 %collective-permute-start.5 = (bf16[384,1024]{1,0:T(8,128)(2,1)S(1)}, bf16[384,1024]{1,0:T(8,128)(2,1)}, u32[]{:S(2)}, u32[]{:S(2)}) collective-permute-start(bf16[384,1024]{1,0:T(8,128)(2,1)S(1)} %bitcast.306), channel_id=1, source_target_pairs={{0,24},{8,16},{16,8},{24,0},{1,25},{9,17},{17,9},{25,1},{2,26},{10... | collective-permute-start | bytes 2359304 | tf_op jit(solution)/shard_map/ppermute | solution.py:777
  80.9 35.2 %collective-permute-start.12 = (bf16[256,2048]{1,0:T(8,128)(2,1)}, bf16[256,2048]{1,0:T(8,128)(2,1)S(1)}, u32[]{:S(2)}, u32[]{:S(2)}) collective-permute-start(bf16[256,2048]{1,0:T(8,128)(2,1)} %copied.5.refs_4_), channel_id=1, source_target_pairs={{0,8},{8,0},{16,24},{24,16},{1,9},{9,1},{17,25},{25,17},{2,10},{10... | collective-permute-start | bytes 3145736 | tf_op jit(solution)/shard_map/ppermute | solution.py:777
  81.7 62.5 %collective-permute-start.13 = (bf16[256,2048]{1,0:T(8,128)(2,1)}, bf16[256,2048]{1,0:T(8,128)(2,1)S(1)}, u32[]{:S(2)}, u32[]{:S(2)}) collective-permute-start(bf16[256,2048]{1,0:T(8,128)(2,1)} %copied.5.refs_4_), channel_id=1, source_target_pairs={{0,16},{8,24},{16,0},{24,8},{1,17},{9,25},{17,1},{25,9},{2,18},{10... | collective-permute-start | bytes 3145736 | tf_op jit(solution)/shard_map/ppermute | solution.py:777
  82.9 61.3 %collective-permute-start.14 = (bf16[256,2048]{1,0:T(8,128)(2,1)}, bf16[256,2048]{1,0:T(8,128)(2,1)S(1)}, u32[]{:S(2)}, u32[]{:S(2)}) collective-permute-start(bf16[256,2048]{1,0:T(8,128)(2,1)} %copied.5.refs_4_), channel_id=1, source_target_pairs={{0,24},{8,16},{16,8},{24,0},{1,25},{9,17},{17,9},{25,1},{2,26},{10... | collective-permute-start | bytes 3145736 | tf_op jit(solution)/shard_map/ppermute | solution.py:777
  113.7 44.5 %collective-permute-start.10 = (bf16[384,1024]{1,0:T(8,128)(2,1)}, bf16[384,1024]{1,0:T(8,128)(2,1)}, u32[]{:S(2)}, u32[]{:S(2)}) collective-permute-start(bf16[384,1024]{1,0:T(8,128)(2,1)} %copied.4.refs_0_), channel_id=1, source_target_pairs={{0,16},{8,24},{16,0},{24,8},{1,17},{9,25},{17,1},{25,9},{2,18},{10... | collective-permute-start | bytes 2359304 | tf_op jit(solution)/shard_map/ppermute | solution.py:777
  114.1 44.1 %collective-permute-start.11 = (bf16[384,1024]{1,0:T(8,128)(2,1)}, bf16[384,1024]{1,0:T(8,128)(2,1)}, u32[]{:S(2)}, u32[]{:S(2)}) collective-permute-start(bf16[384,1024]{1,0:T(8,128)(2,1)} %copied.4.refs_0_), channel_id=1, source_target_pairs={{0,24},{8,16},{16,8},{24,0},{1,25},{9,17},{17,9},{25,1},{2,26},{10... | collective-permute-start | bytes 2359304 | tf_op jit(solution)/shard_map/ppermute | solution.py:777
  116.1 42.2 %collective-permute-start.9 = (bf16[384,1024]{1,0:T(8,128)(2,1)}, bf16[384,1024]{1,0:T(8,128)(2,1)}, u32[]{:S(2)}, u32[]{:S(2)}) collective-permute-start(bf16[384,1024]{1,0:T(8,128)(2,1)} %copied.4.refs_0_), channel_id=1, source_target_pairs={{0,8},{8,0},{16,24},{24,16},{1,9},{9,1},{17,25},{25,17},{2,10},{10... | collective-permute-start | bytes 2359304 | tf_op jit(solution)/shard_map/ppermute | solution.py:777
  166.6 19.3 %collective-permute-start.16 = (bf16[384,512]{1,0:T(8,128)(2,1)}, bf16[384,512]{1,0:T(8,128)(2,1)S(1)}, u32[]{:S(2)}, u32[]{:S(2)}) collective-permute-start(bf16[384,512]{1,0:T(8,128)(2,1)} %get-tuple-element.53.refs_6_), channel_id=1, source_target_pairs={{0,16},{8,24},{16,0},{24,8},{1,17},{9,25},{17,1},{25,9},{2,18},{10... | collective-permute-start | bytes 1179656 | tf_op jit(solution)/shard_map/ppermute | solution.py:777
  166.9 19.0 %collective-permute-start.17 = (bf16[384,512]{1,0:T(8,128)(2,1)}, bf16[384,512]{1,0:T(8,128)(2,1)S(1)}, u32[]{:S(2)}, u32[]{:S(2)}) collective-permute-start(bf16[384,512]{1,0:T(8,128)(2,1)} %get-tuple-element.54.refs_7_), channel_id=1, source_target_pairs={{0,24},{8,16},{16,8},{24,0},{1,25},{9,17},{17,9},{25,1},{2,26},{10... | collective-permute-start | bytes 1179656 | tf_op jit(solution)/shard_map/ppermute | solution.py:777
  193.2 18.5 %collective-permute-start.18 = (bf16[384,1024]{1,0:T(8,128)(2,1)}, bf16[384,1024]{1,0:T(8,128)(2,1)S(1)}, u32[]{:S(2)}, u32[]{:S(2)}) collective-permute-start(bf16[384,1024]{1,0:T(8,128)(2,1)} %get-tuple-element.56.value_ref.refs_0_), channel_id=1, source_target_pairs={{0,8},{8,0},{16,24},{24,16},{1,9},{9,1},{17,25},{25,17},{2,10},{10... | collective-permute-start | bytes 2359304 | tf_op jit(solution)/shard_map/ppermute | solution.py:777
  195.8 31.9 %collective-permute-start.20 = (bf16[384,1024]{1,0:T(8,128)(2,1)S(1)}, bf16[384,1024]{1,0:T(8,128)(2,1)}, u32[]{:S(2)}, u32[]{:S(2)}) collective-permute-start(bf16[384,1024]{1,0:T(8,128)(2,1)S(1)} %copy-done.21), channel_id=1, source_target_pairs={{0,16},{8,24},{16,0},{24,8},{1,17},{9,25},{17,1},{25,9},{2,18},{10... | collective-permute-start | bytes 2359304 | tf_op jit(solution)/shard_map/ppermute | solution.py:777
  218.6 42.7 %collective-permute-start.24 = (bf16[384,1024]{1,0:T(8,128)(2,1)}, bf16[384,1024]{1,0:T(8,128)(2,1)S(1)}, u32[]{:S(2)}, u32[]{:S(2)}) collective-permute-start(bf16[384,1024]{1,0:T(8,128)(2,1)} %convolution_convert_fusion.6), channel_id=1, source_target_pairs={{0,8},{8,0},{16,24},{24,16},{1,9},{9,1},{17,25},{25,17},{2,10},{10... | collective-permute-start | bytes 2359304 | tf_op jit(solution)/shard_map/ppermute | solution.py:777
  226.3 26.4 %collective-permute-start.22 = (bf16[384,1024]{1,0:T(8,128)(2,1)}, bf16[384,1024]{1,0:T(8,128)(2,1)S(1)}, u32[]{:S(2)}, u32[]{:S(2)}) collective-permute-start(bf16[384,1024]{1,0:T(8,128)(2,1)} %copied.6), channel_id=1, source_target_pairs={{0,24},{8,16},{16,8},{24,0},{1,25},{9,17},{17,9},{25,1},{2,26},{10... | collective-permute-start | bytes 2359304 | tf_op jit(solution)/shard_map/ppermute | solution.py:777
  237.0 48.7 %collective-permute-start.25 = (bf16[384,1024]{1,0:T(8,128)(2,1)}, bf16[384,1024]{1,0:T(8,128)(2,1)S(1)}, u32[]{:S(2)}, u32[]{:S(2)}) collective-permute-start(bf16[384,1024]{1,0:T(8,128)(2,1)} %convolution_convert_fusion.5), channel_id=1, source_target_pairs={{0,16},{8,24},{16,0},{24,8},{1,17},{9,25},{17,1},{25,9},{2,18},{10... | collective-permute-start | bytes 2359304 | tf_op jit(solution)/shard_map/ppermute | solution.py:777
  259.5 26.2 %collective-permute-start.26 = (bf16[384,1024]{1,0:T(8,128)(2,1)}, bf16[384,1024]{1,0:T(8,128)(2,1)}, u32[]{:S(2)}, u32[]{:S(2)}) collective-permute-start(bf16[384,1024]{1,0:T(8,128)(2,1)} %convolution_convert_fusion.4), channel_id=1, source_target_pairs={{0,24},{8,16},{16,8},{24,0},{1,25},{9,17},{17,9},{25,1},{2,26},{10... | collective-permute-start | bytes 2359304 | tf_op jit(solution)/shard_map/ppermute | solution.py:777
  271.8 39.0 %collective-permute-start.30 = (bf16[4,4,32,768]{3,2,0,1:T(8,128)(2,1)S(1)}, bf16[4,4,32,768]{3,2,0,1:T(8,128)(2,1)}, u32[]{:S(2)}, u32[]{:S(2)}) collective-permute-start(bf16[4,4,32,768]{3,2,0,1:T(8,128)(2,1)S(1)} %bitcast.316), channel_id=1, source_target_pairs={{0,1},{1,0},{2,3},{3,2},{4,5},{5,4},{6,7},{7,6},{8,9},{9,8},{10,11... | collective-permute-start | bytes 2359304 | tf_op jit(solution)/shard_map/ppermute | solution.py:777
  309.1 49.5 %collective-permute-start.34 = (bf16[4,4,32,1536]{3,2,0,1:T(8,128)(2,1)}, bf16[4,4,32,1536]{3,2,0,1:T(8,128)(2,1)}, u32[]{:S(2)}, u32[]{:S(2)}) collective-permute-start(bf16[4,4,32,1536]{3,2,0,1:T(8,128)(2,1)} %bitcast.267), channel_id=1, source_target_pairs={{0,1},{1,0},{2,3},{3,2},{4,5},{5,4},{6,7},{7,6},{8,9},{9,8},{10,11... | collective-permute-start | bytes 4718600 | tf_op jit(solution)/shard_map/ppermute | solution.py:777
  314.9 17.1 %collective-permute-start.32 = (bf16[4,32,768]{2,1,0:T(8,128)(2,1)S(1)}, bf16[4,32,768]{2,1,0:T(8,128)(2,1)S(1)}, u32[]{:S(2)}, u32[]{:S(2)}) collective-permute-start(bf16[4,32,768]{2,1,0:T(8,128)(2,1)S(1)} %get-tuple-element.134), channel_id=1, source_target_pairs={{0,4},{1,5},{2,6},{3,7},{4,0},{5,1},{6,2},{7,3},{8,12},{9,13},{10,... | collective-permute-start | bytes 589832 | tf_op jit(solution)/shard_map/ppermute | solution.py:777
  319.2 15.9 %collective-permute-start.33 = (bf16[4,32,768]{2,1,0:T(8,128)(2,1)}, bf16[4,32,768]{2,1,0:T(8,128)(2,1)}, u32[]{:S(2)}, u32[]{:S(2)}) collective-permute-start(bf16[4,32,768]{2,1,0:T(8,128)(2,1)} %get-tuple-element.133), channel_id=1, source_target_pairs={{0,6},{1,7},{2,4},{3,5},{4,2},{5,3},{6,0},{7,1},{8,14},{9,15},{10,... | collective-permute-start | bytes 589832 | tf_op jit(solution)/shard_map/ppermute | solution.py:777
  319.2 17.7 %collective-permute-start.27 = (bf16[384,512]{1,0:T(8,128)(2,1)}, bf16[384,512]{1,0:T(8,128)(2,1)S(1)}, u32[]{:S(2)}, u32[]{:S(2)}) collective-permute-start(bf16[384,512]{1,0:T(8,128)(2,1)} %get-tuple-element.65), channel_id=1, source_target_pairs={{0,8},{8,0},{16,24},{24,16},{1,9},{9,1},{17,25},{25,17},{2,10},{10... | collective-permute-start | bytes 1179656 | tf_op jit(solution)/shard_map/ppermute | solution.py:777
  324.2 19.6 %collective-permute-start.28 = (bf16[384,512]{1,0:T(8,128)(2,1)}, bf16[384,512]{1,0:T(8,128)(2,1)}, u32[]{:S(2)}, u32[]{:S(2)}) collective-permute-start(bf16[384,512]{1,0:T(8,128)(2,1)} %get-tuple-element.66), channel_id=1, source_target_pairs={{0,16},{8,24},{16,0},{24,8},{1,17},{9,25},{17,1},{25,9},{2,18},{10... | collective-permute-start | bytes 1179656 | tf_op jit(solution)/shard_map/ppermute | solution.py:777
  345.9 20.7 %collective-permute-start.35 = (bf16[384,1024]{1,0:T(8,128)(2,1)}, bf16[384,1024]{1,0:T(8,128)(2,1)S(1)}, u32[]{:S(2)}, u32[]{:S(2)}) collective-permute-start(bf16[384,1024]{1,0:T(8,128)(2,1)} %copied.7.refs_0_), channel_id=1, source_target_pairs={{0,8},{8,0},{16,24},{24,16},{1,9},{9,1},{17,25},{25,17},{2,10},{10... | collective-permute-start | bytes 2359304 | tf_op jit(solution)/shard_map/ppermute | solution.py:777
  347.1 73.4 %collective-permute-start.36 = (bf16[384,1024]{1,0:T(8,128)(2,1)}, bf16[384,1024]{1,0:T(8,128)(2,1)}, u32[]{:S(2)}, u32[]{:S(2)}) collective-permute-start(bf16[384,1024]{1,0:T(8,128)(2,1)} %copied.7.refs_0_), channel_id=1, source_target_pairs={{0,16},{8,24},{16,0},{24,8},{1,17},{9,25},{17,1},{25,9},{2,18},{10... | collective-permute-start | bytes 2359304 | tf_op jit(solution)/shard_map/ppermute | solution.py:777
  347.7 73.8 %collective-permute-start.37 = (bf16[384,1024]{1,0:T(8,128)(2,1)}, bf16[384,1024]{1,0:T(8,128)(2,1)}, u32[]{:S(2)}, u32[]{:S(2)}) collective-permute-start(bf16[384,1024]{1,0:T(8,128)(2,1)} %copied.7.refs_0_), channel_id=1, source_target_pairs={{0,24},{8,16},{16,8},{24,0},{1,25},{9,17},{17,9},{25,1},{2,26},{10... | collective-permute-start | bytes 2359304 | tf_op jit(solution)/shard_map/ppermute | solution.py:777
  360.5 61.3 %collective-permute-start.38 = (bf16[4,32,1536]{2,1,0:T(8,128)(2,1)S(1)}, bf16[4,32,1536]{2,1,0:T(8,128)(2,1)S(1)}, u32[]{:S(2)}, u32[]{:S(2)}) collective-permute-start(bf16[4,32,1536]{2,1,0:T(8,128)(2,1)S(1)} %get-tuple-element.124), channel_id=1, source_target_pairs={{0,2},{1,3},{2,0},{3,1},{4,6},{5,7},{6,4},{7,5},{8,10},{9,11},{10,... | collective-permute-start | bytes 1179656 | tf_op jit(solution)/shard_map/ppermute | solution.py:777
  360.6 63.3 %collective-permute-start.39 = (bf16[4,32,1536]{2,1,0:T(8,128)(2,1)S(1)}, bf16[4,32,1536]{2,1,0:T(8,128)(2,1)S(1)}, u32[]{:S(2)}, u32[]{:S(2)}) collective-permute-start(bf16[4,32,1536]{2,1,0:T(8,128)(2,1)S(1)} %get-tuple-element.123), channel_id=1, source_target_pairs={{0,4},{1,5},{2,6},{3,7},{4,0},{5,1},{6,2},{7,3},{8,12},{9,13},{10,... | collective-permute-start | bytes 1179656 | tf_op jit(solution)/shard_map/ppermute | solution.py:777
  366.6 57.4 %collective-permute-start.40 = (bf16[4,32,1536]{2,1,0:T(8,128)(2,1)S(1)}, bf16[4,32,1536]{2,1,0:T(8,128)(2,1)}, u32[]{:S(2)}, u32[]{:S(2)}) collective-permute-start(bf16[4,32,1536]{2,1,0:T(8,128)(2,1)S(1)} %get-tuple-element.122), channel_id=1, source_target_pairs={{0,6},{1,7},{2,4},{3,5},{4,2},{5,3},{6,0},{7,1},{8,14},{9,15},{10,... | collective-permute-start | bytes 1179656 | tf_op jit(solution)/shard_map/ppermute | solution.py:777
  420.4 20.7 %collective-permute-start.19 = (bf16[384,1024]{1,0:T(8,128)(2,1)}, bf16[384,1024]{1,0:T(8,128)(2,1)S(1)}, u32[]{:S(2)}, u32[]{:S(2)}) collective-permute-start(bf16[384,1024]{1,0:T(8,128)(2,1)} %convolution_convert_fusion.2), channel_id=1, source_target_pairs={{0,8},{8,0},{16,24},{24,16},{1,9},{9,1},{17,25},{25,17},{2,10},{10... | collective-permute-start | bytes 2359304 | tf_op jit(solution)/shard_map/ppermute | solution.py:777
  421.6 31.8 %collective-permute-start.21 = (bf16[384,1024]{1,0:T(8,128)(2,1)}, bf16[384,1024]{1,0:T(8,128)(2,1)S(1)}, u32[]{:S(2)}, u32[]{:S(2)}) collective-permute-start(bf16[384,1024]{1,0:T(8,128)(2,1)} %convolution_convert_fusion.1), channel_id=1, source_target_pairs={{0,16},{8,24},{16,0},{24,8},{1,17},{9,25},{17,1},{25,9},{2,18},{10... | collective-permute-start | bytes 2359304 | tf_op jit(solution)/shard_map/ppermute | solution.py:777
  421.9 31.5 %collective-permute-start.23 = (bf16[384,1024]{1,0:T(8,128)(2,1)}, bf16[384,1024]{1,0:T(8,128)(2,1)S(1)}, u32[]{:S(2)}, u32[]{:S(2)}) collective-permute-start(bf16[384,1024]{1,0:T(8,128)(2,1)} %convolution_convert_fusion), channel_id=1, source_target_pairs={{0,24},{8,16},{16,8},{24,0},{1,25},{9,17},{17,9},{25,1},{2,26},{10... | collective-permute-start | bytes 2359304 | tf_op jit(solution)/shard_map/ppermute | solution.py:777
  437.6 40.4 %collective-permute-start.49 = (bf16[4,32,1024]{2,1,0:T(8,128)(2,1)}, bf16[4,32,1024]{2,1,0:T(8,128)(2,1)S(1)}, u32[]{:S(2)}, u32[]{:S(2)}) collective-permute-start(bf16[4,32,1024]{2,1,0:T(8,128)(2,1)} %get-tuple-element.130), channel_id=1, source_target_pairs={{0,2},{1,3},{2,0},{3,1},{4,6},{5,7},{6,4},{7,5},{8,10},{9,11},{10,... | collective-permute-start | bytes 786440 | tf_op jit(solution)/shard_map/ppermute | solution.py:777
  437.6 40.4 %collective-permute-start.50 = (bf16[4,32,1024]{2,1,0:T(8,128)(2,1)}, bf16[4,32,1024]{2,1,0:T(8,128)(2,1)S(1)}, u32[]{:S(2)}, u32[]{:S(2)}) collective-permute-start(bf16[4,32,1024]{2,1,0:T(8,128)(2,1)} %get-tuple-element.132), channel_id=1, source_target_pairs={{0,4},{1,5},{2,6},{3,7},{4,0},{5,1},{6,2},{7,3},{8,12},{9,13},{10,... | collective-permute-start | bytes 786440 | tf_op jit(solution)/shard_map/ppermute | solution.py:777
  441.1 36.8 %collective-permute-start.51 = (bf16[4,32,1024]{2,1,0:T(8,128)(2,1)S(1)}, bf16[4,32,1024]{2,1,0:T(8,128)(2,1)}, u32[]{:S(2)}, u32[]{:S(2)}) collective-permute-start(bf16[4,32,1024]{2,1,0:T(8,128)(2,1)S(1)} %get-tuple-element.131), channel_id=1, source_target_pairs={{0,6},{1,7},{2,4},{3,5},{4,2},{5,3},{6,0},{7,1},{8,14},{9,15},{10,... | collective-permute-start | bytes 786440 | tf_op jit(solution)/shard_map/ppermute | solution.py:777
  478.0 28.2 %collective-permute-start.45 = (bf16[4,4,32,1045]{3,2,1,0:T(8,128)(2,1)}, bf16[4,4,32,1045]{3,2,1,0:T(8,128)(2,1)}, u32[]{:S(2)}, u32[]{:S(2)}) collective-permute-start(bf16[4,4,32,1045]{3,2,1,0:T(8,128)(2,1)} %dynamic-slice_bitcast_fusion), channel_id=1, source_target_pairs={{0,1},{1,0},{2,3},{3,2},{4,5},{5,4},{6,7},{7,6},{8,9},{9,8},{10,11... | collective-permute-start | bytes 3210248 | tf_op jit(solution)/shard_map/ppermute | solution.py:777
  480.2 25.8 %all-to-all-start.2 = ((bf16[4,32,3328]{2,1,0:T(8,128)(2,1)}), bf16[4,32,3328]{2,1,0:T(8,128)(2,1)S(1)}, u32[]{:S(2)}, u32[]{:S(2)}) async-start(bf16[4,32,3328]{2,1,0:T(8,128)(2,1)} %pad_maximum_fusion.7), calls=%async_computation.2 | async-start | bytes 1703936 | tf_op jit(solution)/shard_map/all_to_all | solution.py:840
  502.5 37.0 %collective-permute-start.42 = (bf16[384,1024]{1,0:T(8,128)(2,1)}, bf16[384,1024]{1,0:T(8,128)(2,1)}, u32[]{:S(2)}, u32[]{:S(2)}) collective-permute-start(bf16[384,1024]{1,0:T(8,128)(2,1)} %get-tuple-element.94), channel_id=1, source_target_pairs={{0,8},{8,0},{16,24},{24,16},{1,9},{9,1},{17,25},{25,17},{2,10},{10... | collective-permute-start | bytes 2359304 | tf_op jit(solution)/shard_map/ppermute | solution.py:777
  504.5 36.9 %collective-permute-start.43 = (bf16[384,1024]{1,0:T(8,128)(2,1)}, bf16[384,1024]{1,0:T(8,128)(2,1)}, u32[]{:S(2)}, u32[]{:S(2)}) collective-permute-start(bf16[384,1024]{1,0:T(8,128)(2,1)} %get-tuple-element.93), channel_id=1, source_target_pairs={{0,16},{8,24},{16,0},{24,8},{1,17},{9,25},{17,1},{25,9},{2,18},{10... | collective-permute-start | bytes 2359304 | tf_op jit(solution)/shard_map/ppermute | solution.py:777
  508.7 12.5 %collective-permute-start.46 = (bf16[4,32,1045]{2,1,0:T(8,128)(2,1)S(1)}, bf16[4,32,1045]{2,1,0:T(8,128)(2,1)S(1)}, u32[]{:S(2)}, u32[]{:S(2)}) collective-permute-start(bf16[4,32,1045]{2,1,0:T(8,128)(2,1)S(1)} %get-tuple-element.127), channel_id=1, source_target_pairs={{0,2},{1,3},{2,0},{3,1},{4,6},{5,7},{6,4},{7,5},{8,10},{9,11},{10,... | collective-permute-start | bytes 802568 | tf_op jit(solution)/shard_map/ppermute | solution.py:777
  509.5 23.8 %collective-permute-start.47 = (bf16[4,32,1045]{2,1,0:T(8,128)(2,1)}, bf16[4,32,1045]{2,1,0:T(8,128)(2,1)}, u32[]{:S(2)}, u32[]{:S(2)}) collective-permute-start(bf16[4,32,1045]{2,1,0:T(8,128)(2,1)} %get-tuple-element.129), channel_id=1, source_target_pairs={{0,4},{1,5},{2,6},{3,7},{4,0},{5,1},{6,2},{7,3},{8,12},{9,13},{10,... | collective-permute-start | bytes 802568 | tf_op jit(solution)/shard_map/ppermute | solution.py:777
  511.3 22.0 %collective-permute-start.48 = (bf16[4,32,1045]{2,1,0:T(8,128)(2,1)}, bf16[4,32,1045]{2,1,0:T(8,128)(2,1)}, u32[]{:S(2)}, u32[]{:S(2)}) collective-permute-start(bf16[4,32,1045]{2,1,0:T(8,128)(2,1)} %get-tuple-element.128), channel_id=1, source_target_pairs={{0,6},{1,7},{2,4},{3,5},{4,2},{5,3},{6,0},{7,1},{8,14},{9,15},{10,... | collective-permute-start | bytes 802568 | tf_op jit(solution)/shard_map/ppermute | solution.py:777
  521.9 20.4 %collective-permute-start.44 = (bf16[384,1024]{1,0:T(8,128)(2,1)S(1)}, bf16[384,1024]{1,0:T(8,128)(2,1)S(1)}, u32[]{:S(2)}, u32[]{:S(2)}) collective-permute-start(bf16[384,1024]{1,0:T(8,128)(2,1)S(1)} %copy-done.19), channel_id=1, source_target_pairs={{0,24},{8,16},{16,8},{24,0},{1,25},{9,17},{17,9},{25,1},{2,26},{10... | collective-permute-start | bytes 2359304 | tf_op jit(solution)/shard_map/ppermute | solution.py:777
  535.3 12.3 %all-to-all-start.1 = ((bf16[4,32,1045]{2,1,0:T(8,128)(2,1)}), bf16[4,32,1045]{2,1,0:T(8,128)(2,1)S(1)}, u32[]{:S(2)}, u32[]{:S(2)}) async-start(bf16[4,32,1045]{2,1,0:T(8,128)(2,1)} %fusion.14), calls=%async_computation.1 | async-start | bytes 589824 | tf_op jit(solution)/shard_map/all_to_all | solution.py:840
  (75 other events, 630.5 us)
Sparse Core Ops, SparseCore 0:
  9.6 24.7 all-gather.5
  36.7 39.9 all-gather.7
  78.3 50.5 all-gather.9

commit v2 on v1

v2 whole, which is shorter than its diff:
```python
import functools

import jax
import jax.numpy as jnp
from jax import lax
from jax.experimental import pallas as pl
from jax.experimental.pallas import tpu as pltpu
from jax.sharding import PartitionSpec as P

HEAD_COUNT = 8
DK = 128
DV = 256
BLOCK = 128
PER_STEP = 2
F32 = jnp.float32
BF16 = jnp.bfloat16


def mm(left, right):
    return jnp.dot(left.astype(BF16), right.astype(BF16), preferred_element_type=F32)


def mm_nt(left, right):
    return lax.dot_general(
        left.astype(BF16),
        right.astype(BF16),
        (((1,), (1,)), ((), ())),
        preferred_element_type=F32,
    )


def mm_tn(left, right):
    return lax.dot_general(
        left.astype(BF16),
        right.astype(BF16),
        (((0,), (0,)), ((), ())),
        preferred_element_type=F32,
    )


def masks():
    rows = lax.broadcasted_iota(jnp.int32, (BLOCK, BLOCK), 0)
    cols = lax.broadcasted_iota(jnp.int32, (BLOCK, BLOCK), 1)
    return rows, cols


def unit_inverses(mats, rows, cols):
    ident = (rows == cols).astype(F32)
    near = (rows // 16) == (cols // 16)
    power = [jnp.where(near, a, 0.0) for a in mats]
    result = [ident - p for p in power]
    span = 2
    while span < 16:
        power = [mm(p, p) for p in power]
        result = [t + mm(t, p) for t, p in zip(result, power)]
        span *= 2
    size = 16
    while size < BLOCK:
        off = ((rows // (2 * size)) == (cols // (2 * size))) & ((rows // size) != (cols // size))
        reach = [mm(jnp.where(off, a, 0.0), t) for a, t in zip(mats, result)]
        result = [t - mm(t, x) for t, x in zip(result, reach)]
        size *= 2
    return result


def convolve(ext_ref, conv_ref, col_ref, start, first, width):
    cols = pl.ds(first, width)
    total = ext_ref[pl.ds(16 + start, BLOCK), cols] * conv_ref[3:4, cols]
    for tap in range(3):
        keep = col_ref[pl.ds(start, BLOCK), tap : tap + 1]
        total += ext_ref[pl.ds(13 + tap + start, BLOCK), cols] * keep * conv_ref[tap : tap + 1, cols]
    return total


def column(col_ref, start, index):
    return col_ref[pl.ds(start, BLOCK), index : index + 1]


def strength(logit_ref, start, head, heads):
    return jax.nn.sigmoid(column(logit_ref, start, head))


def exact_nt(left, right):
    left_high, right_high = left.astype(BF16), right.astype(BF16)
    left_low = left - left_high.astype(F32)
    right_low = right - right_high.astype(F32)
    return mm_nt(left_high, right_high) + (mm_nt(left_high, right_low) + mm_nt(left_low, right_high))


def decay_matrix(col_ref, row_ref, start, head, heads, rows, cols):
    cum_i = column(col_ref, start, 5 + head)
    cum_j = row_ref[head : head + 1, pl.ds(start, BLOCK)]
    seg_i = column(col_ref, start, 3)
    seg_j = row_ref[heads : heads + 1, pl.ds(start, BLOCK)]
    within = (rows >= cols) & (seg_i == seg_j)
    return jnp.where(within, jnp.exp(jnp.where(within, cum_i - cum_j, 0.0)), 0.0)


def silu(values):
    return values * jax.nn.sigmoid(values)


def forward_kernel(
    heads, edge_ref, proj_ref, conv_ref, col_ref, row_ref, logit_ref, *refs,
):
    o_ref, s_ref, n_ref, t_ref, w_ref, p_ref, ext_ref, state_ref = refs[-8:]
    steps = proj_ref.shape[0] // BLOCK

    @pl.when(pl.program_id(0) == 0)
    def _():
        state_ref[...] = jnp.zeros_like(state_ref)

    ext_ref[:16, :] = edge_ref[...].astype(F32)
    ext_ref[16:, :] = proj_ref[...].astype(F32)
    rows, cols = masks()
    strict = rows > cols
    units = [(g, h) for g in range(steps) for h in range(heads)]
    queries, keys, values, mats, decays, betas = {}, {}, {}, [], {}, {}
    for g, h in units:
        start = g * BLOCK
        taken = functools.partial(convolve, ext_ref, conv_ref, col_ref, start)
        queries[g, h] = silu(taken(h * DK, DK))
        raw = silu(taken((heads + h) * DK, DK))
        keys[g, h] = raw * lax.rsqrt(jnp.sum(raw * raw, axis=1, keepdims=True) + 1e-06)
        values[g, h] = silu(taken(2 * heads * DK + h * DV, DV))
        decays[g, h] = decay_matrix(col_ref, row_ref, start, h, heads, rows, cols)
        betas[g, h] = strength(logit_ref, start, h, heads)
        beta = betas[g, h]
        inner = mm_nt(keys[g, h], keys[g, h])
        mats.append(jnp.where(strict, beta * inner * decays[g, h], 0.0))
    inverses = unit_inverses(mats, rows, cols)
    umats, wmats, pmats, boundary, reads = {}, {}, {}, {}, {}
    for (g, h), inverse in zip(units, inverses):
        start = g * BLOCK
        beta = betas[g, h]
        elog = column(col_ref, start, 5 + heads + h)
        flog = column(col_ref, start, 5 + 2 * heads + h)
        inverse = inverse.astype(BF16)
        t_ref[g, h] = inverse
        umats[g, h] = mm(inverse, beta * values[g, h])
        wmats[g, h] = mm(inverse, (beta * elog) * keys[g, h]).astype(BF16)
        w_ref[g, h] = wmats[g, h]
        pmats[g, h] = (exact_nt(queries[g, h], keys[g, h]) * decays[g, h]).astype(BF16)
        p_ref[g, h] = pmats[g, h]
        boundary[g, h] = (keys[g, h] * flog).T.astype(BF16)
        reads[g, h] = (queries[g, h] * elog).astype(BF16)
    for g in range(steps):
        start = g * BLOCK
        for h in range(heads):
            state = state_ref[h]
            low = state.astype(BF16)
            s_ref[g, h] = low
            news = (umats[g, h] - mm(wmats[g, h], low)).astype(BF16)
            n_ref[g, h] = news
            carried = col_ref[pl.ds(start + BLOCK - 1, 1), 5 + heads + h : 6 + heads + h]
            state_ref[h] = carried * state + mm(boundary[g, h], news)
            output = mm(reads[g, h], low) + mm(pmats[g, h], news)
            o_ref[pl.ds(start, BLOCK), h * DV : (h + 1) * DV] = output.astype(BF16)


def backward_kernel(
    heads, edge_ref, proj_ref, conv_ref, col_ref, row_ref, logit_ref,
    s_ref, n_ref, t_ref, w_ref, p_ref, do_ref, *refs,
):
    grad_ref, gconv_ref, ext_ref, shift_ref, dstate_ref, head_ref = refs[-6:]
    count = proj_ref.shape[0]
    steps = count // BLOCK
    channels = proj_ref.shape[1]

    @pl.when(pl.program_id(0) == 0)
    def _():
        dstate_ref[...] = jnp.zeros_like(dstate_ref)
        head_ref[...] = jnp.zeros_like(head_ref)
        gconv_ref[...] = jnp.zeros_like(gconv_ref)

    ext_ref[:16, :] = edge_ref[...].astype(F32)
    ext_ref[16:, :] = proj_ref[...].astype(F32)
    for tap in range(3):
        shift_ref[tap, count : count + 8, :] = head_ref[tap]
    rows, cols = masks()
    strict = rows > cols
    units = [(g, h) for g in reversed(range(steps)) for h in range(heads)]
    queries, keys, pre, reads, first, gains = {}, {}, {}, {}, {}, {}
    for g, h in units:
        start = g * BLOCK
        taken = functools.partial(convolve, ext_ref, conv_ref, col_ref, start)
        elog = column(col_ref, start, 5 + heads + h)
        out_grad = do_ref[pl.ds(start, BLOCK), h * DV : (h + 1) * DV]
        queries[g, h] = silu(taken(h * DK, DK))
        raw = silu(taken((heads + h) * DK, DK))
        scale = lax.rsqrt(jnp.sum(raw * raw, axis=1, keepdims=True) + 1e-06)
        keys[g, h] = (raw * scale, scale)
        first[g, h] = mm_tn(p_ref[g, h], out_grad)
        gains[g, h] = mm_tn(queries[g, h] * elog, out_grad)
    news_grads, state_grads = {}, {}
    for g in reversed(range(steps)):
        start = g * BLOCK
        for h in range(heads):
            flog = column(col_ref, start, 5 + 2 * heads + h)
            dstate = dstate_ref[h]
            low = dstate.astype(BF16)
            state_grads[g, h] = low
            news_grad = (first[g, h] + mm(keys[g, h][0] * flog, low)).astype(BF16)
            news_grads[g, h] = news_grad
            carried = col_ref[pl.ds(start + BLOCK - 1, 1), 5 + heads + h : 6 + heads + h]
            dstate_ref[h] = gains[g, h] + carried * dstate - mm_tn(w_ref[g, h], news_grad)
    lane = lax.broadcasted_iota(jnp.int32, (BLOCK, 128), 1)

    def through_conv(g, first_col, width, grad):
        start = g * BLOCK
        cols_ = pl.ds(first_col, width)
        value = convolve(ext_ref, conv_ref, col_ref, start, first_col, width)
        gate = jax.nn.sigmoid(value)
        grad = grad * (gate * (1.0 + value * (1.0 - gate)))
        shift_ref[3, pl.ds(start, BLOCK), cols_] = grad * conv_ref[3:4, cols_]
        sums = []
        for tap in range(3):
            kept = grad * col_ref[pl.ds(start, BLOCK), tap : tap + 1]
            shift_ref[tap, pl.ds(start, BLOCK), cols_] = kept * conv_ref[tap : tap + 1, cols_]
            sums.append(
                jnp.sum(kept * ext_ref[pl.ds(13 + tap + start, BLOCK), cols_], axis=0, keepdims=True)
            )
        sums.append(
            jnp.sum(grad * ext_ref[pl.ds(16 + start, BLOCK), cols_], axis=0, keepdims=True)
        )
        for tap in range(4):
            gconv_ref[tap : tap + 1, cols_] += sums[tap]

    logit_grads = {}
    for g, h in units:
        start = g * BLOCK
        beta = strength(logit_ref, start, h, heads)
        elog = column(col_ref, start, 5 + heads + h)
        flog = column(col_ref, start, 5 + 2 * heads + h)
        key, scale = keys[g, h]
        query = queries[g, h]
        out_grad = do_ref[pl.ds(start, BLOCK), h * DV : (h + 1) * DV]
        decay = decay_matrix(col_ref, row_ref, start, h, heads, rows, cols)
        key_low = key.astype(BF16)
        inner = mm_nt(key_low, key_low) * decay
        news, state, dstate = n_ref[g, h], s_ref[g, h], state_grads[g, h]
        rhs_grad = mm_tn(t_ref[g, h], news_grads[g, h])
        rhs_low = rhs_grad.astype(BF16)
        within = (mm_nt(out_grad, news) * decay).astype(BF16)
        mat_grad = jnp.where(strict, -mm_nt(rhs_low, news), 0.0)
        pair = (mat_grad * beta * decay).astype(BF16)
        back = mm_nt(rhs_low, state)
        q_grad = mm(within, key_low) + elog * mm_nt(out_grad, state)
        k_grad = (
            mm_tn(within, query)
            + mm(pair, key_low)
            + mm_tn(pair, key_low)
            + flog * mm_nt(news, dstate)
            - (beta * elog) * back
        )
        value = silu(convolve(ext_ref, conv_ref, col_ref, start, 2 * heads * DK + h * DV, DV))
        beta_grad = (
            jnp.sum(mat_grad * inner - elog * (key * back), axis=1, keepdims=True)
            + jnp.sum(rhs_grad * value, axis=1, keepdims=True)
        )
        logit_grads[g, h] = beta_grad * beta * (1.0 - beta)
        raw_grad = scale * (k_grad - key * jnp.sum(k_grad * key, axis=1, keepdims=True))
        through_conv(g, h * DK, DK, q_grad)
        through_conv(g, (heads + h) * DK, DK, raw_grad)
        through_conv(g, 2 * heads * DK + h * DV, DV, beta * rhs_grad)
    for g in range(steps):
        total = jnp.zeros((BLOCK, 128), F32)
        for h in range(heads):
            total = jnp.where(lane == h, logit_grads[g, h], total)
        grad_ref[pl.ds(g * BLOCK, BLOCK), channels : channels + 128] = total.astype(BF16)
        grad_ref[pl.ds(g * BLOCK, BLOCK), channels + 128 :] = jnp.zeros((BLOCK, 128), BF16)
    total = shift_ref[3, :count, :]
    for tap in range(3):
        total += shift_ref[tap, pl.ds(3 - tap, count), :]
    grad_ref[:, :channels] = total.astype(BF16)
    for tap in range(3):
        head_ref[tap] = shift_ref[tap, :8, :]


def saved_shapes(blocks, heads):
    return (
        jax.ShapeDtypeStruct((blocks, heads, DK, DV), BF16),
        jax.ShapeDtypeStruct((blocks, heads, BLOCK, DV), BF16),
        jax.ShapeDtypeStruct((blocks, heads, BLOCK, BLOCK), BF16),
        jax.ShapeDtypeStruct((blocks, heads, BLOCK, DK), BF16),
        jax.ShapeDtypeStruct((blocks, heads, BLOCK, BLOCK), BF16),
    )


def saved_specs(shapes, index):
    return [
        pl.BlockSpec((PER_STEP,) + shape.shape[1:], lambda i: (index(i), 0, 0, 0))
        for shape in shapes
    ]


def common_specs(step, channels, logits, index):
    return [
        pl.BlockSpec((16, channels), lambda i: (jnp.maximum(index(i) * (step // 16) - 1, 0), 0)),
        pl.BlockSpec((step, channels), lambda i: (index(i), 0)),
        pl.BlockSpec((8, channels), lambda i: (0, 0)),
        pl.BlockSpec((step, 128), lambda i: (index(i), 0)),
        pl.BlockSpec((8, step), lambda i: (0, index(i))),
        pl.BlockSpec((step, logits), lambda i: (index(i), 0)),
    ]


VMEM_BYTES = 56 * 1024 * 1024
SMALL_COST = pl.CostEstimate(flops=10**6, bytes_accessed=10**6, transcendentals=0)
ANYWHERE = pl.BlockSpec(memory_space=pl.ANY)
WHOLE = pl.BlockSpec(memory_space=pltpu.VMEM)
SCALAR = pl.BlockSpec(memory_space=pltpu.SMEM)


def params():
    return pltpu.CompilerParams(dimension_semantics=("arbitrary",), vmem_limit_bytes=VMEM_BYTES)


def forward_recurrence(proj, conv, cols, rows, logits, heads, tokens):
    count, channels = proj.shape
    step = BLOCK * PER_STEP
    shapes = saved_shapes(count // BLOCK, heads)
    index = lambda i: i
    return pl.pallas_call(
        functools.partial(forward_kernel, heads),
        grid=(count // step,),
        in_specs=common_specs(step, channels, 128, index) + [ANYWHERE] * len(tokens),
        out_specs=[pl.BlockSpec((step, heads * DV), lambda i: (i, 0))] + saved_specs(shapes, index),
        out_shape=(jax.ShapeDtypeStruct((count, heads * DV), BF16),) + shapes,
        scratch_shapes=[
            pltpu.VMEM((step + 16, channels), F32),
            pltpu.VMEM((heads, DK, DV), F32),
        ],
        compiler_params=params(),
        cost_estimate=SMALL_COST,
        name="recurrence_forward",
    )(proj, proj, conv, cols, rows, logits, *tokens)


def backward_recurrence(proj, conv, cols, rows, logits, saved, out_grad, heads, tokens):
    count, channels = proj.shape
    step = BLOCK * PER_STEP
    last = count // step - 1
    index = lambda i: last - i
    return pl.pallas_call(
        functools.partial(backward_kernel, heads),
        grid=(count // step,),
        in_specs=common_specs(step, channels, 128, index)
        + saved_specs(saved, index)
        + [pl.BlockSpec((step, heads * DV), lambda i: (index(i), 0))]
        + [ANYWHERE] * len(tokens),
        out_specs=[
            pl.BlockSpec((step, channels + 256), lambda i: (index(i), 0)),
            pl.BlockSpec((8, channels), lambda i: (0, 0)),
        ],
        out_shape=(
            jax.ShapeDtypeStruct((count, channels + 256), BF16),
            jax.ShapeDtypeStruct((8, channels), F32),
        ),
        scratch_shapes=[
            pltpu.VMEM((step + 16, channels), F32),
            pltpu.VMEM((4, step + 8, channels), F32),
            pltpu.VMEM((heads, DK, DV), F32),
            pltpu.VMEM((3, 8, channels), F32),
        ],
        compiler_params=params(),
        cost_estimate=SMALL_COST,
        name="recurrence_backward",
    )(proj, proj, conv, cols, rows, logits, *saved, out_grad, *tokens)


def project_kernel(
    channels, chunks, handed, rank_ref, gain_ref, w_ref, col_ref, *refs
):
    x_refs = refs[:chunks]
    normed_ref, gate_ref, proj_ref, logit_ref, all_ref = refs[chunks + handed : chunks + handed + 5]
    rows_ref = refs[-1]
    step = pl.program_id(0)
    count = x_refs[0].shape[0]

    @pl.when(step == 0)
    def _():
        width = w_ref.shape[0] * w_ref.shape[2]
        for k in range(w_ref.shape[1]):
            place = pl.ds(pl.multiple_of((rank_ref[0] ^ k) * width, width), width)
            all_ref[place, :] = w_ref[:, k].reshape(width, w_ref.shape[3])

    for k in range(chunks):

        @pl.when(step == k)
        def _():
            x = x_refs[k][...].astype(F32)
            scale = lax.rsqrt(jnp.mean(x * x, axis=1, keepdims=True) + 1e-05)
            normed = (x * scale * gain_ref[...]).astype(BF16)
            normed_ref[...] = normed
            total = mm(normed, all_ref[...])
            gates = gate_ref.shape[1]
            gate_ref[...] = total[:, :gates]
            logit = total[:, gates + channels :]
            high = logit.astype(BF16)
            place = slice(k * count, (k + 1) * count)
            rows_ref[place, : channels + 128] = total[:, gates:].astype(BF16)
            rows_ref[place, channels + 128 :] = (logit - high.astype(F32)).astype(BF16)

    @pl.when(step >= chunks)
    def _():
        order = lax.broadcasted_iota(jnp.int32, (proj_ref.shape[0], rows_ref.shape[0]), 1)
        picked = (col_ref[:, 4:5].astype(jnp.int32) == order).astype(F32)
        packed = mm(picked, rows_ref[...])
        proj_ref[...] = packed[:, :channels].astype(BF16)
        logit_ref[...] = packed[:, channels : channels + 128] + packed[:, channels + 128 :]


def project(rank, x_chunks, gain, weights, cols, channels, passed, tokens):
    count, width = x_chunks[0].shape
    total = count * len(x_chunks)
    gates = weights.shape[3] - channels - 128
    chunks = total // count
    block = 256
    first = lambda i: jnp.minimum(i, chunks - 1)
    later = lambda i: jnp.maximum(i - chunks, 0)
    outs = pl.pallas_call(
        functools.partial(project_kernel, channels, chunks, len(passed) + len(tokens)),
        grid=(chunks + total // block,),
        in_specs=[
            SCALAR,
            pl.BlockSpec((1, width), lambda i: (0, 0)),
            pl.BlockSpec(weights.shape, lambda i: (0, 0, 0, 0)),
            pl.BlockSpec((block, 128), lambda i: (later(i), 0)),
        ]
        + [pl.BlockSpec((count, width), lambda i: (0, 0))] * chunks
        + [ANYWHERE] * (len(passed) + len(tokens)),
        out_specs=[
            pl.BlockSpec((count, width), lambda i: (first(i), 0)),
            pl.BlockSpec((count, gates), lambda i: (first(i), 0)),
            pl.BlockSpec((block, channels), lambda i: (later(i), 0)),
            pl.BlockSpec((block, 128), lambda i: (later(i), 0)),
            pl.BlockSpec((width, weights.shape[3]), lambda i: (0, 0)),
        ]
        + [ANYWHERE] * len(passed),
        out_shape=[
            jax.ShapeDtypeStruct((total, width), BF16),
            jax.ShapeDtypeStruct((total, gates), F32),
            jax.ShapeDtypeStruct((total, channels), BF16),
            jax.ShapeDtypeStruct((total, 128), F32),
            jax.ShapeDtypeStruct((width, weights.shape[3]), BF16),
        ]
        + [jax.ShapeDtypeStruct(p.shape, p.dtype) for p in passed],
        input_output_aliases={4 + chunks + i: 5 + i for i in range(len(passed))},
        scratch_shapes=[pltpu.VMEM((total, channels + 256), BF16)],
        compiler_params=params(),
        cost_estimate=SMALL_COST,
        name="project",
    )(rank, gain, weights, cols, *x_chunks, *passed, *tokens)
    return outs[:5], outs[5:]


def gate_kernel(heads, count, first, o_ref, place_ref, gate_ref, gain_ref, *refs):
    chunks = place_ref.shape[1] // count
    dealt_ref, chunk_refs = refs[first], refs[first + 1 : first + 1 + chunks]
    for k, chunk_ref in enumerate(chunk_refs):
        order = lax.broadcasted_iota(jnp.int32, (count, o_ref.shape[0]), 0) + k * count
        picked = (place_ref[...].astype(jnp.int32) == order).astype(F32)
        rows = mm(picked, o_ref[...])
        place = pl.ds(k * count, count)
        dealt_ref[place, :] = rows.astype(BF16)
        for h in range(heads):
            lanes = slice(h * DV, (h + 1) * DV)
            value = rows[:, lanes]
            scale = lax.rsqrt(jnp.mean(value * value, axis=1, keepdims=True) + 1e-05)
            gated = value * scale * gain_ref[...] * silu(gate_ref[place, lanes])
            chunk_ref[:, lanes] = gated.astype(BF16)


def gate_rows(output, place, gate_logit, gain, count, heads, passed, tokens):
    total, cols = output.shape
    chunks = total // count
    others = len(passed) + len(tokens)
    outs = pl.pallas_call(
        functools.partial(gate_kernel, heads, count, others),
        in_specs=[WHOLE] * 4 + [ANYWHERE] * others,
        out_specs=[WHOLE] * (chunks + 1) + [ANYWHERE] * len(passed),
        out_shape=[jax.ShapeDtypeStruct((total, cols), BF16)]
        + [jax.ShapeDtypeStruct((count, cols), BF16)] * chunks
        + [jax.ShapeDtypeStruct(a.shape, a.dtype) for a in passed],
        input_output_aliases={4 + i: 1 + chunks + i for i in range(len(passed))},
        compiler_params=pltpu.CompilerParams(vmem_limit_bytes=VMEM_BYTES),
        cost_estimate=SMALL_COST,
        name="gate_rows",
    )(output, place, gate_logit, gain, *passed, *tokens)
    return outs[0], outs[1 : 1 + chunks], outs[1 + chunks :]


def ungate_kernel(heads, chunks, outs, dealt_ref, col_ref, gate_ref, gain_ref, *refs):
    grad_refs = refs[:chunks]
    gate_grad_ref, o_grad_ref, gain_grad_ref, rows_ref = *refs[outs : outs + 3], refs[-1]
    count = grad_refs[0].shape[0]
    total = dealt_ref.shape[0]
    sums = jnp.zeros((1, DV), F32)
    for k in range(chunks):
        place = pl.ds(k * count, count)
        for h in range(heads):
            lanes = slice(h * DV, (h + 1) * DV)
            value = dealt_ref[place, lanes].astype(F32)
            grad = grad_refs[k][:, lanes].astype(F32)
            logit = gate_ref[place, lanes]
            scale = lax.rsqrt(jnp.mean(value * value, axis=1, keepdims=True) + 1e-05)
            unit = value * scale
            gate = jax.nn.sigmoid(logit)
            slid = logit * gate
            sums += jnp.sum(grad * unit * slid, axis=0, keepdims=True)
            grad = grad * gain_ref[...]
            slope = gate * (1.0 + logit * (1.0 - gate))
            gate_grad_ref[place, lanes] = (grad * unit * slope).astype(BF16)
            grad = grad * slid
            inner = jnp.mean(grad * unit, axis=1, keepdims=True)
            rows_ref[place, lanes] = (scale * (grad - unit * inner)).astype(BF16)
    gain_grad_ref[...] = sums
    for k in range(chunks):
        place = pl.ds(k * count, count)
        order = lax.broadcasted_iota(jnp.int32, (count, total), 1)
        picked = (col_ref[place, 4:5].astype(jnp.int32) == order).astype(F32)
        o_grad_ref[place, :] = mm(picked, rows_ref[...]).astype(BF16)


def ungate_rows(dealt_rows, cols, gate_logit, gain, grads, heads, passed, tokens):
    total, width = dealt_rows.shape
    whole = pl.BlockSpec(memory_space=pltpu.VMEM)
    first = 4 + len(grads)
    outs = pl.pallas_call(
        functools.partial(ungate_kernel, heads, len(grads), len(grads) + len(passed) + len(tokens)),
        in_specs=[whole] * first + [ANYWHERE] * (len(passed) + len(tokens)),
        out_specs=[whole] * 3 + [ANYWHERE] * len(passed),
        out_shape=[
            jax.ShapeDtypeStruct((total, width), BF16),
            jax.ShapeDtypeStruct((total, width), BF16),
            jax.ShapeDtypeStruct((1, DV), F32),
        ]
        + [jax.ShapeDtypeStruct(p.shape, p.dtype) for p in passed],
        input_output_aliases={first + i: 3 + i for i in range(len(passed))},
        scratch_shapes=[pltpu.VMEM((total, width), BF16)],
        compiler_params=pltpu.CompilerParams(vmem_limit_bytes=VMEM_BYTES),
        cost_estimate=SMALL_COST,
        name="ungate_rows",
    )(dealt_rows, cols, gate_logit, gain, *grads, *passed, *tokens)
    return outs[:3], list(outs[3:])


def put_rows(total, split, core_ref, refs):
    total = total.astype(BF16)
    if split is None:
        refs[0][...] = total
        return
    halves = total.reshape(*split, 2, -1, total.shape[1])
    for core in range(2):

        @pl.when(core_ref[0] == core)
        def _():
            refs[0][...] = halves[:, :, core]
            refs[1][...] = halves[:, :, 1 - core]


def row_outputs(split, width, cols, tile):
    if split is None:
        shape, block = (width, cols), (width, tile)
        spec = pl.BlockSpec(block, lambda i: (0, i))
        return [spec], [jax.ShapeDtypeStruct(shape, BF16)]
    shape = (*split, width // (2 * split[0] * split[1]))
    spec = pl.BlockSpec((*shape, tile), lambda i: (0, 0, 0, i))
    return [spec] * 2, [jax.ShapeDtypeStruct((*shape, cols), BF16)] * 2


def unpack_kernel(split, heads, words_ref, grad_ref, gates_ref, place_ref, normed_ref, w_ref, conv_ref, gain_ref, mid_ref, o_ref, *refs):
    count = 2 if split else 1
    dealt_ref, sums_ref = refs[-4 - count], refs[-3 - count]
    row_refs, small_ref, picked_ref = refs[-2 - count : -2], refs[-2], refs[-1]
    step = pl.program_id(0)
    total = grad_ref.shape[0]
    gates = gates_ref.shape[1]
    tile = dealt_ref.shape[1] // 2

    @pl.when(step == 0)
    def _():
        part = 256
        for k in range(total // part):
            order = lax.broadcasted_iota(jnp.int32, (part, total), 0) + k * part
            picked = (place_ref[...].astype(jnp.int32) == order).astype(F32)
            picked_ref[k * part : (k + 1) * part, :] = picked.astype(BF16)
        dealt_ref[:, :gates] = gates_ref[...]
        dealt_ref[:, gates:tile] = mm(picked_ref[...], grad_ref[:, : tile - gates]).astype(BF16)
        share = mm(normed_ref[...], dealt_ref[:, :tile])
        sums_ref[...] = jnp.sum(share * w_ref[:, :tile].astype(F32), axis=1, keepdims=True)
        put_rows(share, split, words_ref, row_refs)

    @pl.when(step == 1)
    def _():
        dealt_ref[:, tile:] = mm(picked_ref[...], grad_ref[:, tile - gates :]).astype(BF16)
        share = mm(normed_ref[...], dealt_ref[:, tile:])
        used = w_ref.shape[1] - tile
        weights = w_ref[:, tile:].astype(F32)
        sums_ref[...] += jnp.sum(share[:, :used] * weights, axis=1, keepdims=True)
        if split:
            devices, rows = 2 * split[0] * split[1], share.shape[0] // (2 * split[0] * split[1])
            gin = jnp.broadcast_to(sums_ref[...], (share.shape[0], 128)).T[:1] / gain_ref[...]
            small_ref[...] = jnp.zeros_like(small_ref)
            gin = jnp.concatenate([gin[:, j * 128 : (j + 1) * 128] for j in range(8)], 0)
            mid = jnp.concatenate([mid_ref[:, j * 128 : (j + 1) * 128] for j in range(8)], 0)
            for d in range(devices):
                small_ref[d * rows + 4 : d * rows + 5, :] = o_ref[:, :128]
                small_ref[d * rows + 5 : d * rows + 6, :] = o_ref[:, 128:]
                small_ref[d * rows + 8 : d * rows + 16, :] = mid
                small_ref[d * rows + 16 : d * rows + 24, :] = gin
            rank = words_ref[2]
            keys = heads * DK // 128
            vals = heads * DV // 128
            owners = [rank * keys + j for j in range(keys)]
            owners += [HEAD_COUNT * DK // 128 + rank * keys + j for j in range(keys)]
            owners += [2 * HEAD_COUNT * DK // 128 + rank * vals + j for j in range(vals)]
            for j, owner in enumerate(owners):
                place = pl.ds(pl.multiple_of(owner * rows, rows), 8)
                old = small_ref[place, :]
                taps = lax.broadcasted_iota(jnp.int32, (8, 128), 0) < 4
                small_ref[place, :] = jnp.where(taps, conv_ref[:, j * 128 : (j + 1) * 128], old)
            share = jnp.concatenate([share[:, :-128], small_ref[...]], 1)
        put_rows(share, split, words_ref, row_refs)


def unpack(split, words, grad, gate_grad, place, normed, weights, g_conv, gain, g_mid, g_o, heads, tokens):
    total = grad.shape[0]
    cols = grad.shape[1] + gate_grad.shape[1]
    width = normed.shape[0]
    operands = (grad, gate_grad, place, normed, weights, g_conv, gain, g_mid, g_o)
    specs, shapes = row_outputs(split, width, cols, cols // 2)
    return pl.pallas_call(
        functools.partial(unpack_kernel, split, heads),
        grid=(2,),
        in_specs=[SCALAR]
        + [pl.BlockSpec(a.shape, lambda i: (0, 0)) for a in operands]
        + [ANYWHERE] * len(tokens),
        out_specs=[
            pl.BlockSpec((total, cols), lambda i: (0, 0)),
            pl.BlockSpec((width, 1), lambda i: (0, 0)),
        ]
        + specs,
        out_shape=[
            jax.ShapeDtypeStruct((total, cols), BF16),
            jax.ShapeDtypeStruct((width, 1), F32),
        ]
        + shapes,
        scratch_shapes=[pltpu.VMEM((width, 128), F32), pltpu.VMEM((total, total), BF16)],
        compiler_params=params(),
        cost_estimate=SMALL_COST,
        name="unpack",
    )(words, *operands, *tokens)


def unproject_kernel(chunks, first, grad_ref, w_ref, *refs):
    part_refs, turned_ref = refs[first : first + chunks], refs[-1]
    step = pl.program_id(0)

    @pl.when(step == 0)
    def _():
        turned_ref[...] = w_ref[...].T

    part = mm(grad_ref[:, : turned_ref.shape[0]], turned_ref[...])
    for k in range(chunks):

        @pl.when(step == k)
        def _():
            part_refs[k][...] = part.astype(BF16)


def unproject(grad, weights, count, passed, tokens):
    total, cols = grad.shape
    width = weights.shape[0]
    chunks = total // count
    outs = pl.pallas_call(
        functools.partial(unproject_kernel, chunks, len(passed) + len(tokens)),
        grid=(chunks,),
        in_specs=[
            pl.BlockSpec((count, cols), lambda i: (i, 0)),
            pl.BlockSpec(weights.shape, lambda i: (0, 0)),
        ]
        + [ANYWHERE] * (len(passed) + len(tokens)),
        out_specs=[pl.BlockSpec((count, width), lambda i: (0, 0))] * chunks
        + [ANYWHERE] * len(passed),
        out_shape=[jax.ShapeDtypeStruct((count, width), BF16)] * chunks
        + [jax.ShapeDtypeStruct(p.shape, p.dtype) for p in passed],
        input_output_aliases={2 + i: chunks + i for i in range(len(passed))},
        scratch_shapes=[pltpu.VMEM(weights.shape[::-1], BF16)],
        compiler_params=params(),
        cost_estimate=SMALL_COST,
        name="unproject",
    )(grad, weights, *passed, *tokens)
    return list(outs[:chunks]), list(outs[chunks:])


def hand_kernel(*refs):
    refs[-1][...] = jnp.zeros_like(refs[-1])


def handed(passed, tokens):
    outs = pl.pallas_call(
        hand_kernel,
        in_specs=[ANYWHERE] * (len(passed) + len(tokens)),
        out_specs=[ANYWHERE] * len(passed) + [WHOLE],
        out_shape=[jax.ShapeDtypeStruct(p.shape, p.dtype) for p in passed]
        + [jax.ShapeDtypeStruct((8, 128), F32)],
        input_output_aliases={i: i for i in range(len(passed))},
        cost_estimate=SMALL_COST,
        name="handed",
    )(*passed, *tokens)
    return outs[:-1]


def weight_grad_kernel(split, tiles, sums, words_ref, *refs):
    row_refs = refs[-2:] if split else refs[-1:]
    step = pl.program_id(0)
    for tile, pairs in enumerate(tiles):

        @pl.when(step == tile)
        def _():
            total = mm_tn(refs[pairs[0][0]][...], refs[pairs[0][1]][...])
            for left, right in pairs[1:]:
                total += mm_tn(refs[left][...], refs[right][...])
            put_rows(total, split, words_ref, row_refs)
            if sums is not None and tile == 0:
                refs[sums[1]][...] = jnp.sum(total * refs[sums[0]][...].astype(F32), axis=1, keepdims=True)


def weight_grad(split, words, groups, tile, tokens, weights=None):
    width = groups[0][0][0].shape[1]
    operands, specs, tiles = [words], [SCALAR], []
    first = 0
    for lefts, rights in groups:
        count = rights[0].shape[1] // tile
        base = len(operands) - 1
        for left in lefts:
            operands.append(left)
            specs.append(pl.BlockSpec((rights[0].shape[0], width), lambda i: (0, 0)))
        for right in rights:
            operands.append(right)
            specs.append(
                pl.BlockSpec(
                    (right.shape[0], tile),
                    lambda i, first=first, count=count: (0, jnp.clip(i - first, 0, count - 1)),
                )
            )
        tiles += [[(base + k, base + len(lefts) + k) for k in range(len(lefts))]] * count
        first += count
    sums = None
    out_specs, out_shapes = row_outputs(split, width, first * tile, tile)
    if weights is not None:
        operands.append(weights)
        specs.append(pl.BlockSpec((width, tile), lambda i: (0, 0)))
        sums = (len(operands) - 2, len(operands) - 1 + len(tokens))
        out_specs = [pl.BlockSpec((width, 1), lambda i: (0, 0))] + out_specs
        out_shapes = [jax.ShapeDtypeStruct((width, 1), F32)] + out_shapes
    return pl.pallas_call(
        functools.partial(weight_grad_kernel, split, tiles, sums),
        grid=(first,),
        in_specs=specs + [ANYWHERE] * len(tokens),
        out_specs=out_specs,
        out_shape=out_shapes,
        compiler_params=params(),
        cost_estimate=SMALL_COST,
        name="weight_grad",
    )(*operands, *tokens)


def join_kernel(pairs, *refs):
    for chip in range(refs[0].shape[1]):
        place = 0
        for k in range(pairs):
            keep_ref, got_ref = refs[2 * k], refs[2 * k + 1]
            width = keep_ref.shape[3]
            total = keep_ref[:, chip].astype(F32) + got_ref[:, chip].astype(F32)
            refs[-1][chip, :, :, place : place + width] = total.astype(BF16)
            place += width


def joined(pairs, tokens):
    seq_count, chips, rows, _ = pairs[0][0].shape
    cols = sum(keep.shape[3] for keep, _ in pairs)
    return pl.pallas_call(
        functools.partial(join_kernel, len(pairs)),
        in_specs=[WHOLE] * (2 * len(pairs)) + [ANYWHERE] * len(tokens),
        out_specs=WHOLE,
        out_shape=jax.ShapeDtypeStruct((chips, seq_count, rows, cols), BF16),
        compiler_params=pltpu.CompilerParams(vmem_limit_bytes=VMEM_BYTES),
        cost_estimate=SMALL_COST,
        name="joined",
    )(*[a for pair in pairs for a in pair], *tokens)


def layer_kernel(chunks, w_ref, low_ref, *refs):
    weights = w_ref[...].T
    count = low_ref.shape[0]
    refs[chunks][...] = mm(refs[0][...], weights).astype(BF16)
    for k in range(1, chunks):
        refs[chunks + k][:count, :] = low_ref[...]
        refs[chunks + k][count:, :] = mm(refs[k][...], weights).astype(BF16)


def layer_products(hiddens, weights, low):
    count, wide = hiddens[0].shape
    width = weights.shape[0]
    chunks = len(hiddens)
    rows = [count] + [2 * count] * (chunks - 1)
    return pl.pallas_call(
        functools.partial(layer_kernel, chunks),
        grid=(1,),
        in_specs=[
            pl.BlockSpec((width, wide), lambda i: (0, weights.shape[1] // wide - 1)),
            pl.BlockSpec((count, width), lambda i: (0, 0)),
        ]
        + [pl.BlockSpec((count, wide), lambda i: (0, 0))] * chunks,
        out_specs=[pl.BlockSpec((r, width), lambda i: (0, 0)) for r in rows],
        out_shape=[jax.ShapeDtypeStruct((r, width), BF16) for r in rows],
        compiler_params=params(),
        cost_estimate=SMALL_COST,
        name="layer_products",
    )(weights, low, *hiddens)


def position_kernel(heads, chunks, words_ref, lengths_ref, order_ref, decay_ref, *refs):
    col_ref, row_ref, place_ref, cum_ref = refs[-4:]
    total = order_ref.shape[1]
    count = total // chunks
    blocks, near = total // BLOCK, count // BLOCK
    rank = words_ref[2]
    ends = [lengths_ref[0]]
    for e in range(1, lengths_ref.shape[0]):
        ends.append(ends[-1] + lengths_ref[e])

    def segment(position):
        found = jnp.zeros(position.shape, jnp.int32)
        for end in ends:
            found += (position >= end).astype(jnp.int32)
        return jnp.where(position < 0, -1, found)

    for k in range(chunks):
        for h in range(heads):
            for b in range(near):
                value = jnp.zeros((1, BLOCK), F32)
                for part in range(3):
                    row = (part * heads + h) * near + b
                    value += decay_ref[k, row : row + 1, :].astype(F32)
                cum_ref[pl.ds(h * blocks + (rank ^ k) * near + b, 1), :] = value
    rows, cols = masks()
    upper = (rows <= cols).astype(F32)
    cums = jnp.dot(
        cum_ref[...], upper, precision=lax.Precision.HIGHEST, preferred_element_type=F32
    )
    order = order_ref[...]
    chunk = jnp.zeros_like(order)
    for k in range(1, chunks):
        chunk += (order >= k * count).astype(jnp.int32)
    place = (order + ((chunk ^ rank) - chunk) * count).astype(F32)
    place_ref[...] = place
    row_ref[...] = jnp.zeros_like(row_ref)
    lane = lax.broadcasted_iota(jnp.int32, (1, BLOCK), 1)
    for b in range(blocks):
        position = lane + b * BLOCK
        here = segment(position)
        low, high = jnp.full((1, BLOCK), b * BLOCK - 1), jnp.full((1, BLOCK), b * BLOCK + BLOCK - 1)
        keep_in = (here == segment(low)).astype(F32)
        keep_out = (here == segment(high)).astype(F32)
        found = [(segment(position - 3 + tap) == here).astype(F32) for tap in range(3)]
        found += [here.astype(F32), place[:, b * BLOCK : (b + 1) * BLOCK]]
        mine = [cums[h * blocks + b : h * blocks + b + 1, :] for h in range(heads)]
        found += mine
        found += [jnp.exp(c) * keep_in for c in mine]
        found += [jnp.exp(c[:, BLOCK - 1 :] - c) * keep_out for c in mine]
        found.append(jnp.zeros((128 - len(found), BLOCK), F32))
        col_ref[b * BLOCK : (b + 1) * BLOCK, :] = jnp.concatenate(found, 0).T
        for h in range(heads):
            row_ref[h : h + 1, b * BLOCK : (b + 1) * BLOCK] = mine[h]
        row_ref[heads : heads + 1, b * BLOCK : (b + 1) * BLOCK] = here.astype(F32)


def positions(words, lengths, order, decays, heads, tokens):
    total = order.shape[1]
    return pl.pallas_call(
        functools.partial(position_kernel, heads, decays.shape[0]),
        in_specs=[SCALAR, SCALAR, WHOLE, WHOLE] + [ANYWHERE] * len(tokens),
        out_specs=[WHOLE] * 3,
        out_shape=(
            jax.ShapeDtypeStruct((total, 128), F32),
            jax.ShapeDtypeStruct((8, total), F32),
            jax.ShapeDtypeStruct((1, total), F32),
        ),
        scratch_shapes=[pltpu.VMEM((heads * total // BLOCK, BLOCK), F32)],
        cost_estimate=SMALL_COST,
        compiler_params=pltpu.CompilerParams(vmem_limit_bytes=VMEM_BYTES),
        name="positions",
    )(words, lengths, order, decays, *tokens)


def out_rows_kernel(others, words_ref, mine_ref, normed_ref, *refs):
    out_ref, turned_ref = refs[-2:]
    core, chip = words_ref[0], words_ref[1]
    if others:
        chunks, chips, rows, _ = mine_ref.shape
        for k in range(chunks):
            for j in range(chips):
                device = k * 2 * chips + 2 * (chip ^ j)
                for ref, side in ((mine_ref, core), (refs[0], 1 - core)):
                    place = pl.ds(pl.multiple_of((device + side) * rows, rows), rows)
                    out_ref[place, :] = ref[k, j]
    else:
        out_ref[...] = mine_ref[...]
    turned_ref[...] = normed_ref[...].T


def out_rows(words, mine, others, normed, rows, tokens):
    return pl.pallas_call(
        functools.partial(out_rows_kernel, len(others)),
        in_specs=[SCALAR] + [WHOLE] * (2 + len(others)) + [ANYWHERE] * len(tokens),
        out_specs=[WHOLE] * 2,
        out_shape=(
            jax.ShapeDtypeStruct((rows, mine.shape[-1]), BF16),
            jax.ShapeDtypeStruct(normed.shape[::-1], BF16),
        ),
        compiler_params=pltpu.CompilerParams(vmem_limit_bytes=VMEM_BYTES),
        cost_estimate=SMALL_COST,
        name="out_rows",
    )(words, mine, normed, *others, *tokens)


def ffn_rows_kernel(words_ref, ffn_ref, *refs):
    width = ffn_ref.shape[0] * ffn_ref.shape[2]
    for k in range(ffn_ref.shape[1]):
        place = pl.ds(pl.multiple_of((words_ref[2] ^ k) * width, width), width)
        refs[-1][place, :] = ffn_ref[:, k].reshape(width, ffn_ref.shape[3])


def ffn_rows(words, ffn, tokens):
    return pl.pallas_call(
        ffn_rows_kernel,
        in_specs=[SCALAR, WHOLE] + [ANYWHERE] * len(tokens),
        out_specs=WHOLE,
        out_shape=jax.ShapeDtypeStruct((ffn.shape[0] * ffn.shape[1] * ffn.shape[2], ffn.shape[3]), BF16),
        compiler_params=pltpu.CompilerParams(vmem_limit_bytes=VMEM_BYTES),
        cost_estimate=SMALL_COST,
        name="ffn_rows",
    )(words, ffn, *tokens)


def out_project_kernel(chunks, rank_ref, x_ref, gain_ref, w_ref, *refs):
    residual_ref, mid_ref, all_ref = refs[-3:]
    rank = rank_ref[0]
    for k in range(chunks):
        width = refs[k].shape[1]
        all_ref[:, pl.ds(pl.multiple_of((rank ^ k) * width, width), width)] = refs[k][...]
    residual = x_ref[...].astype(F32) + mm_nt(all_ref[...], w_ref[...])
    residual_ref[...] = residual
    scale = lax.rsqrt(jnp.mean(residual * residual, axis=1, keepdims=True) + 1e-05)
    mid_ref[...] = (residual * scale * gain_ref[...]).astype(BF16)


def out_project(rank, x, gain, attn, weights):
    count, width = x.shape
    return pl.pallas_call(
        functools.partial(out_project_kernel, len(attn)),
        in_specs=[SCALAR] + [WHOLE] * (3 + len(attn)),
        out_specs=[WHOLE] * 2,
        out_shape=(
            jax.ShapeDtypeStruct((count, width), F32),
            jax.ShapeDtypeStruct((count, width), BF16),
        ),
        scratch_shapes=[pltpu.VMEM((count, weights.shape[1]), BF16)],
        compiler_params=pltpu.CompilerParams(vmem_limit_bytes=VMEM_BYTES),
        cost_estimate=SMALL_COST,
        name="out_project",
    )(rank, x, gain, weights, *attn)


def mid_back_kernel(chunks, handed, rank_ref, grad_ref, residual_ref, gain_ref, w_ref, *refs):
    parts = refs[:chunks]
    outs, all_ref = refs[chunks + handed :], refs[-1]
    res_grad_ref, low_ref, gain_grad_ref, chunk_refs = outs[0], outs[1], outs[2], outs[3 : 3 + chunks]
    rank = rank_ref[0]
    mid_grad = parts[0][...].astype(F32)
    for k in range(1, chunks):
        mid_grad += parts[k][...].astype(F32)
    residual = residual_ref[...]
    scale = lax.rsqrt(jnp.mean(residual * residual, axis=1, keepdims=True) + 1e-05)
    unit = residual * scale
    gain_grad_ref[...] = jnp.sum(mid_grad * unit, axis=0, keepdims=True)
    scaled = mid_grad * gain_ref[...]
    inner = jnp.mean(scaled * unit, axis=1, keepdims=True)
    res_grad = grad_ref[...].astype(F32) + scale * (scaled - unit * inner)
    res_grad_ref[...] = res_grad
    low = res_grad.astype(BF16)
    low_ref[...] = low
    all_ref[...] = mm(low, w_ref[...]).astype(BF16)
    for k in range(chunks):
        width = chunk_refs[k].shape[1]
        chunk_refs[k][...] = all_ref[:, pl.ds(pl.multiple_of((rank ^ k) * width, width), width)]


def mid_back(rank, grad, residual, gain, parts, weights, passed):
    count, width = residual.shape
    chunks = len(parts)
    wide = weights.shape[1]
    first = 5 + chunks
    outs = pl.pallas_call(
        functools.partial(mid_back_kernel, chunks, len(passed)),
        in_specs=[SCALAR] + [WHOLE] * (first - 1) + [ANYWHERE] * len(passed),
        out_specs=[WHOLE] * (3 + chunks) + [ANYWHERE] * len(passed),
        out_shape=[
            jax.ShapeDtypeStruct((count, width), F32),
            jax.ShapeDtypeStruct((count, width), BF16),
            jax.ShapeDtypeStruct((1, width), F32),
        ]
        + [jax.ShapeDtypeStruct((count, wide // chunks), BF16)] * chunks
        + [jax.ShapeDtypeStruct(p.shape, p.dtype) for p in passed],
        input_output_aliases={first + i: 3 + chunks + i for i in range(len(passed))},
        scratch_shapes=[pltpu.VMEM((count, wide), BF16)],
        compiler_params=pltpu.CompilerParams(vmem_limit_bytes=VMEM_BYTES),
        cost_estimate=SMALL_COST,
        name="mid_back",
    )(rank, grad, residual, gain, weights, *parts, *passed)
    return (*outs[:3], outs[3 : 3 + chunks], list(outs[3 + chunks :]))


def in_back_kernel(chunks, x_ref, res_grad_ref, gain_ref, *refs):
    x = x_ref[...].astype(F32)
    grad = refs[0][...].astype(F32)
    for k in range(1, chunks):
        grad += refs[k][...].astype(F32)
    scale = lax.rsqrt(jnp.mean(x * x, axis=1, keepdims=True) + 1e-05)
    unit = x * scale
    scaled = grad * gain_ref[...]
    inner = jnp.mean(scaled * unit, axis=1, keepdims=True)
    refs[-1][...] = (res_grad_ref[...] + scale * (scaled - unit * inner)).astype(BF16)


def in_back(x, res_grad, gain, parts, tokens):
    return pl.pallas_call(
        functools.partial(in_back_kernel, len(parts)),
        in_specs=[WHOLE] * (3 + len(parts)) + [ANYWHERE] * len(tokens),
        out_specs=WHOLE,
        out_shape=jax.ShapeDtypeStruct(x.shape, BF16),
        compiler_params=pltpu.CompilerParams(vmem_limit_bytes=VMEM_BYTES),
        cost_estimate=SMALL_COST,
        name="in_back",
    )(x, res_grad, gain, *parts, *tokens)


def swapped(value, axis, mask):
    devices = lax.axis_size(axis)
    return lax.ppermute(value, axis, [(i, i ^ mask) for i in range(devices)])


def pinned(value, other):
    return value + 0 * other[:1, :1].astype(value.dtype)


def spread(value):
    return [value] + [swapped(value, "seq", k) for k in range(1, lax.axis_size("seq"))]


def returned(chunks):
    return [chunks[0]] + [swapped(chunks[k], "seq", k) for k in range(1, len(chunks))]


class RowSum:
    def __init__(self, outs):
        self.outs = list(outs)

    def pair(self):
        if len(self.outs) == 2:
            self.got = swapped(self.outs[1], "mp", 1)

    def join(self, *tokens):
        seq_count, mp_count = lax.axis_size("seq"), lax.axis_size("mp")
        if len(self.outs) == 1:
            (grad,) = self.outs
            cols = grad.shape[1]
            parts = grad.astype(F32).reshape(seq_count, mp_count, -1, cols).transpose(1, 0, 2, 3)
            own = lax.psum_scatter(parts.reshape(-1, cols), "mp", scatter_dimension=0, tiled=True)
            self.half = grad
            self.parts = own.reshape(1, seq_count, -1, cols)
            return
        self.half = joined([(self.outs[0], self.got)], tokens)
        self.between()

    def between(self):
        mp_count = lax.axis_size("mp")
        groups = [list(range(core, mp_count, 2)) for core in range(2)]
        self.parts = lax.all_to_all(self.half, "mp", 0, 0, axis_index_groups=groups, tiled=True)

    def beside(self, other):
        if len(self.outs) == 1:
            both = RowSum([jnp.concatenate([self.outs[0], other.outs[0]], 1)])
            both.join()
            return both
        both = RowSum([])
        both.half = joined([(s.outs[0], s.got) for s in (self, other)], [])
        both.between()
        return both


def row_sums(sums, tokens):
    groups = [part.parts for part in sums]
    shape = groups[0].shape[1:3]
    cols = [group.shape[3] for group in groups]

    def kernel(*refs):
        place = 0
        for ref, width in zip(refs, cols):
            total = ref[0].astype(F32)
            for k in range(1, ref.shape[0]):
                total += ref[k].astype(F32)
            refs[-1][:, :, place : place + width] = total.astype(BF16)
            place = place + width

    return pl.pallas_call(
        kernel,
        in_specs=[WHOLE] * len(groups) + [ANYWHERE] * len(tokens),
        out_specs=WHOLE,
        out_shape=jax.ShapeDtypeStruct(shape + (sum(cols),), BF16),
        cost_estimate=SMALL_COST,
        compiler_params=pltpu.CompilerParams(vmem_limit_bytes=VMEM_BYTES),
        name="row_sums",
    )(*groups, *tokens)


def dealt(own):
    return lax.all_to_all(own, "seq", 0, 0, tiled=True)


def left_product(left, right):
    return lax.dot_general(
        left, right, (((0,), (0,)), ((), ())), preferred_element_type=jnp.float32
    )


def right_product(left, right):
    return lax.dot_general(
        left, right, (((1,), (1,)), ((), ())), preferred_element_type=jnp.float32
    )


def dot(left, right):
    return jnp.dot(left, right, preferred_element_type=jnp.float32)


def silu_slope(values):
    gate = jax.nn.sigmoid(values)
    return gate * (1.0 + values * (1.0 - gate))


def split_three(values):
    high = values.astype(BF16)
    rest = values - high.astype(F32)
    middle = rest.astype(BF16)
    return jnp.stack([high, middle, (rest - middle.astype(F32)).astype(BF16)])


def body(
    layer_in,
    out_grad,
    seq_lengths,
    dealing,
    log_decay,
    w_qkv,
    w_out_gate,
    w_beta,
    conv_w,
    gain_in,
    gain_o,
    w_out,
    gain_mid,
    w_gate_up,
    w_down,
):
    seq_count, mp_count = lax.axis_size("seq"), lax.axis_size("mp")
    rank, place_mp = lax.axis_index("seq"), lax.axis_index("mp")
    count = layer_in.shape[1]
    rows = w_qkv.shape[0]
    heads = HEAD_COUNT // seq_count
    key_cols, val_cols = heads * DK, heads * DV
    half = w_down.shape[0] // seq_count
    wide = -(-half // 256) * 256
    taps = conv_w.shape[1]
    total = dealing.shape[1]
    devices = seq_count * mp_count
    channels = 2 * key_cols + val_cols
    all_keys, ffn = HEAD_COUNT * DK, w_down.shape[0]
    split = (seq_count, mp_count // 2) if mp_count <= 8 else None
    words = jnp.stack([place_mp % 2, place_mp // 2, rank]).astype(jnp.int32)
    rank_word = rank.astype(jnp.int32).reshape(1)

    small = jnp.concatenate([conv_w.T.reshape(-1), gain_in, gain_mid, gain_o])
    small_count = small.shape[0]
    spare = 128 - heads
    filler = jnp.concatenate([small, jnp.zeros((rows * spare - small_count,), BF16)])
    filler = filler.reshape(rows, spare)
    wide_filler = jnp.zeros((rows, wide - half), BF16)
    turned_down = w_down.T
    decay_lanes = -(-3 * heads * count // (128 * rows)) * 128
    decays = split_three(log_decay[0].T)
    mix_cols = channels + 128 + val_cols
    pieces, ffn_pieces = [], []
    for j in range(seq_count):
        own_decay = decays[:, j * heads : (j + 1) * heads].reshape(-1)
        own_decay = jnp.concatenate(
            [own_decay, jnp.zeros((rows * decay_lanes - own_decay.shape[0],), BF16)]
        )
        pieces.append(
            jnp.concatenate(
                [
                    w_out_gate[:, j * val_cols : (j + 1) * val_cols],
                    w_qkv[:, j * key_cols : (j + 1) * key_cols],
                    w_qkv[:, all_keys + j * key_cols : all_keys + (j + 1) * key_cols],
                    w_qkv[:, 2 * all_keys + j * val_cols : 2 * all_keys + (j + 1) * val_cols],
                    w_beta[:, j * heads : (j + 1) * heads],
                    filler,
                    own_decay.reshape(rows, decay_lanes),
                ],
                1,
            )
        )
        ffn_pieces.append(
            jnp.concatenate(
                [
                    w_gate_up[:, j * half : (j + 1) * half],
                    wide_filler,
                    w_gate_up[:, ffn + j * half : ffn + (j + 1) * half],
                    wide_filler,
                    turned_down[:, j * half : (j + 1) * half],
                    wide_filler,
                ],
                1,
            )
        )
    def near(arrays):
        arrays = jnp.stack(arrays)
        return jnp.stack(
            returned(
                [lax.dynamic_index_in_dim(arrays, rank ^ k, 0, keepdims=False) for k in range(seq_count)]
            )
        )

    pieces = near([jnp.concatenate(p, 1) for p in zip(pieces, ffn_pieces)])
    ffn_pieces = pieces[:, :, -3 * wide :]
    gathered = lax.all_gather(pieces[:, :, :mix_cols], "mp", axis=0, tiled=False)
    chunks_in = spread(layer_in[0] + 0 * pieces[1, :1, :1])

    relative = rank ^ jnp.arange(seq_count)
    smalls = gathered[:, :, :, mix_cols - spare :].transpose(1, 0, 2, 3)
    smalls = jnp.take(smalls, relative, axis=0).reshape(devices, -1)[:, :small_count]
    own_taps = conv_w.shape[0] * taps
    full_conv = smalls[:, :own_taps].reshape(-1, taps, conv_w.shape[0]).transpose(1, 0, 2)
    full_conv = full_conv.reshape(taps, -1).astype(F32)
    conv = jnp.concatenate(
        [
            lax.dynamic_slice_in_dim(full_conv, rank * key_cols, key_cols, 1),
            lax.dynamic_slice_in_dim(full_conv, all_keys + rank * key_cols, key_cols, 1),
            lax.dynamic_slice_in_dim(full_conv, 2 * all_keys + rank * val_cols, val_cols, 1),
        ],
        1,
    )
    conv = jnp.concatenate([conv, jnp.zeros((8 - taps, channels), F32)], 0)
    gains = smalls[:, own_taps:].astype(F32)
    full_gin = gains[:, :rows].reshape(1, -1)
    full_gmid = gains[:, rows : 2 * rows].reshape(1, -1)
    full_go = gains[:, 2 * rows :].reshape(1, -1)

    out_turned = w_out.T
    out_near = []
    if split:
        out_near = [out_turned] + [swapped(out_turned, "mp", 2 * j) for j in range(1, mp_count // 2)]

    decays = pieces[:, :, mix_cols : -3 * wide].reshape(seq_count, -1)[:, : 3 * heads * count]
    col_info, row_info, place_row = positions(
        words, seq_lengths[0], dealing, decays.reshape(seq_count, -1, BLOCK), heads, out_near[1:]
    )

    passed = [ffn_pieces, out_grad[0] + 0 * pieces[1, :1, :1]]
    if split:
        passed.append(jnp.broadcast_to(jnp.stack(out_near), (seq_count, mp_count // 2, *out_turned.shape)))
    passed = handed(passed, chunks_in[1:] + [row_info])
    ffn_all = lax.all_gather(passed[0], "mp", axis=0, tiled=False)
    chunks_grad = spread(passed[1])
    out_mine = [lax.all_to_all(passed[2], "seq", 0, 0, tiled=True)] if split else []
    (normed, gate_logit, proj, logit_parts, mix), _ = project(
        rank_word, chunks_in, full_gin, gathered, col_info, channels,
        [], [conv, full_go, full_gmid],
    )
    outs = forward_recurrence(proj, conv, col_info, row_info, logit_parts, heads, [])
    dealt_rows, attn, out_mine = gate_rows(
        outs[0], place_row, gate_logit, full_go, count, heads, out_mine, chunks_grad[1:]
    )
    if split:
        out_others = [swapped(out_mine[0], "mp", 1)]
    else:
        out_mine, out_others = [lax.all_gather(out_turned, ("seq", "mp"), axis=0, tiled=True)], []
    attn_parts = returned(attn)
    out_w, normed_t = out_rows(words, out_mine[0], out_others, normed, devices * rows, [attn[0]])

    residual, mid_own = out_project(rank_word, layer_in[0], full_gmid, attn_parts, out_w)

    ffn_w = ffn_rows(words, ffn_all, [mid_own])
    w_gu, down_turned = ffn_w[:, : 2 * wide], ffn_w[:, 2 * wide :]
    mids = spread(mid_own)
    hiddens, gu_grads, mid_parts = ([None] * seq_count for _ in range(3))
    last_part = None
    for k in (0, 1, 3, 2):
        mid_k = mids[k] if last_part is None else pinned(mids[k], last_part)
        gate_up = dot(mid_k, w_gu)
        gate, up = gate_up[:, :wide], gate_up[:, wide:]
        hiddens[k] = (silu(gate) * up).astype(BF16)
        hidden_grad = dot(chunks_grad[k], down_turned)
        gu_grads[k] = jnp.concatenate(
            [hidden_grad * up * silu_slope(gate), hidden_grad * silu(gate)], 1
        ).astype(BF16)
        mid_parts[k] = last_part = right_product(gu_grads[k], w_gu).astype(BF16)
    mid_parts = returned(mid_parts)
    ffn_sum = RowSum(
        weight_grad(
            split, words, [(mids, gu_grads), (chunks_grad, hiddens)], wide, [last_part, mid_parts[1]]
        ),
    )
    res_grad, out_proj_grad, g_mid, attn_grads, ffn_sum.outs[-1:] = mid_back(
        rank_word, out_grad[0], residual, full_gmid, mid_parts, out_w, ffn_sum.outs[-1:]
    )
    attn_grads = returned(attn_grads)
    ffn_sum.pair()
    layer_own, *both = layer_products(hiddens, ffn_w, out_proj_grad)

    (gate_grad, o_grad, g_go), both = ungate_rows(
        dealt_rows, col_info, gate_logit, full_go, attn_grads, heads, both, []
    )
    ffn_sum.join(gate_grad)
    both = returned([None] + both)[1:]
    proj_grad, g_conv = backward_recurrence(
        proj, conv, col_info, row_info, logit_parts, outs[1:], o_grad, heads, [ffn_sum.half]
    )
    mix_grad, mix_sums, *mix_outs = unpack(
        split, words, proj_grad, gate_grad, place_row, normed_t, mix, g_conv, full_gin, g_mid, g_go,
        heads, [],
    )
    mix_sum = RowSum(mix_outs)
    mix_sum.pair()
    out_sum = RowSum(
        weight_grad(split, words, [([out_proj_grad] + both, attn)], val_cols, [mix_grad])
    )
    out_sum.pair()
    last_sum = mix_sum.beside(out_sum)
    normed_parts, _ = unproject(mix_grad, mix, count, [], [last_sum.half])
    normed_chunks = returned(normed_parts)
    in_grad = in_back(layer_in[0], res_grad, full_gin, normed_chunks, [])
    layer_out = residual + sum(
        c.astype(F32) for c in [layer_own] + [b[count:] for b in both]
    )
    all_pieces = dealt(row_sums([ffn_sum, last_sum], [in_grad]))
    ffn_pieces, all_pieces = all_pieces[:, :, : 3 * wide], all_pieces[:, :, 3 * wide :]
    gate_pieces, mix_pieces = all_pieces[:, :, :val_cols], all_pieces[:, :, val_cols:-val_cols]
    out_pieces = all_pieces[:, :, -val_cols:]

    def columns(pieces, first, width):
        parts = [pieces[j, :, first : first + width] for j in range(seq_count)]
        return jnp.concatenate(parts, 1).astype(F32)

    if split:
        small_sum = jnp.sum(mix_pieces[:, :, channels + 128 :].astype(F32), axis=0)
        device = rank * mp_count + place_mp
        grad_conv = small_sum[:taps].T
        grad_go = lax.dynamic_slice_in_dim(
            small_sum[4:6].reshape(-1), device * gain_o.shape[0], gain_o.shape[0]
        )
        grad_gmid = lax.dynamic_slice_in_dim(small_sum[8:16].reshape(-1), device * rows, rows)
        grad_gin = lax.dynamic_slice_in_dim(small_sum[16:24].reshape(-1), device * rows, rows)
    else:
        everywhere = ("seq", "mp")
        conv_full = jnp.zeros((taps, conv_w.shape[0] * devices), F32)
        for first, width in ((0, key_cols), (key_cols, key_cols), (2 * key_cols, val_cols)):
            conv_full = lax.dynamic_update_slice_in_dim(
                conv_full,
                g_conv[:taps, first : first + width],
                first * seq_count + rank * width,
                1,
            )
        grad_conv = lax.psum_scatter(conv_full.T, everywhere, scatter_dimension=0, tiled=True)
        g_gin = mix_sums[:, 0] / full_gin[0]
        grad_gin, grad_gmid, grad_go = (
            lax.psum_scatter(g, everywhere, scatter_dimension=0, tiled=True)
            for g in (g_gin, g_mid[0], g_go[0])
        )
    grad_qkv = jnp.concatenate(
        [
            columns(mix_pieces, 0, key_cols),
            columns(mix_pieces, key_cols, key_cols),
            columns(mix_pieces, 2 * key_cols, val_cols),
        ],
        1,
    )
    return (
        layer_out.astype(BF16)[None],
        in_grad[None],
        grad_qkv,
        columns(gate_pieces, 0, val_cols),
        columns(mix_pieces, channels, heads),
        grad_conv,
        grad_gin,
        grad_go,
        columns(out_pieces, 0, val_cols).T,
        grad_gmid,
        jnp.concatenate([columns(ffn_pieces, 0, half), columns(ffn_pieces, wide, half)], 1),
        columns(ffn_pieces, 2 * wide, half).T,
    )


def solution(mesh):
    in_specs = (
        P("mp", "seq", None),
        P("mp", "seq", None),
        P("mp", None),
        P("mp", None),
        P("mp", "seq", None),
        P(("seq", "mp"), None),
        P(("seq", "mp"), None),
        P(("seq", "mp"), None),
        P(("seq", "mp"), None),
        P(("seq", "mp")),
        P(("seq", "mp")),
        P(None, ("seq", "mp")),
        P(("seq", "mp")),
        P(("seq", "mp"), None),
        P(None, ("seq", "mp")),
    )
    out_specs = (
        P("mp", "seq", None),
        P("mp", "seq", None),
        P(("seq", "mp"), None),
        P(("seq", "mp"), None),
        P(("seq", "mp"), None),
        P(("seq", "mp"), None),
        P(("seq", "mp")),
        P(("seq", "mp")),
        P(None, ("seq", "mp")),
        P(("seq", "mp")),
        P(("seq", "mp"), None),
        P(None, ("seq", "mp")),
    )
    return jax.shard_map(body, mesh=mesh, in_specs=in_specs, out_specs=out_specs, check_vma=False)
```

time: 568 us -> 496 us (0.87); the launches traced: 558 us -> 492 us
  local copies, waits for them, and re-layouts: 72.2 us -> 35.3 us
  Pallas kernels: 187 us -> 214 us
  starting transfers between devices: 69.1 us -> 55 us
  matrix products: 38.2 us -> 24.6 us
  other arithmetic: 32.9 us -> 19.8 us
  blocking collectives: 12.3 us -> 0 us
  waiting for transfers between devices: 131 us -> 125 us
    pallas_call x15 -> x17, Pallas kernels: 117 us -> 144 us  [the longest x1 23.5 us: unpack(): pl.pallas_call(functools.partial(unpack_kernel, split, heads), grid=(2,),...]
    ppermute x52 -> x34, starting transfers between devices: 62 us -> 36.7 us  [swapped(): return lax.ppermute(value, axis, [(i, i ^ mask) for i in range(devices)])]
    ppermute x52 -> x34, waiting for transfers between devices: 130 us -> 114 us  [swapped(): return lax.ppermute(value, axis, [(i, i ^ mask) for i in range(devices)])]
    dot_general x8 -> x4, matrix products: 19 us -> 5.72 us  [right_product(): lax.dot_general(left, right, (((1,), (1,)), ((), ())), preferred_element_...]
    all_to_all x1 -> x0, blocking collectives: 12.3 us -> none  [gathered_rows(): own = lax.all_to_all(pieces, 'seq', 0, 0, tiled=True)]
    convert_element_type x14 -> x2, other arithmetic: 12.6 us -> 1.32 us  [columns(): return jnp.concatenate(parts, 1).astype(F32)]
    all_to_all x2 -> x4, starting transfers between devices: 6.95 us -> 18.2 us  [the longest x2 10.6 us: between(): lax.all_to_all(self.half, 'mp', 0, 0, axis_index_groups=groups, tiled=True)]
    all_to_all x2 -> x4, waiting for transfers between devices: 0.01 us -> 11.1 us  [the longest x1 11.1 us: dealt(): return lax.all_to_all(own, 'seq', 0, 0, tiled=True)]
  transfers between devices with their start and end apart: 57 -> 40, of which waited for: 19 -> 16; matrix products, arithmetic and copies ran while one was open for 23% -> 10% of each run, Pallas kernels for 34% -> 40%
where the time goes in v2:
time: 496 us; the launch traced here: 492 us
  Pallas kernels  214 us (43%)
  waiting for transfers between devices  125 us (25%)
  starting transfers between devices  55 us (11%)
  local copies, waits for them, and re-layouts  35.3 us (7%)
  matrix products  24.6 us (5%)
  other arithmetic  19.8 us (4%)
  between operations  17.7 us (4%)
    ppermute x34, waiting for transfers between devices, swapped(): return lax.ppermute(value, axis, [(i, i ^ mask) for i in range(devices)])  114 us
    pallas_call x1, Pallas kernels, backward_recurrence(): pl.pallas_call(functools.partial(backward_kernel, heads), grid=(count //...  41.8 us
    ppermute x34, starting transfers between devices, swapped(): return lax.ppermute(value, axis, [(i, i ^ mask) for i in range(devices)])  36.7 us
    pallas_call x1, Pallas kernels, forward_recurrence(): pl.pallas_call(functools.partial(forward_kernel, heads), grid=(count // s...  24 us
    pallas_call x1, Pallas kernels, unpack(): pl.pallas_call(functools.partial(unpack_kernel, split, heads), grid=(2,),...  23.5 us
    pallas_call x2, Pallas kernels, weight_grad(): pl.pallas_call(functools.partial(weight_grad_kernel, split, tiles, sums),...  23 us
    pallas_call x1, Pallas kernels, project(): pl.pallas_call(functools.partial(project_kernel, channels, chunks, len(pa...  21.5 us
    dot_general x8, matrix products, dot(): return jnp.dot(left, right, preferred_element_type=jnp.float32)  18.9 us
  transfers between devices with their start and end apart: 40, of which 16 were waited for; matrix products, arithmetic and copies ran while one was open for 10% of the time, Pallas kernels for 40%

profile of v2, /device:TPU:0, one launch (start us, length us, event | category | flops | bytes accessed | tf_op | source)
XLA Modules:
  0.0 491.9 jit_solution(5301163111423876201)
XLA Ops:
  10.5 2.8 concatenate.80
  16.7 3.0 collective-permute-start
  21.2 5.6 %collective-permute-done = bf16[32,4096]{1,0:T(8,128)(2,1)S(1)} collective-permute-done((bf16[32,4096]{1,0:T(8,128)(2,1)S(1)}, bf16[32,4096]{1,0:T(8,128)(2,1)S(1)}, u32[]{:S(2)}, u32[]{:S(2)}) %collective-permute-start) | collective-permute-done | bytes 262176 | tf_op jit(solution)/shard_map/ppermute | solution.py:1054
  26.8 6.2 %collective-permute-done.1 = bf16[32,4096]{1,0:T(8,128)(2,1)S(1)} collective-permute-done((bf16[32,4096]{1,0:T(8,128)(2,1)S(1)}, bf16[32,4096]{1,0:T(8,128)(2,1)S(1)}, u32[]{:S(2)}, u32[]{:S(2)}) %collective-permute-start.1) | collective-permute-done | bytes 262176 | tf_op jit(solution)/shard_map/ppermute | solution.py:1054
  41.4 2.6 collective-permute-start.4
  44.8 16.2 %collective-permute-done.4.refs_1_ = bf16[32,2048]{1,0:T(8,128)(2,1)S(1)} collective-permute-done((bf16[32,2048]{1,0:T(8,128)(2,1)}, bf16[32,2048]{1,0:T(8,128)(2,1)S(1)}, u32[]{:S(2)}, u32[]{:S(2)}) %collective-permute-start.4) | collective-permute-done | bytes 131104 | tf_op jit(solution)/shard_map/ppermute | solution.py:1054
  65.9 2.2 positions.1
  69.1 5.0 %collective-permute-done.7.refs_2_.refs_4_ = bf16[384,1024]{1,0:T(8,128)(2,1)S(1)} collective-permute-done((bf16[384,1024]{1,0:T(8,128)(2,1)}, bf16[384,1024]{1,0:T(8,128)(2,1)S(1)}, u32[]{:S(2)}, u32[]{:S(2)}) %collective-permute-start.7) | collective-permute-done | bytes 786464 | tf_op jit(solution)/shard_map/ppermute | solution.py:1054
  80.0 3.9 all-to-all-start
  89.0 21.5 %project.1 = (bf16[1536,1024]{1,0:T(8,128)(2,1)}, f32[1536,512]{1,0:T(8,128)}, bf16[1536,1024]{1,0:T(8,128)(2,1)}, f32[1536,128]{1,0:T(8,128)}, bf16[1024,1664]{1,0:T(8,128)(2,1)}) custom-call(s32[1]{0:T(128)} %bitcast.rank_ref, f32[1,1024]{1,0:T(1,128)} %reshape.126.gain_ref, bf16[8,4,32,1664]{3,2,1,0:T(8,128)(2,1)} %bitcast.210, ...), custom_call_target="tpu_custom_call" | custom-call | flops 1000000 | bytes 1000000 | tf_op jit(solution)/shard_map/project/pallas_call | solution.py:422
  110.5 24.0 %recurrence_forward.1 = (bf16[1536,512]{1,0:T(8,128)(2,1)}, bf16[12,2,128,256]{3,2,1,0:T(8,128)(2,1)}, bf16[12,2,128,256]{3,2,1,0:T(8,128)(2,1)}, bf16[12,2,128,...) custom-call(bf16[1536,1024]{1,0:T(8,128)(2,1)} %get-tuple-element.71.edge_ref.proj_ref, ...), custom_call_target="tpu_custom_call" | custom-call | flops 1000000 | bytes 1000000 | tf_op jit(solution)/shard_map/recurrence_forward/pallas_call | solution.py:324
  136.1 6.7 %gate_rows.1 = (bf16[1536,512]{1,0:T(8,128)(2,1)}, bf16[384,512]{1,0:T(8,128)(2,1)}, bf16[384,512]{1,0:T(8,128)(2,1)}, bf16[384,512]{1,0:T(8,128)(2,1)}, bf16[38...) custom-call(bf16[1536,512]{1,0:T(8,128)(2,1)} %get-tuple-element.74.o_ref, ...), custom_call_target="tpu_custom_call", output_to_operand_aliasing={{5}: (4, {})} | custom-call | flops 1000000 | bytes 1000000 | tf_op jit(solution)/shard_map/gate_rows/pallas_call | solution.py:479
  142.8 2.0 collective-permute-start.13
  148.5 7.1 %out_rows.1 = (bf16[1024,2048]{1,0:T(8,128)(2,1)}, bf16[1024,1536]{1,0:T(8,128)(2,1)}) custom-call(s32[3]{0:T(128)} %pad_add_fusion.words_ref, bf16[4,4,32,2048]{3,2,1,0:T(8,128)(2,1)} %get-tuple-element.79.mine_ref, bf16[1536,1024]{1,0:T(8,128)(2,1)} %get-tuple-element.80.normed_ref, bf16[4,4,32,2048]{3,2,1,0:T(8,128)(2,1)} %copy-done.19, ...), custom_call_target="tpu_custom_call" | custom-call | flops 1000000 | bytes 1000000 | tf_op jit(solution)/shard_map/out_rows/pallas_call | solution.py:917
  155.7 9.0 %collective-permute-done.14.refs_2_ = bf16[384,512]{1,0:T(8,128)(2,1)S(1)} collective-permute-done((bf16[384,512]{1,0:T(8,128)(2,1)}, bf16[384,512]{1,0:T(8,128)(2,1)S(1)}, u32[]{:S(2)}, u32[]{:S(2)}) %collective-permute-start.14) | collective-permute-done | bytes 393248 | tf_op jit(solution)/shard_map/ppermute | solution.py:1054
  165.6 6.2 %out_project.1 = (f32[384,1024]{1,0:T(8,128)}, bf16[384,1024]{1,0:T(8,128)(2,1)}) custom-call(s32[1]{0:T(128)} %bitcast.rank_ref, bf16[384,1024]{1,0:T(8,128)(2,1)} %bitcast.206, f32[1,1024]{1,0:T(1,128)} %reshape.125.refs_6_.gain_ref, bf16[1024,2048]{1,0:T(8,128)(2,1)} %get-tuple-element.82.w_ref, ...), custom_call_target="tpu_custom_call" | custom-call | flops 1000000 | bytes 1000000 | tf_op jit(solution)/shard_map/out_project/pallas_call | solution.py:964
  172.8 1.9 collective-permute-start.19
  175.3 4.8 ffn_rows.1.w_ref
  180.1 3.4 fusion.26
  183.6 1.9 multiply_convert_fusion.11
  188.1 4.3 collective-permute-done.16.refs_1_
  193.9 3.1 multiply_convert_fusion.9
  200.5 9.7 %collective-permute-done.19.refs_3_ = bf16[384,1024]{1,0:T(8,128)(2,1)S(1)} collective-permute-done((bf16[384,1024]{1,0:T(8,128)(2,1)}, bf16[384,1024]{1,0:T(8,128)(2,1)S(1)}, u32[]{:S(2)}, u32[]{:S(2)}) %collective-permute-start.19) | collective-permute-done | bytes 786464 | tf_op jit(solution)/shard_map/ppermute | solution.py:1054
  211.8 3.0 multiply_convert_fusion.7
  219.6 2.6 fusion.13
  222.2 1.9 multiply_convert_fusion.5
  230.9 17.3 %weight_grad.2 = (bf16[4,4,32,2304]{3,2,1,0:T(8,128)(2,1)}, bf16[4,4,32,2304]{3,2,1,0:T(8,128)(2,1)}) custom-call(s32[3]{0:T(128)} %pad_add_fusion.words_ref, bf16[384,1024]{1,0:T(8,128)(2,1)} %get-tuple-element.88.refs_0_, bf16[384,1024]{1,0:T(8,128)(2,1)} %copy-done.23, bf16[384,1024]{1,0:T(8,128)(2,1)} %collective-permute-done.18.refs_2_, ...), custom_call_target="tpu_custom_call" | custom-call | flops 1000000 | bytes 1000000 | tf_op jit(solution)/shard_map/weight_grad/pallas_call | solution.py:759
  248.2 10.2 %collective-permute-done.20.refs_2_ = bf16[384,1024]{1,0:T(8,128)(2,1)S(1)} collective-permute-done((bf16[384,1024]{1,0:T(8,128)(2,1)S(1)}, bf16[384,1024]{1,0:T(8,128)(2,1)S(1)}, u32[]{:S(2)}, u32[]{:S(2)}) %collective-permute-start.20) | collective-permute-done | bytes 786464 | tf_op jit(solution)/shard_map/ppermute | solution.py:1054
  259.5 7.7 %mid_back.1 = (f32[384,1024]{1,0:T(8,128)}, bf16[384,1024]{1,0:T(8,128)(2,1)}, f32[1,1024]{1,0:T(1,128)}, bf16[384,512]{1,0:T(8,128)(2,1)}, bf16[384,512]{1,0:T(...) custom-call(s32[1]{0:T(128)} %bitcast.rank_ref, ...), custom_call_target="tpu_custom_call", output_to_operand_aliasing={{7}: (9, {})} | custom-call | flops 1000000 | bytes 1000000 | tf_op jit(solution)/shard_map/mid_back/pallas_call | solution.py:1008
  270.7 7.1 %layer_products.1 = (bf16[384,1024]{1,0:T(8,128)(2,1)}, bf16[768,1024]{1,0:T(8,128)(2,1)}, bf16[768,1024]{1,0:T(8,128)(2,1)}, bf16[768,1024]{1,0:T(8,128)(2,1)}) custom-call(bf16[1024,2304]{1,0:T(8,128)(2,1)} %ffn_rows.1.w_ref, bf16[384,1024]{1,0:T(8,128)(2,1)} %get-tuple-element.90.low_ref.refs_0_, bf16[384,768]{1,0:T(8,128)(2,1)} %get-tuple-element.139.refs_12_.refs_0_, ...), custom_call_target="tpu_custom_call" | custom-call | flops 1000000 | bytes 1000000 | tf_op jit(solution)/shard_map/layer_products/pallas_call | solution.py:810
  279.4 8.0 %collective-permute-done.23.refs_2_ = bf16[384,512]{1,0:T(8,128)(2,1)S(1)} collective-permute-done((bf16[384,512]{1,0:T(8,128)(2,1)}, bf16[384,512]{1,0:T(8,128)(2,1)S(1)}, u32[]{:S(2)}, u32[]{:S(2)}) %collective-permute-start.23) | collective-permute-done | bytes 393248 | tf_op jit(solution)/shard_map/ppermute | solution.py:1054
  288.3 9.2 %ungate_rows.1 = (bf16[1536,512]{1,0:T(8,128)(2,1)}, bf16[1536,512]{1,0:T(8,128)(2,1)}, f32[1,256]{1,0:T(1,128)}, bf16[768,1024]{1,0:T(8,128)(2,1)}, bf16[768,10...) custom-call(bf16[1536,512]{1,0:T(8,128)(2,1)} %get-tuple-element.92.dealt_r, ...), custom_call_target="tpu_custom_call", output_to_operand_aliasing={{3}: (8, {}), {4}: (9, {}), {5}: (10, {})} | custom-call | flops 1000000 | bytes 1000000 | tf_op jit(solution)/shard_map/ungate_rows/pallas_call | solution.py:530
  298.9 4.3 joined.2.refs_0_
  303.3 5.8 %all-to-all-start.1 = ((bf16[4,4,32,2304]{3,2,1,0:T(8,128)(2,1)}), bf16[4,4,32,2304]{3,2,1,0:T(8,128)(2,1)S(1)}, u32[]{:S(2)}, u32[]{:S(2)}) async-start(bf16[4,4,32,2304]{3,2,1,0:T(8,128)(2,1)} %joined.2.refs_0_), calls=%async_computation.1 | async-start | bytes 4718592 | tf_op jit(solution)/shard_map/all_to_all | solution.py:1093
  312.5 41.8 %recurrence_backward.1 = (bf16[1536,1280]{1,0:T(8,128)(2,1)}, f32[8,1024]{1,0:T(8,128)}) custom-call(bf16[1536,1024]{1,0:T(8,128)(2,1)} %get-tuple-element.71.edge_ref.proj_ref, bf16[1536,1024]{1,0:T(8,128)(2,1)} %get-tuple-element.71.edge_ref.proj_ref, f32[8,1024]{1,0:T(8,128)} %select_maximum_fusion.refs_4_.conv_ref, ...), custom_call_target="tpu_custom_call" | custom-call | flops 1000000 | bytes 1000000 | tf_op jit(solution)/shard_map/recurrence_backward/pallas_call | solution.py:345
  354.3 23.5 %unpack.1 = (bf16[1536,1792]{1,0:T(8,128)(2,1)}, f32[1024,1]{1,0:T(8,128)}, bf16[4,4,32,1792]{3,2,1,0:T(8,128)(2,1)}, bf16[4,4,32,1792]{3,2,1,0:T(8,128)(2,1)}) custom-call(s32[3]{0:T(128)} %pad_add_fusion.words_ref, bf16[1536,1280]{1,0:T(8,128)(2,1)} %get-tuple-element.113.grad_ref, bf16[1536,512]{1,0:T(8,128)(2,1)} %get-tuple-element.112.refs_2_.gates_ref, ...), custom_call_target="tpu_custom_call" | custom-call | flops 1000000 | bytes 1000000 | tf_op jit(solution)/shard_map/unpack/pallas_call | solution.py:634
  381.4 5.7 %weight_grad.3 = (bf16[4,4,32,512]{3,2,1,0:T(8,128)(2,1)}, bf16[4,4,32,512]{3,2,1,0:T(8,128)(2,1)}) custom-call(s32[3]{0:T(128)} %pad_add_fusion.words_ref, bf16[384,1024]{1,0:T(8,128)(2,1)} %get-tuple-element.90.low_ref.refs_0_, bf16[768,1024]{1,0:T(8,128)(2,1)} %copy-done.6, bf16[768,1024]{1,0:T(8,128)(2,1)} %copy-done.7, bf16[768,1024]{1,0:T(8,128)(2,1)} %copy-done.8, ...), custom_call_target="tpu_custom_call" | custom-call | flops 1000000 | bytes 1000000 | tf_op jit(solution)/shard_map/weight_grad/pallas_call | solution.py:759
  387.1 2.1 collective-permute-done.30.refs_3_
  390.1 4.3 joined.3.refs_0_
  395.7 4.8 all-to-all-start.2
  400.5 11.8 %unproject.1 = (bf16[384,1024]{1,0:T(8,128)(2,1)}, bf16[384,1024]{1,0:T(8,128)(2,1)}, bf16[384,1024]{1,0:T(8,128)(2,1)}, bf16[384,1024]{1,0:T(8,128)(2,1)}) custom-call(bf16[1536,1792]{1,0:T(8,128)(2,1)} %get-tuple-element.119.refs_8_.grad_ref, bf16[1024,1664]{1,0:T(8,128)(2,1)} %get-tuple-element.115.w_ref, bf16[4,4,32,2304]{3,2,1,0:T(8,128)(2,1)} %joined.3.refs_0_), custom_call_target="tpu_custom_call" | custom-call | flops 1000000 | bytes 1000000 | tf_op jit(solution)/shard_map/unproject/pallas_call | solution.py:677
  415.8 17.2 %collective-permute-done.31.refs_1_ = bf16[384,1024]{1,0:T(8,128)(2,1)S(1)} collective-permute-done((bf16[384,1024]{1,0:T(8,128)(2,1)}, bf16[384,1024]{1,0:T(8,128)(2,1)S(1)}, u32[]{:S(2)}, u32[]{:S(2)}) %collective-permute-start.31) | collective-permute-done | bytes 786464 | tf_op jit(solution)/shard_map/ppermute | solution.py:1054
  433.0 16.5 %collective-permute-done.32.refs_2_ = bf16[384,1024]{1,0:T(8,128)(2,1)S(1)} collective-permute-done((bf16[384,1024]{1,0:T(8,128)(2,1)}, bf16[384,1024]{1,0:T(8,128)(2,1)S(1)}, u32[]{:S(2)}, u32[]{:S(2)}) %collective-permute-start.32) | collective-permute-done | bytes 786464 | tf_op jit(solution)/shard_map/ppermute | solution.py:1054
  450.7 4.4 in_back.1.refs_2_
  455.1 4.0 row_sums.1
  459.1 3.7 all-to-all-start.3
  462.8 3.2 fusion.12
  465.9 11.1 %all-to-all-done.3 = bf16[4,32,4608]{2,1,0:T(8,128)(2,1)S(1)} async-done(((bf16[4,32,4608]{2,1,0:T(8,128)(2,1)}), bf16[4,32,4608]{2,1,0:T(8,128)(2,1)S(1)}, u32[]{:S(2)}, u32[]{:S(2)}) %all-to-all-start.3) | async-done | bytes 1179680 | tf_op jit(solution)/shard_map/all_to_all | solution.py:1132
  (257 shorter events, 89.8 us)
Async XLA Ops:
  7.2 76.8 %all-gather.5.cloned.1.call-start = ((), (), s32[]{:S(2)}) async-start(), calls=%async_computation.4 | async-start | bytes 3833856 | tf_op jit(solution)/shard_map/all_gather | solution.py:1250
  16.6 17.4 %copy-start.17 = (bf16[1,32,4096]{2,1,0:T(8,128)(2,1)}, bf16[1,32,4096]{2,1,0:T(8,128)(2,1)S(1)}, u32[]{:S(2)}) copy-start(bf16[1,32,4096]{2,1,0:T(8,128)(2,1)S(1)} %get-tuple-element.164) | copy-start | bytes 786436
  16.7 10.1 %collective-permute-start = (bf16[32,4096]{1,0:T(8,128)(2,1)S(1)}, bf16[32,4096]{1,0:T(8,128)(2,1)S(1)}, u32[]{:S(2)}, u32[]{:S(2)}) collective-permute-start(bf16[32,4096]{1,0:T(8,128)(2,1)S(1)} %get-tuple-element.167), channel_id=1, source_target_pairs={{0,8},{8,0},{16,24},{24,16},{1,9},{9,1},{17,25},{25,17},{2,10},{10... | collective-permute-start | bytes 786440 | tf_op jit(solution)/shard_map/ppermute | solution.py:1054
  19.7 13.4 %collective-permute-start.1 = (bf16[32,4096]{1,0:T(8,128)(2,1)S(1)}, bf16[32,4096]{1,0:T(8,128)(2,1)S(1)}, u32[]{:S(2)}, u32[]{:S(2)}) collective-permute-start(bf16[32,4096]{1,0:T(8,128)(2,1)S(1)} %get-tuple-element.166), channel_id=1, source_target_pairs={{0,16},{8,24},{16,0},{24,8},{1,17},{9,25},{17,1},{25,9},{2,18},{10... | collective-permute-start | bytes 786440 | tf_op jit(solution)/shard_map/ppermute | solution.py:1054
  21.2 11.9 %collective-permute-start.2 = (bf16[32,4096]{1,0:T(8,128)(2,1)S(1)}, bf16[32,4096]{1,0:T(8,128)(2,1)S(1)}, u32[]{:S(2)}, u32[]{:S(2)}) collective-permute-start(bf16[32,4096]{1,0:T(8,128)(2,1)S(1)} %get-tuple-element.165), channel_id=1, source_target_pairs={{0,24},{8,16},{16,8},{24,0},{1,25},{9,17},{17,9},{25,1},{2,26},{10... | collective-permute-start | bytes 786440 | tf_op jit(solution)/shard_map/ppermute | solution.py:1054
  26.8 9.0 %copy-start.20 = (bf16[32,4096]{1,0:T(8,128)(2,1)}, bf16[32,4096]{1,0:T(8,128)(2,1)S(1)}, u32[]{:S(2)}) copy-start(bf16[32,4096]{1,0:T(8,128)(2,1)S(1)} %collective-permute-done) | copy-start | bytes 786436
  34.1 141.2 %all-gather.7.cloned.1.call-start = ((), (), s32[]{:S(2)}) async-start(), calls=%async_computation.5 | async-start | bytes 5308416 | tf_op jit(solution)/shard_map/all_gather | solution.py:1287
  34.1 9.8 %collective-permute-start.3 = (bf16[32,2048]{1,0:T(8,128)(2,1)}, bf16[32,2048]{1,0:T(8,128)(2,1)S(1)}, u32[]{:S(2)}, u32[]{:S(2)}) collective-permute-start(bf16[32,2048]{1,0:T(8,128)(2,1)} %bitcast.31), channel_id=1, source_target_pairs={{0,2},{1,3},{2,0},{3,1},{4,6},{5,7},{6,4},{7,5},{8,10},{9,11},{10,... | collective-permute-start | bytes 393224 | tf_op jit(solution)/shard_map/ppermute | solution.py:1054
  37.9 31.2 %collective-permute-start.6 = (bf16[384,1024]{1,0:T(8,128)(2,1)}, bf16[384,1024]{1,0:T(8,128)(2,1)S(1)}, u32[]{:S(2)}, u32[]{:S(2)}) collective-permute-start(bf16[384,1024]{1,0:T(8,128)(2,1)} %broadcast_add_fusion.1.refs_0_), channel_id=1, source_target_pairs={{0,8},{8,0},{16,24},{24,16},{1,9},{9,1},{17,25},{25,17},{2,10},{10... | collective-permute-start | bytes 2359304 | tf_op jit(solution)/shard_map/ppermute | solution.py:1054
  39.1 34.9 %collective-permute-start.7 = (bf16[384,1024]{1,0:T(8,128)(2,1)}, bf16[384,1024]{1,0:T(8,128)(2,1)S(1)}, u32[]{:S(2)}, u32[]{:S(2)}) collective-permute-start(bf16[384,1024]{1,0:T(8,128)(2,1)} %broadcast_add_fusion.1.refs_0_), channel_id=1, source_target_pairs={{0,16},{8,24},{16,0},{24,8},{1,17},{9,25},{17,1},{25,9},{2,18},{10... | collective-permute-start | bytes 2359304 | tf_op jit(solution)/shard_map/ppermute | solution.py:1054
  39.9 34.1 %collective-permute-start.8 = (bf16[384,1024]{1,0:T(8,128)(2,1)}, bf16[384,1024]{1,0:T(8,128)(2,1)}, u32[]{:S(2)}, u32[]{:S(2)}) collective-permute-start(bf16[384,1024]{1,0:T(8,128)(2,1)} %broadcast_add_fusion.1.refs_0_), channel_id=1, source_target_pairs={{0,24},{8,16},{16,8},{24,0},{1,25},{9,17},{17,9},{25,1},{2,26},{10... | collective-permute-start | bytes 2359304 | tf_op jit(solution)/shard_map/ppermute | solution.py:1054
  41.4 19.7 %collective-permute-start.4 = (bf16[32,2048]{1,0:T(8,128)(2,1)}, bf16[32,2048]{1,0:T(8,128)(2,1)S(1)}, u32[]{:S(2)}, u32[]{:S(2)}) collective-permute-start(bf16[32,2048]{1,0:T(8,128)(2,1)} %bitcast.31), channel_id=1, source_target_pairs={{0,4},{1,5},{2,6},{3,7},{4,0},{5,1},{6,2},{7,3},{8,12},{9,13},{10,... | collective-permute-start | bytes 393224 | tf_op jit(solution)/shard_map/ppermute | solution.py:1054
  44.0 21.2 %copy-start.34 = (bf16[32,2048]{1,0:T(8,128)(2,1)}, bf16[32,2048]{1,0:T(8,128)(2,1)S(1)}, u32[]{:S(2)}) copy-start(bf16[32,2048]{1,0:T(8,128)(2,1)S(1)} %collective-permute-done.3.refs_0_) | copy-start | bytes 393220
  44.0 17.1 %collective-permute-start.5 = (bf16[32,2048]{1,0:T(8,128)(2,1)}, bf16[32,2048]{1,0:T(8,128)(2,1)S(1)}, u32[]{:S(2)}, u32[]{:S(2)}) collective-permute-start(bf16[32,2048]{1,0:T(8,128)(2,1)} %bitcast.31), channel_id=1, source_target_pairs={{0,6},{1,7},{2,4},{3,5},{4,2},{5,3},{6,0},{7,1},{8,14},{9,15},{10,... | collective-permute-start | bytes 393224 | tf_op jit(solution)/shard_map/ppermute | solution.py:1054
  64.4 9.6 %copy-start.18 = (bf16[4,32,2048]{2,1,0:T(8,128)(2,1)S(1)}, bf16[4,32,2048]{2,1,0:T(8,128)(2,1)}, u32[]{:S(2)}) copy-start(bf16[4,32,2048]{2,1,0:T(8,128)(2,1)} %pad_maximum_fusion.6) | copy-start | bytes 1572868
  76.5 58.0 %collective-permute-start.10 = (bf16[384,1024]{1,0:T(8,128)(2,1)}, bf16[384,1024]{1,0:T(8,128)(2,1)S(1)}, u32[]{:S(2)}, u32[]{:S(2)}) collective-permute-start(bf16[384,1024]{1,0:T(8,128)(2,1)} %get-tuple-element.78.refs_8_), channel_id=1, source_target_pairs={{0,16},{8,24},{16,0},{24,8},{1,17},{9,25},{17,1},{25,9},{2,18},{10... | collective-permute-start | bytes 2359304 | tf_op jit(solution)/shard_map/ppermute | solution.py:1054
  77.1 57.4 %collective-permute-start.11 = (bf16[384,1024]{1,0:T(8,128)(2,1)}, bf16[384,1024]{1,0:T(8,128)(2,1)}, u32[]{:S(2)}, u32[]{:S(2)}) collective-permute-start(bf16[384,1024]{1,0:T(8,128)(2,1)} %get-tuple-element.78.refs_8_), channel_id=1, source_target_pairs={{0,24},{8,16},{16,8},{24,0},{1,25},{9,17},{17,9},{25,1},{2,26},{10... | collective-permute-start | bytes 2359304 | tf_op jit(solution)/shard_map/ppermute | solution.py:1054
  78.6 55.9 %collective-permute-start.9 = (bf16[384,1024]{1,0:T(8,128)(2,1)}, bf16[384,1024]{1,0:T(8,128)(2,1)}, u32[]{:S(2)}, u32[]{:S(2)}) collective-permute-start(bf16[384,1024]{1,0:T(8,128)(2,1)} %get-tuple-element.78.refs_8_), channel_id=1, source_target_pairs={{0,8},{8,0},{16,24},{24,16},{1,9},{9,1},{17,25},{25,17},{2,10},{10... | collective-permute-start | bytes 2359304 | tf_op jit(solution)/shard_map/ppermute | solution.py:1054
  80.0 54.5 %all-to-all-start = ((bf16[4,4,32,2048]{3,2,1,0:T(8,128)(2,1)}), bf16[4,4,32,2048]{3,2,1,0:T(8,128)(2,1)S(1)}, u32[]{:S(2)}, u32[]{:S(2)}) async-start(bf16[4,4,32,2048]{3,2,1,0:T(8,128)(2,1)} %get-tuple-element.77), calls=%async_computation | async-start | bytes 4194304 | tf_op jit(solution)/shard_map/all_to_all | solution.py:1289
  142.8 4.4 collective-permute-start.12
  142.8 12.9 %collective-permute-start.13 = (bf16[384,512]{1,0:T(8,128)(2,1)}, bf16[384,512]{1,0:T(8,128)(2,1)S(1)}, u32[]{:S(2)}, u32[]{:S(2)}) collective-permute-start(bf16[384,512]{1,0:T(8,128)(2,1)} %get-tuple-element.83.refs_5_), channel_id=1, source_target_pairs={{0,8},{8,0},{16,24},{24,16},{1,9},{9,1},{17,25},{25,17},{2,10},{10... | collective-permute-start | bytes 1179656 | tf_op jit(solution)/shard_map/ppermute | solution.py:1054
  144.8 19.9 %collective-permute-start.14 = (bf16[384,512]{1,0:T(8,128)(2,1)}, bf16[384,512]{1,0:T(8,128)(2,1)S(1)}, u32[]{:S(2)}, u32[]{:S(2)}) collective-permute-start(bf16[384,512]{1,0:T(8,128)(2,1)} %get-tuple-element.84.refs_6_), channel_id=1, source_target_pairs={{0,16},{8,24},{16,0},{24,8},{1,17},{9,25},{17,1},{25,9},{2,18},{10... | collective-permute-start | bytes 1179656 | tf_op jit(solution)/shard_map/ppermute | solution.py:1054
  146.3 18.4 %collective-permute-start.15 = (bf16[384,512]{1,0:T(8,128)(2,1)}, bf16[384,512]{1,0:T(8,128)(2,1)S(1)}, u32[]{:S(2)}, u32[]{:S(2)}) collective-permute-start(bf16[384,512]{1,0:T(8,128)(2,1)} %get-tuple-element.85.refs_7_), channel_id=1, source_target_pairs={{0,24},{8,16},{16,8},{24,0},{1,25},{9,17},{17,9},{25,1},{2,26},{10... | collective-permute-start | bytes 1179656 | tf_op jit(solution)/shard_map/ppermute | solution.py:1054
  155.7 9.0 %copy-start.40 = (bf16[384,512]{1,0:T(8,128)(2,1)}, bf16[384,512]{1,0:T(8,128)(2,1)S(1)}, u32[]{:S(2)}) copy-start(bf16[384,512]{1,0:T(8,128)(2,1)S(1)} %collective-permute-done.13.refs_1_) | copy-start | bytes 1179652
  171.8 20.7 %collective-permute-start.16 = (bf16[384,1024]{1,0:T(8,128)(2,1)}, bf16[384,1024]{1,0:T(8,128)(2,1)S(1)}, u32[]{:S(2)}, u32[]{:S(2)}) collective-permute-start(bf16[384,1024]{1,0:T(8,128)(2,1)} %get-tuple-element.88.refs_0_), channel_id=1, source_target_pairs={{0,8},{8,0},{16,24},{24,16},{1,9},{9,1},{17,25},{25,17},{2,10},{10... | collective-permute-start | bytes 2359304 | tf_op jit(solution)/shard_map/ppermute | solution.py:1054
  172.8 37.5 %collective-permute-start.19 = (bf16[384,1024]{1,0:T(8,128)(2,1)}, bf16[384,1024]{1,0:T(8,128)(2,1)S(1)}, u32[]{:S(2)}, u32[]{:S(2)}) collective-permute-start(bf16[384,1024]{1,0:T(8,128)(2,1)} %get-tuple-element.88.refs_0_), channel_id=1, source_target_pairs={{0,24},{8,16},{16,8},{24,0},{1,25},{9,17},{17,9},{25,1},{2,26},{10... | collective-permute-start | bytes 2359304 | tf_op jit(solution)/shard_map/ppermute | solution.py:1054
  174.7 44.9 %collective-permute-start.18 = (bf16[384,1024]{1,0:T(8,128)(2,1)}, bf16[384,1024]{1,0:T(8,128)(2,1)}, u32[]{:S(2)}, u32[]{:S(2)}) collective-permute-start(bf16[384,1024]{1,0:T(8,128)(2,1)} %get-tuple-element.88.refs_0_), channel_id=1, source_target_pairs={{0,16},{8,24},{16,0},{24,8},{1,17},{9,25},{17,1},{25,9},{2,18},{10... | collective-permute-start | bytes 2359304 | tf_op jit(solution)/shard_map/ppermute | solution.py:1054
  186.9 6.9 %copy-start.26 = (bf16[384,1024]{1,0:T(8,128)(2,1)}, bf16[384,1024]{1,0:T(8,128)(2,1)S(1)}, u32[]{:S(2)}) copy-start(bf16[384,1024]{1,0:T(8,128)(2,1)S(1)} %convolution_convert_fusion.3.refs_0_) | copy-start | bytes 2359300
  198.9 31.1 %collective-permute-start.17 = (bf16[384,1024]{1,0:T(8,128)(2,1)S(1)}, bf16[384,1024]{1,0:T(8,128)(2,1)S(1)}, u32[]{:S(2)}, u32[]{:S(2)}) collective-permute-start(bf16[384,1024]{1,0:T(8,128)(2,1)S(1)} %convolution_convert_fusion.2), channel_id=1, source_target_pairs={{0,8},{8,0},{16,24},{24,16},{1,9},{9,1},{17,25},{25,17},{2,10},{10... | collective-permute-start | bytes 2359304 | tf_op jit(solution)/shard_map/ppermute | solution.py:1054
  216.8 41.6 %collective-permute-start.21 = (bf16[384,1024]{1,0:T(8,128)(2,1)S(1)}, bf16[384,1024]{1,0:T(8,128)(2,1)S(1)}, u32[]{:S(2)}, u32[]{:S(2)}) collective-permute-start(bf16[384,1024]{1,0:T(8,128)(2,1)S(1)} %convolution_convert_fusion.1), channel_id=1, source_target_pairs={{0,24},{8,16},{16,8},{24,0},{1,25},{9,17},{17,9},{25,1},{2,26},{10... | collective-permute-start | bytes 2359304 | tf_op jit(solution)/shard_map/ppermute | solution.py:1054
  225.6 32.8 %collective-permute-start.20 = (bf16[384,1024]{1,0:T(8,128)(2,1)S(1)}, bf16[384,1024]{1,0:T(8,128)(2,1)S(1)}, u32[]{:S(2)}, u32[]{:S(2)}) collective-permute-start(bf16[384,1024]{1,0:T(8,128)(2,1)S(1)} %convolution_convert_fusion.refs_16_), channel_id=1, source_target_pairs={{0,16},{8,24},{16,0},{24,8},{1,17},{9,25},{17,1},{25,9},{2,18},{10... | collective-permute-start | bytes 2359304 | tf_op jit(solution)/shard_map/ppermute | solution.py:1054
  267.2 30.3 %collective-permute-start.28 = (bf16[4,4,32,2304]{3,2,1,0:T(8,128)(2,1)}, bf16[4,4,32,2304]{3,2,1,0:T(8,128)(2,1)S(1)}, u32[]{:S(2)}, u32[]{:S(2)}) collective-permute-start(bf16[4,4,32,2304]{3,2,1,0:T(8,128)(2,1)} %get-tuple-element.111), channel_id=1, source_target_pairs={{0,1},{1,0},{2,3},{3,2},{4,5},{5,4},{6,7},{7,6},{8,9},{9,8},{10,11... | collective-permute-start | bytes 7077896 | tf_op jit(solution)/shard_map/ppermute | solution.py:1054
  267.2 12.2 %collective-permute-start.22 = (bf16[384,512]{1,0:T(8,128)(2,1)}, bf16[384,512]{1,0:T(8,128)(2,1)S(1)}, u32[]{:S(2)}, u32[]{:S(2)}) collective-permute-start(bf16[384,512]{1,0:T(8,128)(2,1)} %get-tuple-element.94), channel_id=1, source_target_pairs={{0,8},{8,0},{16,24},{24,16},{1,9},{9,1},{17,25},{25,17},{2,10},{10... | collective-permute-start | bytes 1179656 | tf_op jit(solution)/shard_map/ppermute | solution.py:1054
  267.5 19.9 %collective-permute-start.23 = (bf16[384,512]{1,0:T(8,128)(2,1)}, bf16[384,512]{1,0:T(8,128)(2,1)S(1)}, u32[]{:S(2)}, u32[]{:S(2)}) collective-permute-start(bf16[384,512]{1,0:T(8,128)(2,1)} %get-tuple-element.95), channel_id=1, source_target_pairs={{0,16},{8,24},{16,0},{24,8},{1,17},{9,25},{17,1},{25,9},{2,18},{10... | collective-permute-start | bytes 1179656 | tf_op jit(solution)/shard_map/ppermute | solution.py:1054
  269.2 18.1 %collective-permute-start.24 = (bf16[384,512]{1,0:T(8,128)(2,1)}, bf16[384,512]{1,0:T(8,128)(2,1)S(1)}, u32[]{:S(2)}, u32[]{:S(2)}) collective-permute-start(bf16[384,512]{1,0:T(8,128)(2,1)} %get-tuple-element.96), channel_id=1, source_target_pairs={{0,24},{8,16},{16,8},{24,0},{1,25},{9,17},{17,9},{25,1},{2,26},{10... | collective-permute-start | bytes 1179656 | tf_op jit(solution)/shard_map/ppermute | solution.py:1054
  279.4 8.0 %copy-start.37 = (bf16[384,512]{1,0:T(8,128)(2,1)}, bf16[384,512]{1,0:T(8,128)(2,1)S(1)}, u32[]{:S(2)}) copy-start(bf16[384,512]{1,0:T(8,128)(2,1)S(1)} %collective-permute-done.22.refs_1_) | copy-start | bytes 1179652
  303.3 91.1 %all-to-all-start.1 = ((bf16[4,4,32,2304]{3,2,1,0:T(8,128)(2,1)}), bf16[4,4,32,2304]{3,2,1,0:T(8,128)(2,1)S(1)}, u32[]{:S(2)}, u32[]{:S(2)}) async-start(bf16[4,4,32,2304]{3,2,1,0:T(8,128)(2,1)} %joined.2.refs_0_), calls=%async_computation.1 | async-start | bytes 4718592 | tf_op jit(solution)/shard_map/all_to_all | solution.py:1093
  309.1 68.9 %collective-permute-start.25 = (bf16[768,1024]{1,0:T(8,128)(2,1)}, bf16[768,1024]{1,0:T(8,128)(2,1)S(1)}, u32[]{:S(2)}, u32[]{:S(2)}) collective-permute-start(bf16[768,1024]{1,0:T(8,128)(2,1)} %get-tuple-element.100), channel_id=1, source_target_pairs={{0,8},{8,0},{16,24},{24,16},{1,9},{9,1},{17,25},{25,17},{2,10},{10... | collective-permute-start | bytes 4718600 | tf_op jit(solution)/shard_map/ppermute | solution.py:1054
  310.8 68.9 %collective-permute-start.26 = (bf16[768,1024]{1,0:T(8,128)(2,1)}, bf16[768,1024]{1,0:T(8,128)(2,1)S(1)}, u32[]{:S(2)}, u32[]{:S(2)}) collective-permute-start(bf16[768,1024]{1,0:T(8,128)(2,1)} %get-tuple-element.101), channel_id=1, source_target_pairs={{0,16},{8,24},{16,0},{24,8},{1,17},{9,25},{17,1},{25,9},{2,18},{10... | collective-permute-start | bytes 4718600 | tf_op jit(solution)/shard_map/ppermute | solution.py:1054
  311.1 68.6 %collective-permute-start.27 = (bf16[768,1024]{1,0:T(8,128)(2,1)}, bf16[768,1024]{1,0:T(8,128)(2,1)S(1)}, u32[]{:S(2)}, u32[]{:S(2)}) collective-permute-start(bf16[768,1024]{1,0:T(8,128)(2,1)} %get-tuple-element.102), channel_id=1, source_target_pairs={{0,24},{8,16},{16,8},{24,0},{1,25},{9,17},{17,9},{25,1},{2,26},{10... | collective-permute-start | bytes 4718600 | tf_op jit(solution)/shard_map/ppermute | solution.py:1054
  377.9 11.4 %collective-permute-start.29 = (bf16[4,4,32,1792]{3,2,1,0:T(8,128)(2,1)}, bf16[4,4,32,1792]{3,2,1,0:T(8,128)(2,1)}, u32[]{:S(2)}, u32[]{:S(2)}) collective-permute-start(bf16[4,4,32,1792]{3,2,1,0:T(8,128)(2,1)} %get-tuple-element.121), channel_id=1, source_target_pairs={{0,1},{1,0},{2,3},{3,2},{4,5},{5,4},{6,7},{7,6},{8,9},{9,8},{10,11... | collective-permute-start | bytes 5505032 | tf_op jit(solution)/shard_map/ppermute | solution.py:1054
  387.1 2.1 collective-permute-start.30
  395.7 59.3 %all-to-all-start.2 = ((bf16[4,4,32,2304]{3,2,1,0:T(8,128)(2,1)}), bf16[4,4,32,2304]{3,2,1,0:T(8,128)(2,1)}, u32[]{:S(2)}, u32[]{:S(2)}) async-start(bf16[4,4,32,2304]{3,2,1,0:T(8,128)(2,1)} %joined.3.refs_0_), calls=%async_computation.2 | async-start | bytes 4718592 | tf_op jit(solution)/shard_map/all_to_all | solution.py:1093
  412.4 20.6 %collective-permute-start.31 = (bf16[384,1024]{1,0:T(8,128)(2,1)}, bf16[384,1024]{1,0:T(8,128)(2,1)S(1)}, u32[]{:S(2)}, u32[]{:S(2)}) collective-permute-start(bf16[384,1024]{1,0:T(8,128)(2,1)} %get-tuple-element.125), channel_id=1, source_target_pairs={{0,8},{8,0},{16,24},{24,16},{1,9},{9,1},{17,25},{25,17},{2,10},{10... | collective-permute-start | bytes 2359304 | tf_op jit(solution)/shard_map/ppermute | solution.py:1054
  413.2 36.3 %collective-permute-start.32 = (bf16[384,1024]{1,0:T(8,128)(2,1)}, bf16[384,1024]{1,0:T(8,128)(2,1)S(1)}, u32[]{:S(2)}, u32[]{:S(2)}) collective-permute-start(bf16[384,1024]{1,0:T(8,128)(2,1)} %get-tuple-element.126), channel_id=1, source_target_pairs={{0,16},{8,24},{16,0},{24,8},{1,17},{9,25},{17,1},{25,9},{2,18},{10... | collective-permute-start | bytes 2359304 | tf_op jit(solution)/shard_map/ppermute | solution.py:1054
  414.4 35.1 %collective-permute-start.33 = (bf16[384,1024]{1,0:T(8,128)(2,1)}, bf16[384,1024]{1,0:T(8,128)(2,1)S(1)}, u32[]{:S(2)}, u32[]{:S(2)}) collective-permute-start(bf16[384,1024]{1,0:T(8,128)(2,1)} %get-tuple-element.127), channel_id=1, source_target_pairs={{0,24},{8,16},{16,8},{24,0},{1,25},{9,17},{17,9},{25,1},{2,26},{10... | collective-permute-start | bytes 2359304 | tf_op jit(solution)/shard_map/ppermute | solution.py:1054
  433.0 16.5 %copy-start.30 = (bf16[384,1024]{1,0:T(8,128)(2,1)}, bf16[384,1024]{1,0:T(8,128)(2,1)S(1)}, u32[]{:S(2)}) copy-start(bf16[384,1024]{1,0:T(8,128)(2,1)S(1)} %collective-permute-done.31.refs_1_) | copy-start | bytes 2359300
  459.1 18.0 %all-to-all-start.3 = ((bf16[4,32,4608]{2,1,0:T(8,128)(2,1)}), bf16[4,32,4608]{2,1,0:T(8,128)(2,1)S(1)}, u32[]{:S(2)}, u32[]{:S(2)}) async-start(bf16[4,32,4608]{2,1,0:T(8,128)(2,1)} %row_sums.1), calls=%async_computation.3 | async-start | bytes 2359296 | tf_op jit(solution)/shard_map/all_to_all | solution.py:1132
  (35 other events, 68.4 us)
Sparse Core Ops, SparseCore 0:
  34.2 48.6 all-gather.4
  85.1 50.9 all-gather.6
